TPU v7x, 32 devices: a whole 2x2x4 slice. The times are simulated.
32 devices in a mesh: dp: 16 (over z, x, core), seq: 2 (over y).
Axes of the slice: x: 2, y: 2, z: 4, core: 2. Of those that a mesh axis runs over, the one named last changes fastest.
Arguments:
- inputs: bfloat16 [16, 256, 1536], P('dp', 'seq'), may hold values from -45 to 45
- dilated_tap_weight: bfloat16 [3, 768, 1536], P(None, 'seq'), may hold values from -0.09375 to 0.09375
- point_weight: bfloat16 [768, 1536], P('seq'), may hold values from -0.21875 to 0.21875
- query_weight: bfloat16 [1536, 1536], P('seq'), may hold values from -0.21875 to 0.21875
- key_weight: bfloat16 [1536, 1536], P('seq'), may hold values from -0.21875 to 0.21875
- value_weight: bfloat16 [1536, 1536], P('seq'), may hold values from -0.15625 to 0.15625
- out_weight: bfloat16 [1536, 1536], P('seq'), may hold values from -0.4375 to 0.4375
- cotangent: bfloat16 [16, 256, 1536], P('dp', 'seq'), may hold values from -6 to 6
Outputs:
- output: bfloat16 [16, 256, 1536], P('dp', 'seq')
- dilated_tap_gradient: float32 [3, 1536, 768], P(None, 'dp', 'seq')
- point_grad: float32 [768, 1536], P('seq', 'dp')
- query_grad: float32 [1536, 1536], P('dp', 'seq')
- key_grad: float32 [1536, 1536], P('dp', 'seq')
- value_grad: float32 [1536, 1536], P('dp', 'seq')
- out_grad: float32 [1536, 1536], P('seq', 'dp')
All inputs are finite; a program needn't handle non-finite values.
Results may differ from a plain program's by a relative error of at most 0.033.
Values may be sent and summed in bfloat16 or wider, within the bound.
No kernel may reach another device: no remote copies, remote signals or barrier semaphores. Data moves between devices by JAX's collectives and lax.ppermute only.
A program may use at most 128 MiB of HBM per device.

v0:
```python
import math

import jax
import jax.numpy as jnp
from jax import lax
from jax.sharding import PartitionSpec as P

HSIZE = 192
DILATION_STEP = 16


EPSILON = 1e-06
SOFT_CAP = 6.0


def rms_scale(value_rows):
    return lax.rsqrt(jnp.mean(value_rows * value_rows, axis=-1, keepdims=True) + EPSILON)


def rows_shifted(value_rows, tap_shift):
    padded_rows = jnp.pad(value_rows, ((DILATION_STEP, DILATION_STEP), (0, 0)))
    return padded_rows[DILATION_STEP + tap_shift : DILATION_STEP + tap_shift + value_rows.shape[0]]


def gelu_back(pre_act, upstream):
    return jax.vjp(jax.nn.gelu, pre_act)[1](upstream)[0]


def split_heads(matrix):
    head_count = matrix.shape[1] // HSIZE
    return matrix.reshape(matrix.shape[0], head_count, HSIZE).transpose(1, 0, 2)


def join_heads(stacked):
    return stacked.transpose(1, 0, 2).reshape(stacked.shape[1], -1)


def inner_rows(left_side, right_side):
    return lax.dot_general(
        left_side, right_side, (((0,), (0,)), ((), ())), preferred_element_type=jnp.float32
    )


def outer_cols(left_side, right_side):
    return lax.dot_general(
        left_side, right_side, (((1,), (1,)), ((), ())), preferred_element_type=jnp.float32
    )


def norm_back(grad_normed, residual_f32, scale):
    return scale * grad_normed - residual_f32 * scale**3 * jnp.mean(
        grad_normed * residual_f32, axis=-1, keepdims=True
    )


def head_pass(packed):
    query_h, key_h, value_h, dout_h = packed
    inv_root = 1.0 / math.sqrt(HSIZE)
    raw_score = outer_cols(query_h, key_h) * inv_root
    capped = SOFT_CAP * jnp.tanh(raw_score / SOFT_CAP)
    unnormed = jnp.exp(capped)
    soft_weights = unnormed / jnp.sum(unnormed, axis=-1, keepdims=True)
    soft_low = soft_weights.astype(jnp.bfloat16)
    out_h = jnp.dot(soft_low, value_h, preferred_element_type=jnp.float32).astype(jnp.bfloat16)
    grad_soft = outer_cols(dout_h, value_h)
    grad_capped = soft_weights * (
        grad_soft - jnp.sum(soft_weights * grad_soft, axis=-1, keepdims=True)
    )
    ratio = capped / SOFT_CAP
    grad_score = (grad_capped * (1.0 - ratio * ratio)).astype(jnp.bfloat16)
    grad_query = (jnp.dot(grad_score, key_h, preferred_element_type=jnp.float32) * inv_root).astype(
        jnp.bfloat16
    )
    grad_key = (inner_rows(grad_score, query_h) * inv_root).astype(jnp.bfloat16)
    grad_value = inner_rows(soft_low, dout_h).astype(jnp.bfloat16)
    return (out_h, grad_query, grad_key, grad_value)


def shards(
    inputs,
    dilated_tap_weight,
    point_weight,
    query_weight,
    key_weight,
    value_weight,
    out_weight,
    cotangent,
):
    channels = inputs.shape[2]
    input_rows = inputs[0]
    input_whole = lax.all_gather(input_rows, "seq", axis=0, tiled=True)
    length = input_whole.shape[0]
    inv_tokens = 1.0 / math.sqrt(inputs.shape[0] * lax.axis_size("dp") * length)
    input_full = input_whole.astype(jnp.float32)
    gelu_output = jax.nn.gelu(input_full * rms_scale(input_full)).astype(jnp.bfloat16)
    middle_local = dilated_tap_weight.shape[1]
    tap_output = outer_cols(gelu_output, dilated_tap_weight.reshape(3 * middle_local, channels))
    convolution_preact = (
        rows_shifted(tap_output[:, :middle_local], -DILATION_STEP)
        + tap_output[:, middle_local : 2 * middle_local]
        + rows_shifted(tap_output[:, 2 * middle_local :], DILATION_STEP)
    )
    middle = jax.nn.gelu(convolution_preact).astype(jnp.bfloat16)
    conv_part = lax.psum_scatter(
        jnp.dot(middle, point_weight, preferred_element_type=jnp.float32).astype(jnp.bfloat16),
        "seq",
        scatter_dimension=0,
        tiled=True,
    ).astype(jnp.float32)
    residual = (input_rows.astype(jnp.float32) + conv_part).astype(jnp.bfloat16)
    residual_f32 = lax.optimization_barrier(residual).astype(jnp.float32)
    scale_rows = rms_scale(residual_f32)
    normed = lax.all_gather(
        (residual_f32 * scale_rows).astype(jnp.bfloat16), "seq", axis=0, tiled=True
    )
    query_mat = outer_cols(normed, query_weight).astype(jnp.bfloat16)
    key_mat = outer_cols(normed, key_weight).astype(jnp.bfloat16)
    value_mat = outer_cols(normed, value_weight).astype(jnp.bfloat16)
    grad_rows_low = (cotangent[0].astype(jnp.float32) * inv_tokens).astype(jnp.bfloat16)
    grad_y = lax.all_gather(grad_rows_low, "seq", axis=0, tiled=True)
    grad_heads = outer_cols(grad_y, out_weight).astype(jnp.bfloat16)
    results = lax.map(
        head_pass,
        (
            split_heads(query_mat),
            split_heads(key_mat),
            split_heads(value_mat),
            split_heads(grad_heads),
        ),
    )
    attended, query_delta, key_delta, value_delta = [join_heads(stacked) for stacked in results]
    attn_part = lax.psum_scatter(
        jnp.dot(attended, out_weight, preferred_element_type=jnp.float32).astype(jnp.bfloat16),
        "seq",
        scatter_dimension=0,
        tiled=True,
    ).astype(jnp.float32)
    output = (residual_f32 + attn_part).astype(jnp.bfloat16)[None]
    out_grad = inner_rows(attended, grad_y)
    query_grad = inner_rows(normed, query_delta)
    key_grad = inner_rows(normed, key_delta)
    value_grad = inner_rows(normed, value_delta)
    grad_normed_rows = lax.psum_scatter(
        (
            jnp.dot(query_delta, query_weight, preferred_element_type=jnp.float32)
            + jnp.dot(key_delta, key_weight, preferred_element_type=jnp.float32)
            + jnp.dot(value_delta, value_weight, preferred_element_type=jnp.float32)
        ).astype(jnp.bfloat16),
        "seq",
        scatter_dimension=0,
        tiled=True,
    ).astype(jnp.float32)
    grad_resid_rows = (
        grad_rows_low.astype(jnp.float32) + norm_back(grad_normed_rows, residual_f32, scale_rows)
    ).astype(jnp.bfloat16)
    grad_resid = lax.all_gather(grad_resid_rows, "seq", axis=0, tiled=True)
    grad_middle = outer_cols(grad_resid, point_weight)
    convolution_gradient = gelu_back(convolution_preact, grad_middle).astype(jnp.bfloat16)
    point_grad = inner_rows(middle, grad_resid)
    moved_conv = jnp.concatenate(
        [
            rows_shifted(convolution_gradient, DILATION_STEP),
            convolution_gradient,
            rows_shifted(convolution_gradient, -DILATION_STEP),
        ],
        axis=1,
    )
    dilated_tap_gradient = (
        inner_rows(gelu_output, moved_conv).reshape(channels, 3, middle_local).transpose(1, 0, 2)
    )
    sent_dilated, sent_point, sent_query, sent_key, sent_value, sent_out = (
        lax.psum_scatter(
            dilated_tap_gradient.astype(jnp.bfloat16), "dp", scatter_dimension=1, tiled=True
        ).astype(jnp.float32),
        lax.psum_scatter(
            point_grad.astype(jnp.bfloat16), "dp", scatter_dimension=1, tiled=True
        ).astype(jnp.float32),
        lax.psum_scatter(
            query_grad.astype(jnp.bfloat16), "dp", scatter_dimension=0, tiled=True
        ).astype(jnp.float32),
        lax.psum_scatter(
            key_grad.astype(jnp.bfloat16), "dp", scatter_dimension=0, tiled=True
        ).astype(jnp.float32),
        lax.psum_scatter(
            value_grad.astype(jnp.bfloat16), "dp", scatter_dimension=0, tiled=True
        ).astype(jnp.float32),
        lax.psum_scatter(
            out_grad.astype(jnp.bfloat16), "dp", scatter_dimension=1, tiled=True
        ).astype(jnp.float32),
    )
    return (output, sent_dilated, sent_point, sent_query, sent_key, sent_value, sent_out)


def solution(mesh):
    placed = (
        P("dp", "seq", None),
        P(None, "seq", None),
        P("seq", None),
        P("seq", None),
        P("seq", None),
        P("seq", None),
        P("seq", None),
        P("dp", "seq", None),
    )
    return jax.shard_map(
        shards,
        mesh=mesh,
        in_specs=placed,
        out_specs=(
            P("dp", "seq", None),
            P(None, "dp", "seq"),
            P("seq", "dp"),
            P("dp", "seq"),
            P("dp", "seq"),
            P("dp", "seq"),
            P("seq", "dp"),
        ),
        check_vma=False,
    )
```

profile of v0, /device:TPU:0, one launch (start us, length us, event | category | flops | bytes accessed | tf_op | source)
XLA Modules:
  0.0 576.9 jit_solution(7994699589530829010)
XLA Ops:
  7.2 13.1 %all-gather = bf16[1,256,1536]{2,1,0:T(8,128)(2,1)S(1)} all-gather(bf16[1,128,1536]{2,1,0:T(8,128)(2,1)} %param.10), channel_id=2, replica_groups=mesh['dp'=16,'seq'=2] {'seq'}, dimensions={1}, use_global_device_ids=true | all-gather | bytes 1179648 | tf_op jit(solution)/shard_map/all_gather | solution.py:91
  26.3 15.5 %all-gather.1 = bf16[1,256,1536]{2,1,0:T(8,128)(2,1)S(1)} all-gather(bf16[1,128,1536]{2,1,0:T(8,128)(2,1)S(1)} %multiply_convert_fusion.1), channel_id=3, replica_groups=mesh['dp'=16,'seq'=2] {'seq'}, dimensions={1}, use_global_device_ids=true | all-gather | bytes 1179648 | tf_op jit(solution)/shard_map/all_gather | solution.py:120
  42.7 3.2 convolution_convert_fusion.10
  50.1 10.6 %all_gather.13 = bf16[256,1536]{1,0:T(8,128)(2,1)S(1)} all-gather(bf16[128,1536]{1,0:T(8,128)(2,1)S(1)} %fusion.54), channel_id=1, replica_groups=mesh['dp'=16,'seq'=2] {'seq'}, dimensions={0}, use_global_device_ids=true | all-gather | bytes 1179648 | tf_op jit(solution)/shard_map/all_gather | solution.py:113
  65.1 3.5 convolution_convert_fusion.12
  70.5 3.5 convolution_convert_fusion.13
  75.9 37.9 %while.18 = (s32[]{:T(128)}, bf16[4,256,192]{1,2,0:T(8,128)(2,1)}, bf16[4,256,192]{1,2,0:T(8,128)(2,1)}, bf16[4,256,192]{1,2,0:T(8,128)(2,1)}, bf16[4,256,192]{1...) while((s32[]{:T(128)}, bf16[4,256,192]{1,2,0:T(8,128)(2,1)}, ...), condition=%wide.region_6.7_spmd, body=%wide.region_3.6_spmd.sunk | while | flops 152665600 | bytes 3421293 | solution.py:122
  113.8 2.7 fusion.81
  120.0 3.5 convolution_convert_fusion.8
  123.6 15.2 %reduce-scatter.14.cloned.1.call-done = bf16[128,1536]{1,0:T(8,128)(2,1)} async-done(((bf16[256,1536]{1,0:T(8,128)(2,1)}), bf16[128,1536]{1,0:T(8,128)(2,1)}) %reduce-scatter.14.cloned.1.call-update) | async-done | bytes 393232 | tf_op jit(solution)/shard_map/reduce_scatter | solution.py:143
  140.1 18.4 %reduce-scatter.12.cloned.1.call-done = bf16[128,1536]{1,0:T(8,128)(2,1)} async-done(((bf16[256,1536]{1,0:T(8,128)(2,1)}), bf16[128,1536]{1,0:T(8,128)(2,1)}) %reduce-scatter.12.cloned.1.call-update) | async-done | bytes 393232 | tf_op jit(solution)/shard_map/reduce_scatter | solution.py:132
  161.0 11.5 %all_gather.15 = bf16[256,1536]{1,0:T(8,128)(2,1)S(1)} all-gather(bf16[128,1536]{1,0:T(8,128)(2,1)S(1)} %get-tuple-element.161), channel_id=1, replica_groups=mesh['dp'=16,'seq'=2] {'seq'}, dimensions={0}, use_global_device_ids=true | all-gather | bytes 1179648 | tf_op jit(solution)/shard_map/all_gather | solution.py:156
  175.2 3.5 convolution_convert_fusion.3
  178.8 3.5 convolution_convert_fusion.4
  182.5 3.6 convolution_convert_fusion.5
  186.2 3.5 convolution_convert_fusion.6
  192.2 3.3 convolution_convert_fusion.2
  195.5 6.0 %copy.28 = bf16[1536,3,384]{2,0,1:T(8,128)(2,1)} copy(bf16[1536,3,384]{0,2,1:T(8,128)(2,1)} %bitcast.157) | data formatting | bytes 7077888 | tf_op jit(solution)/shard_map/convert_element_type | solution.py:173
  201.5 31.8 %reduce-scatter.18.cloned.1.call-done = bf16[384,96]{0,1:T(8,128)(2,1)} async-done(((bf16[384,1536]{0,1:T(8,128)(2,1)}), bf16[384,96]{0,1:T(8,128)(2,1)}) %reduce-scatter.18.cloned.1.call-update) | async-done | bytes 73744 | tf_op jit(solution)/shard_map/reduce_scatter | solution.py:175
  234.9 64.6 %reduce-scatter.26.cloned.1.call-done = bf16[768,96]{0,1:T(8,128)(2,1)} async-done(((bf16[768,1536]{0,1:T(8,128)(2,1)}), bf16[768,96]{0,1:T(8,128)(2,1)}) %reduce-scatter.26.cloned.1.call-update) | async-done | bytes 147472 | tf_op jit(solution)/shard_map/reduce_scatter | solution.py:187
  301.1 63.9 %reduce-scatter.24.cloned.1.call-done = bf16[96,768]{1,0:T(8,128)(2,1)} async-done(((bf16[1536,768]{1,0:T(8,128)(2,1)}), bf16[96,768]{1,0:T(8,128)(2,1)}) %reduce-scatter.24.cloned.1.call-update) | async-done | bytes 147472 | tf_op jit(solution)/shard_map/reduce_scatter | solution.py:184
  366.7 64.6 %reduce-scatter.22.cloned.1.call-done = bf16[96,768]{1,0:T(8,128)(2,1)} async-done(((bf16[1536,768]{1,0:T(8,128)(2,1)}), bf16[96,768]{1,0:T(8,128)(2,1)}) %reduce-scatter.22.cloned.1.call-update) | async-done | bytes 147472 | tf_op jit(solution)/shard_map/reduce_scatter | solution.py:181
  433.0 64.1 %reduce-scatter.20.cloned.1.call-done = bf16[96,768]{1,0:T(8,128)(2,1)} async-done(((bf16[1536,768]{1,0:T(8,128)(2,1)}), bf16[96,768]{1,0:T(8,128)(2,1)}) %reduce-scatter.20.cloned.1.call-update) | async-done | bytes 147472 | tf_op jit(solution)/shard_map/reduce_scatter | solution.py:178
  498.8 69.9 %reduce-scatter.16.cloned.1.call-done = bf16[3,96,384]{2,1,0:T(8,128)(2,1)} async-done(((bf16[3,1536,384]{2,1,0:T(8,128)(2,1)}), bf16[3,96,384]{2,1,0:T(8,128)(2,1)}) %reduce-scatter.16.cloned.1.call-update) | async-done | bytes 221200 | tf_op jit(solution)/shard_map/reduce_scatter | solution.py:172
  (111 shorter events, 79.7 us)
Async XLA Ops:
  7.2 13.4 %copy-start = (bf16[3,384,1536]{2,1,0:T(8,128)(2,1)S(1)}, bf16[3,384,1536]{2,1,0:T(8,128)(2,1)}, u32[]{:S(2)}) copy-start(bf16[3,384,1536]{2,1,0:T(8,128)(2,1)} %param.11) | copy-start | bytes 10616836
  7.2 40.7 %reduce-scatter.10.cloned.1.call-start = ((), (), s32[]{:S(2)}) async-start(), calls=%async_computation.9 | async-start | bytes 1179648 | tf_op jit(solution)/shard_map/reduce_scatter | solution.py:104
  20.3 1.9 copy-start.3
  22.2 1.4 copy-start.14
  22.3 0.7 copy-start.12
  25.1 113.6 %reduce-scatter.14.cloned.1.call-start = ((), (), s32[]{:S(2)}) async-start(), calls=%async_computation.11 | async-start | bytes 1179648 | tf_op jit(solution)/shard_map/reduce_scatter | solution.py:143
  41.8 0.9 copy-start.6
  47.9 13.8 %copy-start.7 = (bf16[768,1536]{1,0:T(8,128)(2,1)S(1)}, bf16[768,1536]{1,0:T(8,128)(2,1)}, u32[]{:S(2)}) copy-start(bf16[768,1536]{1,0:T(8,128)(2,1)} %param.15) | copy-start | bytes 7077892
  49.2 0.8 copy-start.2
  60.8 0.9 copy-start.1
  113.8 2.7 copy-start.9
  113.8 2.7 copy-start.11
  116.6 1.7 copy-start.8
  116.6 1.7 copy-start.10
  120.0 38.5 %reduce-scatter.12.cloned.1.call-start = ((), (), s32[]{:S(2)}) async-start(), calls=%async_computation.10 | async-start | bytes 1179648 | tf_op jit(solution)/shard_map/reduce_scatter | solution.py:132
  123.5 109.8 %reduce-scatter.18.cloned.1.call-start = ((), (), s32[]{:S(2)}) async-start(), calls=%async_computation.13 | async-start | bytes 1253376 | tf_op jit(solution)/shard_map/reduce_scatter | solution.py:175
  158.5 14.9 %copy-start.13 = (f32[256,384]{1,0:T(8,128)S(1)}, f32[256,384]{1,0:T(8,128)}, u32[]{:S(2)}) copy-start(f32[256,384]{1,0:T(8,128)} %copy-done.12) | copy-start | bytes 1179652
  172.5 0.9 copy-start.5
  175.1 124.3 %reduce-scatter.26.cloned.1.call-start = ((), (), s32[]{:S(2)}) async-start(), calls=%async_computation.17 | async-start | bytes 2506752 | tf_op jit(solution)/shard_map/reduce_scatter | solution.py:187
  178.8 186.3 %reduce-scatter.24.cloned.1.call-start = ((), (), s32[]{:S(2)}) async-start(), calls=%async_computation.16 | async-start | bytes 2506752 | tf_op jit(solution)/shard_map/reduce_scatter | solution.py:184
  182.3 249.1 %reduce-scatter.22.cloned.1.call-start = ((), (), s32[]{:S(2)}) async-start(), calls=%async_computation.15 | async-start | bytes 2506752 | tf_op jit(solution)/shard_map/reduce_scatter | solution.py:181
  186.1 311.0 %reduce-scatter.20.cloned.1.call-start = ((), (), s32[]{:S(2)}) async-start(), calls=%async_computation.14 | async-start | bytes 2506752 | tf_op jit(solution)/shard_map/reduce_scatter | solution.py:178
  189.7 379.0 %reduce-scatter.16.cloned.1.call-start = ((), (), s32[]{:S(2)}) async-start(), calls=%async_computation.12 | async-start | bytes 3760128 | tf_op jit(solution)/shard_map/reduce_scatter | solution.py:172
  189.7 2.5 copy-start.4
Sparse Core Ops, SparseCore 0:
  25.2 21.4 reduce-scatter.9
  120.1 18.6 reduce-scatter.13
  141.0 17.4 reduce-scatter.11
  175.3 58.0 reduce-scatter.17
  237.4 61.9 reduce-scatter.25
  303.1 61.9 reduce-scatter.23
  369.3 62.0 reduce-scatter.21
  435.1 61.9 reduce-scatter.19
  501.5 67.0 reduce-scatter.15
where the time goes:
time: 579 us; the launch traced here: 577 us
  waiting for transfers between devices  393 us (68%)
  matrix products  82.5 us (14%)
  blocking collectives  50.8 us (9%)
  local copies, waits for them, and re-layouts  19.2 us (3%)
  other arithmetic  17.1 us (3%)
  between operations  14.1 us (2%)
    reduce_scatter x1, waiting for transfers between devices, shards(): lax.psum_scatter(dilated_tap_gradient.astype(jnp.bfloat16), 'dp', scatter...  69.9 us
    reduce_scatter x1, waiting for transfers between devices, shards(): lax.psum_scatter(key_grad.astype(jnp.bfloat16), 'dp', scatter_dimension=0...  64.6 us
    reduce_scatter x1, waiting for transfers between devices, shards(): lax.psum_scatter(out_grad.astype(jnp.bfloat16), 'dp', scatter_dimension=1...  64.6 us
    reduce_scatter x1, waiting for transfers between devices, shards(): lax.psum_scatter(query_grad.astype(jnp.bfloat16), 'dp', scatter_dimension...  64.1 us
    reduce_scatter x1, waiting for transfers between devices, shards(): lax.psum_scatter(value_grad.astype(jnp.bfloat16), 'dp', scatter_dimension...  63.9 us
    dot_general x14, matrix products, inner_rows(): lax.dot_general(left_side, right_side, (((0,), (0,)), ((), ())), preferre...  33.1 us
    reduce_scatter x1, waiting for transfers between devices, shards(): lax.psum_scatter(point_grad.astype(jnp.bfloat16), 'dp', scatter_dimension...  31.8 us
    dot_general x14, matrix products, outer_cols(): lax.dot_general(left_side, right_side, (((1,), (1,)), ((), ())), preferre...  25.5 us
  transfers between devices with their start and end apart: 9, of which 8 were waited for; matrix products, arithmetic and copies ran while one was open for 8% of the time, Pallas kernels for 0%

commit v1 on v0

v1 whole, which is shorter than its diff:
```python
import functools
import math

import jax
import jax.numpy as jnp
from jax import lax
from jax.experimental import pallas as pl
from jax.experimental.pallas import tpu as pltpu
from jax.sharding import PartitionSpec as P

HSIZE = 192
DILATION_STEP = 16
EPSILON = 1e-06
SOFT_CAP = 6.0
GELU_C = math.sqrt(2.0 / math.pi)
GELU_A = 0.044715
BF = jnp.bfloat16
F32 = jnp.float32
VMEM_BYTES = 56 * 1024 * 1024


def gelu(x):
    return 0.5 * x * (1.0 + jnp.tanh(GELU_C * (x + GELU_A * (x * x * x))))


def gelu_slope(x):
    t = jnp.tanh(GELU_C * (x + GELU_A * (x * x * x)))
    return 0.5 * (1.0 + t) + 0.5 * x * (1.0 - t * t) * GELU_C * (1.0 + 3.0 * GELU_A * x * x)


def dot_nn(a, b):
    return lax.dot_general(a, b, (((1,), (0,)), ((), ())), preferred_element_type=F32)


def dot_nt(a, b):
    return lax.dot_general(a, b, (((1,), (1,)), ((), ())), preferred_element_type=F32)


def dot_tn(a, b):
    return lax.dot_general(a, b, (((0,), (0,)), ((), ())), preferred_element_type=F32)


def rms_scale(x):
    return lax.rsqrt(jnp.mean(x * x, axis=-1, keepdims=True) + EPSILON)


def row_chunk(rows):
    return 128 if rows % 128 == 0 else rows


def loop_chunks(count, body):
    if count <= 2:
        for i in range(count):
            body(i)
    else:

        def step(i, carry):
            body(i)
            return carry

        lax.fori_loop(0, count, step, 0)


def rows_at(i, size):
    if isinstance(i, int):
        return pl.ds(i * size, size)
    return pl.ds(pl.multiple_of(i * size, size), size)


def emit_rows(starts, wide, outs):
    group = len(outs)
    for p in range(group):
        out = outs[p]
        ring = starts.shape[0] // group
        size = out.shape[0] // ring
        for k in range(ring):
            at = pl.multiple_of(starts[p * ring + k], 16)
            out[k * size : (k + 1) * size, :] = wide[pl.ds(at, size), :]


def shifted_sum(first, middle, last, offset):
    length = middle.shape[0]
    step = DILATION_STEP
    pos = lax.rem(lax.broadcasted_iota(jnp.int32, (length, 1), 0) + offset, length)
    down = jnp.concatenate([first[length - step :], first[: length - step]], axis=0)
    up = jnp.concatenate([last[step:], last[:step]], axis=0)
    return jnp.where(pos >= step, down, 0.0) + middle + jnp.where(pos < length - step, up, 0.0)


def call(kernel, out_shape, operands, smem=1, scratch=(), flops=0):
    specs = [pl.BlockSpec(memory_space=pltpu.SMEM)] * smem
    specs += [pl.BlockSpec(memory_space=pltpu.VMEM)] * (len(operands) - smem)
    moved = sum(math.prod(t.shape) * t.dtype.itemsize for t in list(operands) + list(out_shape))
    return pl.pallas_call(
        kernel,
        out_shape=out_shape,
        in_specs=specs,
        out_specs=[pl.BlockSpec(memory_space=pltpu.VMEM)] * len(out_shape),
        scratch_shapes=list(scratch),
        compiler_params=pltpu.CompilerParams(vmem_limit_bytes=VMEM_BYTES),
        cost_estimate=pl.CostEstimate(flops=flops, bytes_accessed=moved, transcendentals=0),
    )(*operands)


def shape_of(rows, cols, dtype=BF):
    return jax.ShapeDtypeStruct((rows, cols), dtype)


def conv_block(starts, offset, pieces, taps, point, ring_rows, group):
    count = len(pieces)
    rows = pieces[0].shape[0]
    length, channels = rows * count, pieces[0].shape[1]
    inner = point.shape[0]

    def kernel(*refs):
        starts_ref, offset_ref = refs[:2]
        ins = refs[2 : 2 + count]
        taps_ref, point_ref = refs[2 + count : 4 + count]
        pre_ref, mid_ref, part_ref = refs[4 + count : 7 + count]
        sent = refs[7 + count : 7 + count + group]
        act, wide, prod = refs[7 + count + group :]
        size = row_chunk(rows)
        for j in range(count):

            def body(i, j=j):
                x = ins[j][rows_at(i, size), :].astype(F32)
                a = gelu(x * rms_scale(x)).astype(BF)
                if isinstance(i, int):
                    here = pl.ds(j * rows + i * size, size)
                else:
                    here = pl.ds(pl.multiple_of(j * rows + i * size, size), size)
                act[here, :] = a
                wide[:, here] = a.T

            loop_chunks(rows // size, body)
        emit_rows(starts_ref, wide, sent)
        big = min(256, length)

        def product(i):
            here = rows_at(i, big)
            prod[here, :] = dot_nt(act[here, :], taps_ref[...])

        loop_chunks(length // big, product)
        pre = shifted_sum(
            prod[:, :inner], prod[:, inner : 2 * inner], prod[:, 2 * inner :], offset_ref[0]
        )
        pre_ref[...] = pre
        mid_ref[...] = gelu(pre).astype(BF)

        def back(i):
            here = rows_at(i, big)
            part_ref[here, :] = dot_nn(mid_ref[here, :], point_ref[...]).astype(BF)

        loop_chunks(length // big, back)

    outs = [shape_of(length, inner, F32), shape_of(length, inner), shape_of(length, channels)]
    outs += [shape_of(ring_rows, length)] * group
    scratch = [
        pltpu.VMEM((length, channels), BF),
        pltpu.VMEM((channels, length), BF),
        pltpu.VMEM((length, 3 * inner), F32),
    ]
    res = call(
        kernel, outs, [starts, offset, *pieces, taps, point], 2, scratch, 8 * length * inner * channels
    )
    return res[0], res[1], res[2], res[3:]


def norm_block(starts, pieces, part, moved, ring_rows, group):
    count = len(pieces)
    rows = pieces[0].shape[0]
    length, channels = part.shape

    def kernel(*refs):
        starts_ref = refs[0]
        ins = refs[1 : 1 + count]
        part_ref = refs[1 + count]
        adds = refs[2 + count : 2 + count + len(moved)]
        rest = refs[2 + count + len(moved) :]
        res_ref, norm_ref = rest[:2]
        sent = rest[2 : 2 + group]
        wide = rest[2 + group]
        size = row_chunk(rows)
        for j in range(count):

            def body(i, j=j):
                if isinstance(i, int):
                    here = pl.ds(j * rows + i * size, size)
                else:
                    here = pl.ds(pl.multiple_of(j * rows + i * size, size), size)
                total = part_ref[here, :].astype(F32)
                if adds:
                    total = total + adds[j][rows_at(i, size), :].astype(F32)
                res = (ins[j][rows_at(i, size), :].astype(F32) + total).astype(BF)
                res_ref[here, :] = res
                res = res.astype(F32)
                a = (res * rms_scale(res)).astype(BF)
                norm_ref[here, :] = a
                wide[:, here] = a.T

            loop_chunks(rows // size, body)
        emit_rows(starts_ref, wide, sent)

    outs = [shape_of(length, channels), shape_of(length, channels)]
    outs += [shape_of(ring_rows, length)] * group
    scratch = [pltpu.VMEM((channels, length), BF)]
    res = call(kernel, outs, [starts, *pieces, part, *moved], 1, scratch)
    return res[0], res[1], res[2:]


def widen_block(starts, pieces, ring_rows, group):
    count = len(pieces)
    rows, channels = pieces[0].shape
    length = rows * count

    def kernel(*refs):
        starts_ref = refs[0]
        ins = refs[1 : 1 + count]
        whole_ref = refs[1 + count]
        sent = refs[2 + count : 2 + count + group]
        wide = refs[2 + count + group]
        size = row_chunk(rows)
        for j in range(count):

            def body(i, j=j):
                if isinstance(i, int):
                    here = pl.ds(j * rows + i * size, size)
                else:
                    here = pl.ds(pl.multiple_of(j * rows + i * size, size), size)
                a = ins[j][rows_at(i, size), :]
                whole_ref[here, :] = a
                wide[:, here] = a.T

            loop_chunks(rows // size, body)
        emit_rows(starts_ref, wide, sent)

    outs = [shape_of(length, channels)] + [shape_of(ring_rows, length)] * group
    scratch = [pltpu.VMEM((channels, length), BF)]
    res = call(kernel, outs, [starts, *pieces], 1, scratch)
    return res[0], res[1:]


def attention_block(normed, grad_y, query_w, key_w, value_w, out_w):
    length, channels = normed.shape
    features = query_w.shape[0]
    heads = features // HSIZE
    per_step = 2 if heads % 2 == 0 else 1
    width = per_step * HSIZE
    inv_root = 1.0 / math.sqrt(HSIZE)
    chunk = min(256, length)

    def kernel(n_ref, gy_ref, wq, wk, wv, wo, dq_ref, dk_ref, dv_ref, at_ref, dn_ref, acc):
        step = pl.program_id(0)
        n = n_ref[...]
        gy = gy_ref[...]
        dqs, dks, dvs, ats = [], [], [], []
        for h in range(per_step):
            rows = pl.ds(h * HSIZE, HSIZE)
            q = dot_nt(n, wq[rows, :]).astype(BF)
            k = dot_nt(n, wk[rows, :]).astype(BF)
            v = dot_nt(n, wv[rows, :]).astype(BF)
            g = dot_nt(gy, wo[rows, :]).astype(BF)
            dq, at = [], []
            dk = dv = None
            for c in range(length // chunk):
                qc = q[c * chunk : (c + 1) * chunk]
                gc = g[c * chunk : (c + 1) * chunk]
                ratio = jnp.tanh(dot_nt(qc, k) * (inv_root / SOFT_CAP))
                unnormed = jnp.exp(SOFT_CAP * ratio)
                soft = unnormed / jnp.sum(unnormed, axis=-1, keepdims=True)
                low = soft.astype(BF)
                at.append(dot_nn(low, v))
                gs = dot_nt(gc, v)
                gs = soft * (gs - jnp.sum(soft * gs, axis=-1, keepdims=True))
                gs = (gs * (1.0 - ratio * ratio)).astype(BF)
                dq.append(dot_nn(gs, k) * inv_root)
                dk_c = dot_tn(gs, qc)
                dv_c = dot_tn(low, gc)
                dk = dk_c if dk is None else dk + dk_c
                dv = dv_c if dv is None else dv + dv_c
            join = (lambda parts: parts[0] if len(parts) == 1 else jnp.concatenate(parts, axis=0))
            dqs.append(join(dq))
            ats.append(join(at))
            dks.append(dk * inv_root)
            dvs.append(dv)
        side = (lambda parts: parts[0] if len(parts) == 1 else jnp.concatenate(parts, axis=1))
        dq, dk, dv, at = [side(t).astype(BF) for t in (dqs, dks, dvs, ats)]
        dq_ref[...] = dq
        dk_ref[...] = dk
        dv_ref[...] = dv
        at_ref[...] = at
        total = dot_nn(dq, wq[...]) + dot_nn(dk, wk[...]) + dot_nn(dv, wv[...])

        @pl.when(step == 0)
        def _():
            acc[...] = total

        @pl.when(step > 0)
        def _():
            acc[...] += total

        @pl.when(step == pl.num_programs(0) - 1)
        def _():
            dn_ref[...] = acc[...].astype(BF)

    whole = pl.BlockSpec((length, channels), lambda i: (0, 0))
    weight = pl.BlockSpec((width, channels), lambda i: (i, 0))
    column = pl.BlockSpec((length, width), lambda i: (0, i))
    return pl.pallas_call(
        kernel,
        grid=(heads // per_step,),
        out_shape=[shape_of(length, features)] * 4 + [shape_of(length, channels)],
        in_specs=[whole, whole, weight, weight, weight, weight],
        out_specs=[column] * 4 + [whole],
        scratch_shapes=[pltpu.VMEM((length, channels), F32)],
        compiler_params=pltpu.CompilerParams(vmem_limit_bytes=VMEM_BYTES),
        cost_estimate=pl.CostEstimate(
            flops=14 * length * features * channels + 12 * length * length * features,
            bytes_accessed=2 * (4 * features * channels + 3 * length * channels),
            transcendentals=2 * heads * length * length,
        ),
    )(normed, grad_y, query_w, key_w, value_w, out_w)


def back_block(starts, residual, grad_y, part, moved, pre, point, ring_rows, group):
    length, channels = residual.shape
    inner = point.shape[0]
    rows = length // max(1, len(moved))

    def kernel(*refs):
        starts_ref, res_ref, gy_ref, part_ref = refs[:4]
        adds = refs[4 : 4 + len(moved)]
        pre_ref, point_ref = refs[4 + len(moved) : 6 + len(moved)]
        rest = refs[6 + len(moved) :]
        gc_ref = rest[0]
        sent = rest[1 : 1 + group]
        wide, resid_grad = rest[1 + group :]
        size = row_chunk(rows)
        for j in range(length // rows):

            def body(i, j=j):
                if isinstance(i, int):
                    here = pl.ds(j * rows + i * size, size)
                else:
                    here = pl.ds(pl.multiple_of(j * rows + i * size, size), size)
                gn = part_ref[here, :].astype(F32)
                if adds:
                    gn = gn + adds[j][rows_at(i, size), :].astype(F32)
                res = res_ref[here, :].astype(F32)
                scale = rms_scale(res)
                inner_mean = jnp.mean(gn * res, axis=-1, keepdims=True)
                a = gy_ref[here, :].astype(F32) + (
                    scale * gn - res * (scale * scale * scale) * inner_mean
                )
                a = a.astype(BF)
                resid_grad[here, :] = a
                wide[:, here] = a.T

            loop_chunks(rows // size, body)
        big = min(256, length)

        def product(i):
            here = rows_at(i, big)
            gm = dot_nt(resid_grad[here, :], point_ref[...])
            gc_ref[here, :] = (gelu_slope(pre_ref[here, :]) * gm).astype(BF)

        loop_chunks(length // big, product)
        emit_rows(starts_ref, wide, sent)

    outs = [shape_of(length, inner)] + [shape_of(ring_rows, length)] * group
    scratch = [pltpu.VMEM((channels, length), BF), pltpu.VMEM((length, channels), BF)]
    res = call(
        kernel,
        outs,
        [starts, residual, grad_y, part, *moved, pre, point],
        1,
        scratch,
        2 * length * inner * channels,
    )
    return res[0], res[1:]


def weight_sum(wides, narrows):
    group = len(wides)
    rows, length = wides[0].shape
    cols = narrows[0].shape[1]

    def kernel(*refs):
        total = None
        for a, b in zip(refs[:group], refs[group : 2 * group]):
            term = dot_nn(a[...], b[...])
            total = term if total is None else total + term
        refs[-1][...] = total.astype(BF)

    return call(
        kernel,
        [shape_of(rows, cols)],
        [*wides, *narrows],
        0,
        (),
        2 * group * rows * length * cols,
    )[0]


def tap_sum(offset, wides, narrows):
    group = len(wides)
    rows, length = wides[0].shape
    inner = narrows[0].shape[1]
    step = DILATION_STEP

    def kernel(offset_ref, *refs):
        pos = lax.rem(
            lax.broadcasted_iota(jnp.int32, (length, 1), 0) + offset_ref[0], length
        )
        total = [None, None, None]
        for a_ref, b_ref in zip(refs[:group], refs[group : 2 * group]):
            a = a_ref[...]
            b = b_ref[...]
            up = jnp.concatenate([b[step:], b[:step]], axis=0).astype(F32)
            down = jnp.concatenate([b[length - step :], b[: length - step]], axis=0).astype(F32)
            first = jnp.where(pos < length - step, up, 0.0).astype(BF)
            last = jnp.where(pos >= step, down, 0.0).astype(BF)
            for k, moved in enumerate((first, b, last)):
                term = dot_nn(a, moved)
                total[k] = term if total[k] is None else total[k] + term
        for k in range(3):
            refs[-1][:, k * inner : (k + 1) * inner] = total[k].astype(BF)

    return call(
        kernel,
        [shape_of(rows, 3 * inner)],
        [offset, *wides, *narrows],
        1,
        (),
        6 * group * rows * length * inner,
    )[0]


def shards(
    inputs,
    dilated_tap_weight,
    point_weight,
    query_weight,
    key_weight,
    value_weight,
    out_weight,
    cotangent,
):
    channels = inputs.shape[2]
    own = inputs[0]
    rows = own.shape[0]
    n_seq = lax.axis_size("seq")
    n_dp = lax.axis_size("dp")
    length = rows * n_seq
    pair = n_seq == 2
    group = 4 if n_dp % 4 == 0 else 2 if n_dp % 2 == 0 else 1
    ring = n_dp // group
    block = channels // n_dp
    ring_rows = ring * block
    inner = point_weight.shape[0]
    features = query_weight.shape[0]
    inv_tokens = 1.0 / math.sqrt(inputs.shape[0] * n_dp * length)

    me_dp = lax.axis_index("dp")
    me_seq = lax.axis_index("seq")
    me_ring, me_group = me_dp // group, me_dp % group
    order = jnp.arange(group, dtype=jnp.int32)[:, None]
    turn = jnp.arange(ring, dtype=jnp.int32)[None, :]
    starts = (((me_ring + turn) % ring * group + (me_group ^ order)) * block).reshape(-1)
    starts = starts.astype(jnp.int32)
    offset = (me_seq * rows if pair else jnp.int32(0)).astype(jnp.int32).reshape(1)

    def swap_seq(x):
        return lax.ppermute(x, "seq", [(0, 1), (1, 0)])

    def to_peer(x, bits):
        if bits == 0:
            return x
        return lax.ppermute(x, "dp", [(i, i ^ bits) for i in range(n_dp)])

    def gather_seq(x):
        if pair:
            return [x, swap_seq(x)]
        return [lax.all_gather(x, "seq", axis=0, tiled=True)]

    def add_seq(part):
        if pair:
            return part, [swap_seq(part[rows:]), swap_seq(part[:rows])]
        summed = lax.psum_scatter(part, "seq", scatter_dimension=0, tiled=True)
        return lax.all_gather(summed, "seq", axis=0, tiled=True), []

    def share_wide(pieces):
        return [to_peer(piece, p) for p, piece in enumerate(pieces)]

    def share_narrow(x):
        got = [x]
        if group >= 2:
            got.append(to_peer(x, 1))
        if group >= 4:
            far = to_peer(x, 2)
            got += [far, to_peer(far, 1)]
        return got

    def reduce_ring(total):
        out = total[:block].astype(F32)
        for k in range(1, ring):
            hops = [(i, ((i // group + k) % ring) * group + i % group) for i in range(n_dp)]
            moved = lax.ppermute(total[k * block : (k + 1) * block], "dp", hops)
            out = out + moved.astype(F32)
        return out

    pieces = gather_seq(own)
    grad_own = (cotangent[0].astype(F32) * inv_tokens).astype(BF)
    taps = dilated_tap_weight.reshape(3 * inner, channels)
    pre, middle, part, act_sent = conv_block(
        starts, offset, pieces, taps, point_weight, ring_rows, group
    )
    grad_pieces = gather_seq(grad_own)
    part, moved = add_seq(part)
    grad_y, grad_sent = widen_block(starts, grad_pieces, ring_rows, group)
    residual, normed, norm_sent = norm_block(starts, pieces, part, moved, ring_rows, group)
    act_wide = share_wide(act_sent)
    middle_all = share_narrow(middle)
    grad_wide = share_wide(grad_sent)
    norm_wide = share_wide(norm_sent)

    dq, dk, dv, attended, grad_part = attention_block(
        normed, grad_y, query_weight, key_weight, value_weight, out_weight
    )
    grad_part, grad_moved = add_seq(grad_part)

    attn_part = dot_nn(attended, out_weight).astype(BF)
    if pair:
        attn_rows = attn_part[:rows].astype(F32) + swap_seq(attn_part[rows:]).astype(F32)
    else:
        attn_rows = lax.psum_scatter(attn_part, "seq", scatter_dimension=0, tiled=True)
        attn_rows = attn_rows.astype(F32)
    if pair:
        res_own = residual[:rows]
    else:
        res_own = lax.dynamic_slice_in_dim(residual, me_seq * rows, rows, 0)
    output = (res_own.astype(F32) + attn_rows).astype(BF)[None]

    query_sum = reduce_ring(weight_sum(norm_wide, share_narrow(dq)))
    key_sum = reduce_ring(weight_sum(norm_wide, share_narrow(dk)))
    value_sum = reduce_ring(weight_sum(norm_wide, share_narrow(dv)))
    out_sum = reduce_ring(weight_sum(grad_wide, share_narrow(attended))).T

    grad_conv, resid_sent = back_block(
        starts, residual, grad_y, grad_part, grad_moved, pre, point_weight, ring_rows, group
    )
    tap_total = reduce_ring(tap_sum(offset, act_wide, share_narrow(grad_conv)))
    tap_total = tap_total.reshape(block, 3, inner).transpose(1, 0, 2)
    point_sum = reduce_ring(weight_sum(share_wide(resid_sent), middle_all)).T
    return (output, tap_total, point_sum, query_sum, key_sum, value_sum, out_sum)


def solution(mesh):
    placed = (
        P("dp", "seq", None),
        P(None, "seq", None),
        P("seq", None),
        P("seq", None),
        P("seq", None),
        P("seq", None),
        P("seq", None),
        P("dp", "seq", None),
    )
    return jax.shard_map(
        shards,
        mesh=mesh,
        in_specs=placed,
        out_specs=(
            P("dp", "seq", None),
            P(None, "dp", "seq"),
            P("seq", "dp"),
            P("dp", "seq"),
            P("dp", "seq"),
            P("dp", "seq"),
            P("seq", "dp"),
        ),
        check_vma=False,
    )
```

time: 579 us -> 237 us (0.41)
  waiting for transfers between devices: 393 us -> 100 us
  matrix products: 82.5 us -> 2.43 us
  starting transfers between devices: 0.55 us -> 58.5 us
  blocking collectives: 50.8 us -> 0 us
  Pallas kernels: 0 us -> 49.8 us
  between operations: 14.1 us -> 1.16 us
  other arithmetic: 17.1 us -> 9.62 us
  local copies, waits for them, and re-layouts: 19.2 us -> 12.6 us
    reduce_scatter x9 -> x0, waiting for transfers between devices: 393 us -> none  [the longest x1 69.9 us: shards(): lax.psum_scatter(dilated_tap_gradient.astype(jnp.bfloat16), 'dp', scatter...]
    ppermute x0 -> x55, waiting for transfers between devices: none -> 100 us  [the longest x30 43.9 us: to_peer(): return lax.ppermute(x, 'dp', [(i, i ^ bits) for i in range(n_dp)])]
    dot_general x41 -> x1, matrix products: 82.5 us -> 2.43 us  [dot_nn(): lax.dot_general(a, b, (((1,), (0,)), ((), ())), preferred_element_type=F32)]
    ppermute x0 -> x55, starting transfers between devices: none -> 58.5 us  [the longest x18 35 us: reduce_ring(): moved = lax.ppermute(total[k * block:(k + 1) * block], 'dp', hops)]
    all_gather x4 -> x0, blocking collectives: 50.8 us -> none  [the longest x1 15.5 us: shards(): grad_y = lax.all_gather(grad_rows_low, 'seq', axis=0, tiled=True)]
    pallas_call x0 -> x11, Pallas kernels: none -> 49.8 us  [the longest x10 36.2 us: call(): pl.pallas_call(kernel, out_shape=out_shape, in_specs=specs, out_specs=[pl...]
    convert_element_type x14 -> x1, other arithmetic: 15.3 us -> 1.06 us  [shards(): grad_own = (cotangent[0].astype(F32) * inv_tokens).astype(BF)]
    convert_element_type x5 -> x0, local copies, waits for them, and re-layouts: 13.7 us -> none  [the longest x1 6.04 us: shards(): dilated_tap_gradient.astype(jnp.bfloat16)]
  transfers between devices with their start and end apart: 9 -> 55, of which waited for: 8 -> 19; matrix products, arithmetic and copies ran while one was open for 8% -> 7% of each run, Pallas kernels for 0% -> 14%
where the time goes in v1:
time: 237 us; the launch traced here: 234 us
  waiting for transfers between devices  100 us (42%)
  starting transfers between devices  58.5 us (25%)
  Pallas kernels  49.8 us (21%)
  local copies, waits for them, and re-layouts  12.6 us (5%)
  other arithmetic  9.62 us (4%)
  matrix products  2.43 us (1%)
    ppermute x30, waiting for transfers between devices, to_peer(): return lax.ppermute(x, 'dp', [(i, i ^ bits) for i in range(n_dp)])  43.9 us
    pallas_call x10, Pallas kernels, call(): pl.pallas_call(kernel, out_shape=out_shape, in_specs=specs, out_specs=[pl...  36.2 us
    ppermute x18, starting transfers between devices, reduce_ring(): moved = lax.ppermute(total[k * block:(k + 1) * block], 'dp', hops)  35 us
    ppermute x18, waiting for transfers between devices, reduce_ring(): moved = lax.ppermute(total[k * block:(k + 1) * block], 'dp', hops)  28 us
    ppermute x7, waiting for transfers between devices, swap_seq(): return lax.ppermute(x, 'seq', [(0, 1), (1, 0)])  28 us
    ppermute x30, starting transfers between devices, to_peer(): return lax.ppermute(x, 'dp', [(i, i ^ bits) for i in range(n_dp)])  14.6 us
    pallas_call x1, Pallas kernels, attention_block(): pl.pallas_call(kernel, grid=(heads // per_step,), out_shape=[shape_of(len...  13.6 us
    ppermute x7, starting transfers between devices, swap_seq(): return lax.ppermute(x, 'seq', [(0, 1), (1, 0)])  8.92 us
  transfers between devices with their start and end apart: 55, of which 19 were waited for; matrix products, arithmetic and copies ran while one was open for 7% of the time, Pallas kernels for 14%

profile of v1, /device:TPU:0, one launch (start us, length us, event | category | flops | bytes accessed | tf_op | source)
XLA Modules:
  0.0 234.0 jit_solution(8748470882391819118)
XLA Ops:
  5.5 8.3 %collective-permute-done.refs_3_.refs_2_ = bf16[128,1536]{1,0:T(8,128)(2,1)S(1)} collective-permute-done((bf16[128,1536]{1,0:T(8,128)(2,1)}, bf16[128,1536]{1,0:T(8,128)(2,1)S(1)}, u32[]{:S(2)}, u32[]{:S(2)}) %collective-permute-start) | collective-permute-done | bytes 393248 | tf_op jit(solution)/shard_map/ppermute | solution.py:474
  14.6 6.0 %shard_map.135 = (f32[256,384]{1,0:T(8,128)}, bf16[256,384]{1,0:T(8,128)(2,1)}, bf16[256,1536]{1,0:T(8,128)(2,1)}, bf16[384,256]{1,0:T(8,128)(2,1)}, bf16[384,25...) custom-call(s32[16]{0:T(128)} %mul.27.refs_0_, s32[1]{0:T(128)} %bitcast.1.refs_1_.offset_ref, ...), custom_call_target="tpu_custom_call" | custom-call | flops 1207959552 | bytes 7667780 | tf_op jit(solution)/shard_map/pallas_call | solution.py:94
  27.2 6.8 %collective-permute-done.1.refs_4_ = bf16[128,1536]{1,0:T(8,128)(2,1)S(1)} collective-permute-done((bf16[128,1536]{1,0:T(8,128)(2,1)S(1)}, bf16[128,1536]{1,0:T(8,128)(2,1)S(1)}, u32[]{:S(2)}, u32[]{:S(2)}) %collective-permute-start.1) | collective-permute-done | bytes 393248 | tf_op jit(solution)/shard_map/ppermute | solution.py:474
  33.9 5.8 %collective-permute-done.2.refs_5_ = bf16[128,1536]{1,0:T(8,128)(2,1)S(1)} collective-permute-done((bf16[128,1536]{1,0:T(8,128)(2,1)S(1)}, bf16[128,1536]{1,0:T(8,128)(2,1)S(1)}, u32[]{:S(2)}, u32[]{:S(2)}) %collective-permute-start.2) | collective-permute-done | bytes 393248 | tf_op jit(solution)/shard_map/ppermute | solution.py:474
  40.5 3.5 %shard_map.136 = (bf16[256,1536]{1,0:T(8,128)(2,1)}, bf16[256,1536]{1,0:T(8,128)(2,1)}, bf16[384,256]{1,0:T(8,128)(2,1)}, bf16[384,256]{1,0:T(8,128)(2,1)}, bf16...) custom-call(s32[16]{0:T(128)} %mul.27.refs_0_, bf16[128,1536]{1,0:T(8,128)(2,1)} %bitcast.18, bf16[128,1536]{1,0:T(8,128)(2,1)} %copy-done.6, ...), custom_call_target="tpu_custom_call" | custom-call | bytes 4718656 | tf_op jit(solution)/shard_map/pallas_call | solution.py:94
  44.1 13.6 %shard_map.138 = (bf16[256,768]{1,0:T(8,128)(2,1)}, bf16[256,768]{1,0:T(8,128)(2,1)}, bf16[256,768]{1,0:T(8,128)(2,1)}, bf16[256,768]{1,0:T(8,128)(2,1)}, bf16[256,1536]{1,0:T(8,128)(2,1)}) custom-call(bf16[256,1536]{1,0:T(8,128)(2,1)} %get-tuple-element.37.n_ref, bf16[256,1536]{1,0:T(8,128)(2,1)} %get-tuple-element.38.gy_ref.refs_2_, bf16[768,1536]{1,0:T(8,128)(2,1)} %wq.1, ...), custom_call_target="tpu_custom_call" | custom-call | flops 4831838208 | bytes 11796480 | tf_op jit(solution)/shard_map/pallas_call | solution.py:309
  64.0 4.7 %collective-permute-done.20.refs_6_ = bf16[256,384]{1,0:T(8,128)(2,1)S(1)} collective-permute-done((bf16[256,384]{1,0:T(8,128)(2,1)S(1)}, bf16[256,384]{1,0:T(8,128)(2,1)S(1)}, u32[]{:S(2)}, u32[]{:S(2)}) %collective-permute-start.20) | collective-permute-done | bytes 196640 | tf_op jit(solution)/shard_map/ppermute | solution.py:479
  70.9 4.9 %collective-permute-done.9.refs_5_ = bf16[128,1536]{1,0:T(8,128)(2,1)S(1)} collective-permute-done((bf16[128,1536]{1,0:T(8,128)(2,1)S(1)}, bf16[128,1536]{1,0:T(8,128)(2,1)S(1)}, u32[]{:S(2)}, u32[]{:S(2)}) %collective-permute-start.9) | collective-permute-done | bytes 393248 | tf_op jit(solution)/shard_map/ppermute | solution.py:474
  76.6 4.5 %shard_map.139 = (bf16[256,384]{1,0:T(8,128)(2,1)}, bf16[384,256]{1,0:T(8,128)(2,1)}, bf16[384,256]{1,0:T(8,128)(2,1)}, bf16[384,256]{1,0:T(8,128)(2,1)}, bf16[384,256]{1,0:T(8,128)(2,1)}) custom-call(s32[16]{0:T(128)} %mul.27.refs_0_, bf16[256,1536]{1,0:T(8,128)(2,1)} %get-tuple-element.36.refs_1_, bf16[256,1536]{1,0:T(8,128)(2,1)} %get-tuple-element.38.gy_ref.refs_2_, ...), custom_call_target="tpu_custom_call" | custom-call | flops 301989888 | bytes 5701696 | tf_op jit(solution)/shard_map/pallas_call | solution.py:94
  87.7 9.7 %collective-permute-done.26.refs_2_ = bf16[384,256]{1,0:T(8,128)(2,1)S(1)} collective-permute-done((bf16[384,256]{1,0:T(8,128)(2,1)S(1)}, bf16[384,256]{1,0:T(8,128)(2,1)S(1)}, u32[]{:S(2)}, u32[]{:S(2)}) %collective-permute-start.26) | collective-permute-done | bytes 196640 | tf_op jit(solution)/shard_map/ppermute | solution.py:479
  98.4 3.3 %collective-permute-done.17.refs_2_ = bf16[384,256]{1,0:T(8,128)(2,1)S(1)} collective-permute-done((bf16[384,256]{1,0:T(8,128)(2,1)}, bf16[384,256]{1,0:T(8,128)(2,1)S(1)}, u32[]{:S(2)}, u32[]{:S(2)}) %collective-permute-start.17) | collective-permute-done | bytes 196640 | tf_op jit(solution)/shard_map/ppermute | solution.py:479
  114.3 7.2 %collective-permute-done.35.refs_6_ = bf16[256,768]{1,0:T(8,128)(2,1)S(1)} collective-permute-done((bf16[256,768]{1,0:T(8,128)(2,1)S(1)}, bf16[256,768]{1,0:T(8,128)(2,1)S(1)}, u32[]{:S(2)}, u32[]{:S(2)}) %collective-permute-start.35) | collective-permute-done | bytes 393248 | tf_op jit(solution)/shard_map/ppermute | solution.py:479
  131.7 3.3 %shard_map.145 = bf16[384,768]{1,0:T(8,128)(2,1)} custom-call(bf16[384,256]{1,0:T(8,128)(2,1)} %get-tuple-element.59.refs_0_, bf16[384,256]{1,0:T(8,128)(2,1)} %copy-done.29, bf16[384,256]{1,0:T(8,128)(2,1)} %copy-done.30, bf16[384,256]{1,0:T(8,128)(2,1)} %copy-done.31, bf16[256,768]{1,0:T(8,128)(2,1)} %get-tuple-element.39.refs_4_, ...), custom_call_target="tpu_custom_call" | custom-call | flops 603979776 | bytes 2949120 | tf_op jit(solution)/shard_map/pallas_call | solution.py:94
  138.0 3.3 %shard_map.144 = bf16[384,768]{1,0:T(8,128)(2,1)} custom-call(bf16[384,256]{1,0:T(8,128)(2,1)} %get-tuple-element.52.refs_0_, bf16[384,256]{1,0:T(8,128)(2,1)} %copy-done.2, bf16[384,256]{1,0:T(8,128)(2,1)} %copy-done.3, bf16[384,256]{1,0:T(8,128)(2,1)} %copy-done.4, bf16[256,768]{1,0:T(8,128)(2,1)} %get-tuple-element.58.refs_4_, ...), custom_call_target="tpu_custom_call" | custom-call | flops 603979776 | bytes 2949120 | tf_op jit(solution)/shard_map/pallas_call | solution.py:94
  146.9 13.3 %collective-permute-done.11.refs_6_ = bf16[256,384]{1,0:T(8,128)(2,1)S(1)} collective-permute-done((bf16[256,384]{1,0:T(8,128)(2,1)S(1)}, bf16[256,384]{1,0:T(8,128)(2,1)S(1)}, u32[]{:S(2)}, u32[]{:S(2)}) %collective-permute-start.11) | collective-permute-done | bytes 196640 | tf_op jit(solution)/shard_map/ppermute | solution.py:479
  167.1 3.8 %shard_map.140 = bf16[384,1152]{1,0:T(8,128)(2,1)} custom-call(s32[1]{0:T(128)} %bitcast.1.refs_1_.offset_ref, bf16[384,256]{1,0:T(8,128)(2,1)} %get-tuple-element.40.refs_0_, bf16[384,256]{1,0:T(8,128)(2,1)} %copy-done.46, bf16[384,256]{1,0:T(8,128)(2,1)} %copy-done.48, bf16[384,256]{1,0:T(8,128)(2,1)} %copy-done.49, ...), custom_call_target="tpu_custom_call" | custom-call | flops 905969664 | bytes 2457604 | tf_op jit(solution)/shard_map/pallas_call | solution.py:94
  181.2 5.2 %collective-permute-start.38 = (bf16[96,768]{1,0:T(8,128)(2,1)S(1)}, bf16[96,768]{1,0:T(8,128)(2,1)S(1)}, u32[]{:S(2)}, u32[]{:S(2)}) collective-permute-start(bf16[96,768]{1,0:T(8,128)(2,1)S(1)} %get-tuple-element.85), channel_id=1, source_target_pairs={{0,16},{2,18},{4,20},{6,22},{8,24},{10,26},{12,28},{14,30},{16,0},... | collective-permute-start | bytes 442376 | tf_op jit(solution)/shard_map/ppermute | solution.py:508
  187.2 3.7 %collective-permute-start.39 = (bf16[96,768]{1,0:T(8,128)(2,1)S(1)}, bf16[96,768]{1,0:T(8,128)(2,1)S(1)}, u32[]{:S(2)}, u32[]{:S(2)}) collective-permute-start(bf16[96,768]{1,0:T(8,128)(2,1)S(1)} %get-tuple-element.84), channel_id=1, source_target_pairs={{0,24},{2,26},{4,28},{6,30},{8,0},{10,2},{12,4},{14,6},{16,8},{18,... | collective-permute-start | bytes 442376 | tf_op jit(solution)/shard_map/ppermute | solution.py:508
  190.9 4.8 %collective-permute-done.44 = bf16[96,768]{1,0:T(8,128)(2,1)S(1)} collective-permute-done((bf16[96,768]{1,0:T(8,128)(2,1)S(1)}, bf16[96,768]{1,0:T(8,128)(2,1)S(1)}, u32[]{:S(2)}, u32[]{:S(2)}) %collective-permute-start.44) | collective-permute-done | bytes 147488 | tf_op jit(solution)/shard_map/ppermute | solution.py:508
  196.7 3.4 %collective-permute-start.32 = (bf16[96,768]{1,0:T(8,128)(2,1)S(1)}, bf16[96,768]{1,0:T(8,128)(2,1)S(1)}, u32[]{:S(2)}, u32[]{:S(2)}) collective-permute-start(bf16[96,768]{1,0:T(8,128)(2,1)S(1)} %get-tuple-element.88), channel_id=1, source_target_pairs={{0,16},{2,18},{4,20},{6,22},{8,24},{10,26},{12,28},{14,30},{16,0},... | collective-permute-start | bytes 442376 | tf_op jit(solution)/shard_map/ppermute | solution.py:508
  202.5 5.8 %collective-permute-done.38 = bf16[96,768]{1,0:T(8,128)(2,1)S(1)} collective-permute-done((bf16[96,768]{1,0:T(8,128)(2,1)S(1)}, bf16[96,768]{1,0:T(8,128)(2,1)S(1)}, u32[]{:S(2)}, u32[]{:S(2)}) %collective-permute-start.38) | collective-permute-done | bytes 147488 | tf_op jit(solution)/shard_map/ppermute | solution.py:508
  209.3 3.4 %collective-permute-start.14 = (bf16[96,1152]{1,0:T(8,128)(2,1)S(1)}, bf16[96,1152]{1,0:T(8,128)(2,1)S(1)}, u32[]{:S(2)}, u32[]{:S(2)}) collective-permute-start(bf16[96,1152]{1,0:T(8,128)(2,1)S(1)} %get-tuple-element.72), channel_id=1, source_target_pairs={{0,16},{2,18},{4,20},{6,22},{8,24},{10,26},{12,28},{14,30},{16,0},... | collective-permute-start | bytes 663560 | tf_op jit(solution)/shard_map/ppermute | solution.py:508
  216.1 8.0 %collective-permute-done.32 = bf16[96,768]{1,0:T(8,128)(2,1)S(1)} collective-permute-done((bf16[96,768]{1,0:T(8,128)(2,1)S(1)}, bf16[96,768]{1,0:T(8,128)(2,1)S(1)}, u32[]{:S(2)}, u32[]{:S(2)}) %collective-permute-start.32) | collective-permute-done | bytes 147488 | tf_op jit(solution)/shard_map/ppermute | solution.py:508
  225.8 6.2 %collective-permute-done.14 = bf16[96,1152]{1,0:T(8,128)(2,1)S(1)} collective-permute-done((bf16[96,1152]{1,0:T(8,128)(2,1)S(1)}, bf16[96,1152]{1,0:T(8,128)(2,1)S(1)}, u32[]{:S(2)}, u32[]{:S(2)}) %collective-permute-start.14) | collective-permute-done | bytes 221216 | tf_op jit(solution)/shard_map/ppermute | solution.py:508
  (230 shorter events, 90.5 us)
Async XLA Ops:
  4.7 19.2 %collective-permute-start.3 = (bf16[128,1536]{1,0:T(8,128)(2,1)S(1)}, bf16[128,1536]{1,0:T(8,128)(2,1)S(1)}, u32[]{:S(2)}, u32[]{:S(2)}) collective-permute-start(bf16[128,1536]{1,0:T(8,128)(2,1)S(1)} %fusion.refs_1_), channel_id=1, source_target_pairs={{0,1},{1,0},{2,3},{3,2},{4,5},{5,4},{6,7},{7,6},{8,9},{9,8},{10,11... | collective-permute-start | bytes 1179656 | tf_op jit(solution)/shard_map/ppermute | solution.py:474
  62.4 18.8 %collective-permute-start.47 = (bf16[384,256]{1,0:T(8,128)(2,1)S(1)}, bf16[384,256]{1,0:T(8,128)(2,1)S(1)}, u32[]{:S(2)}, u32[]{:S(2)}) collective-permute-start(bf16[384,256]{1,0:T(8,128)(2,1)S(1)} %copy-done.50), channel_id=1, source_target_pairs={{0,4},{2,6},{4,0},{6,2},{8,12},{10,14},{12,8},{14,10},{16,20},{18,... | collective-permute-start | bytes 589832 | tf_op jit(solution)/shard_map/ppermute | solution.py:479
  63.0 19.0 %collective-permute-start.48 = (bf16[384,256]{1,0:T(8,128)(2,1)S(1)}, bf16[384,256]{1,0:T(8,128)(2,1)S(1)}, u32[]{:S(2)}, u32[]{:S(2)}) collective-permute-start(bf16[384,256]{1,0:T(8,128)(2,1)S(1)} %copy-done.47), channel_id=1, source_target_pairs={{0,6},{2,4},{4,2},{6,0},{8,14},{10,12},{12,10},{14,8},{16,22},{18,... | collective-permute-start | bytes 589832 | tf_op jit(solution)/shard_map/ppermute | solution.py:479
  81.2 28.4 %collective-permute-start.50 = (bf16[256,768]{1,0:T(8,128)(2,1)S(1)}, bf16[256,768]{1,0:T(8,128)(2,1)S(1)}, u32[]{:S(2)}, u32[]{:S(2)}) collective-permute-start(bf16[256,768]{1,0:T(8,128)(2,1)S(1)} %copy-done.16), channel_id=1, source_target_pairs={{0,4},{2,6},{4,0},{6,2},{8,12},{10,14},{12,8},{14,10},{16,20},{18,... | collective-permute-start | bytes 1179656 | tf_op jit(solution)/shard_map/ppermute | solution.py:479
  83.4 18.3 %collective-permute-start.17 = (bf16[384,256]{1,0:T(8,128)(2,1)}, bf16[384,256]{1,0:T(8,128)(2,1)S(1)}, u32[]{:S(2)}, u32[]{:S(2)}) collective-permute-start(bf16[384,256]{1,0:T(8,128)(2,1)} %get-tuple-element.49), channel_id=1, source_target_pairs={{0,4},{2,6},{4,0},{6,2},{8,12},{10,14},{12,8},{14,10},{16,20},{18,... | collective-permute-start | bytes 589832 | tf_op jit(solution)/shard_map/ppermute | solution.py:479
  84.2 20.1 %collective-permute-start.18 = (bf16[384,256]{1,0:T(8,128)(2,1)}, bf16[384,256]{1,0:T(8,128)(2,1)S(1)}, u32[]{:S(2)}, u32[]{:S(2)}) collective-permute-start(bf16[384,256]{1,0:T(8,128)(2,1)} %get-tuple-element.50), channel_id=1, source_target_pairs={{0,6},{2,4},{4,2},{6,0},{8,14},{10,12},{12,10},{14,8},{16,22},{18,... | collective-permute-start | bytes 589832 | tf_op jit(solution)/shard_map/ppermute | solution.py:479
  101.7 19.8 %collective-permute-start.35 = (bf16[256,768]{1,0:T(8,128)(2,1)S(1)}, bf16[256,768]{1,0:T(8,128)(2,1)S(1)}, u32[]{:S(2)}, u32[]{:S(2)}) collective-permute-start(bf16[256,768]{1,0:T(8,128)(2,1)S(1)} %copy-done.14), channel_id=1, source_target_pairs={{0,4},{2,6},{4,0},{6,2},{8,12},{10,14},{12,8},{14,10},{16,20},{18,... | collective-permute-start | bytes 1179656 | tf_op jit(solution)/shard_map/ppermute | solution.py:479
  111.3 25.0 %collective-permute-start.40 = (bf16[256,768]{1,0:T(8,128)(2,1)S(1)}, bf16[256,768]{1,0:T(8,128)(2,1)S(1)}, u32[]{:S(2)}, u32[]{:S(2)}) collective-permute-start(bf16[256,768]{1,0:T(8,128)(2,1)S(1)} %copy-done.15), channel_id=1, source_target_pairs={{0,2},{2,0},{4,6},{6,4},{8,10},{10,8},{12,14},{14,12},{16,18},{18,... | collective-permute-start | bytes 1179656 | tf_op jit(solution)/shard_map/ppermute | solution.py:479
  136.2 25.1 %collective-permute-start.6 = (bf16[384,256]{1,0:T(8,128)(2,1)S(1)}, bf16[384,256]{1,0:T(8,128)(2,1)S(1)}, u32[]{:S(2)}, u32[]{:S(2)}) collective-permute-start(bf16[384,256]{1,0:T(8,128)(2,1)S(1)} %copy-done.40), channel_id=1, source_target_pairs={{0,4},{2,6},{4,0},{6,2},{8,12},{10,14},{12,8},{14,10},{16,20},{18,... | collective-permute-start | bytes 589832 | tf_op jit(solution)/shard_map/ppermute | solution.py:479
  137.2 24.8 %collective-permute-start.7 = (bf16[384,256]{1,0:T(8,128)(2,1)S(1)}, bf16[384,256]{1,0:T(8,128)(2,1)S(1)}, u32[]{:S(2)}, u32[]{:S(2)}) collective-permute-start(bf16[384,256]{1,0:T(8,128)(2,1)S(1)} %copy-done.39), channel_id=1, source_target_pairs={{0,6},{2,4},{4,2},{6,0},{8,14},{10,12},{12,10},{14,8},{16,22},{18,... | collective-permute-start | bytes 589832 | tf_op jit(solution)/shard_map/ppermute | solution.py:479
  141.4 20.6 %collective-permute-start.29 = (bf16[256,768]{1,0:T(8,128)(2,1)S(1)}, bf16[256,768]{1,0:T(8,128)(2,1)S(1)}, u32[]{:S(2)}, u32[]{:S(2)}) collective-permute-start(bf16[256,768]{1,0:T(8,128)(2,1)S(1)} %copy-done.13), channel_id=1, source_target_pairs={{0,4},{2,6},{4,0},{6,2},{8,12},{10,14},{12,8},{14,10},{16,20},{18,... | collective-permute-start | bytes 1179656 | tf_op jit(solution)/shard_map/ppermute | solution.py:479
  142.5 17.7 %collective-permute-start.11 = (bf16[256,384]{1,0:T(8,128)(2,1)S(1)}, bf16[256,384]{1,0:T(8,128)(2,1)S(1)}, u32[]{:S(2)}, u32[]{:S(2)}) collective-permute-start(bf16[256,384]{1,0:T(8,128)(2,1)S(1)} %copy-done.42), channel_id=1, source_target_pairs={{0,4},{2,6},{4,0},{6,2},{8,12},{10,14},{12,8},{14,10},{16,20},{18,... | collective-permute-start | bytes 589832 | tf_op jit(solution)/shard_map/ppermute | solution.py:479
  163.9 17.3 %collective-permute-start.53 = (bf16[96,768]{1,0:T(8,128)(2,1)S(1)}, bf16[96,768]{1,0:T(8,128)(2,1)S(1)}, u32[]{:S(2)}, u32[]{:S(2)}) collective-permute-start(bf16[96,768]{1,0:T(8,128)(2,1)S(1)} %get-tuple-element.79), channel_id=1, source_target_pairs={{0,16},{2,18},{4,20},{6,22},{8,24},{10,26},{12,28},{14,30},{16,0},... | collective-permute-start | bytes 442376 | tf_op jit(solution)/shard_map/ppermute | solution.py:508
  173.6 22.0 %collective-permute-start.44 = (bf16[96,768]{1,0:T(8,128)(2,1)S(1)}, bf16[96,768]{1,0:T(8,128)(2,1)S(1)}, u32[]{:S(2)}, u32[]{:S(2)}) collective-permute-start(bf16[96,768]{1,0:T(8,128)(2,1)S(1)} %get-tuple-element.82), channel_id=1, source_target_pairs={{0,16},{2,18},{4,20},{6,22},{8,24},{10,26},{12,28},{14,30},{16,0},... | collective-permute-start | bytes 442376 | tf_op jit(solution)/shard_map/ppermute | solution.py:508
  178.7 17.9 %collective-permute-start.45 = (bf16[96,768]{1,0:T(8,128)(2,1)S(1)}, bf16[96,768]{1,0:T(8,128)(2,1)S(1)}, u32[]{:S(2)}, u32[]{:S(2)}) collective-permute-start(bf16[96,768]{1,0:T(8,128)(2,1)S(1)} %get-tuple-element.81), channel_id=1, source_target_pairs={{0,24},{2,26},{4,28},{6,30},{8,0},{10,2},{12,4},{14,6},{16,8},{18,... | collective-permute-start | bytes 442376 | tf_op jit(solution)/shard_map/ppermute | solution.py:508
  181.2 19.6 %collective-permute-start.37 = (bf16[96,768]{1,0:T(8,128)(2,1)S(1)}, bf16[96,768]{1,0:T(8,128)(2,1)S(1)}, u32[]{:S(2)}, u32[]{:S(2)}) collective-permute-start(bf16[96,768]{1,0:T(8,128)(2,1)S(1)} %get-tuple-element.83), channel_id=1, source_target_pairs={{0,8},{2,10},{4,12},{6,14},{8,16},{10,18},{12,20},{14,22},{16,24},... | collective-permute-start | bytes 442376 | tf_op jit(solution)/shard_map/ppermute | solution.py:508
  181.2 27.1 %collective-permute-start.38 = (bf16[96,768]{1,0:T(8,128)(2,1)S(1)}, bf16[96,768]{1,0:T(8,128)(2,1)S(1)}, u32[]{:S(2)}, u32[]{:S(2)}) collective-permute-start(bf16[96,768]{1,0:T(8,128)(2,1)S(1)} %get-tuple-element.85), channel_id=1, source_target_pairs={{0,16},{2,18},{4,20},{6,22},{8,24},{10,26},{12,28},{14,30},{16,0},... | collective-permute-start | bytes 442376 | tf_op jit(solution)/shard_map/ppermute | solution.py:508
  187.2 22.1 %collective-permute-start.39 = (bf16[96,768]{1,0:T(8,128)(2,1)S(1)}, bf16[96,768]{1,0:T(8,128)(2,1)S(1)}, u32[]{:S(2)}, u32[]{:S(2)}) collective-permute-start(bf16[96,768]{1,0:T(8,128)(2,1)S(1)} %get-tuple-element.84), channel_id=1, source_target_pairs={{0,24},{2,26},{4,28},{6,30},{8,0},{10,2},{12,4},{14,6},{16,8},{18,... | collective-permute-start | bytes 442376 | tf_op jit(solution)/shard_map/ppermute | solution.py:508
  195.7 18.8 %collective-permute-start.31 = (bf16[96,768]{1,0:T(8,128)(2,1)S(1)}, bf16[96,768]{1,0:T(8,128)(2,1)S(1)}, u32[]{:S(2)}, u32[]{:S(2)}) collective-permute-start(bf16[96,768]{1,0:T(8,128)(2,1)S(1)} %get-tuple-element.86), channel_id=1, source_target_pairs={{0,8},{2,10},{4,12},{6,14},{8,16},{10,18},{12,20},{14,22},{16,24},... | collective-permute-start | bytes 442376 | tf_op jit(solution)/shard_map/ppermute | solution.py:508
  196.7 27.4 %collective-permute-start.32 = (bf16[96,768]{1,0:T(8,128)(2,1)S(1)}, bf16[96,768]{1,0:T(8,128)(2,1)S(1)}, u32[]{:S(2)}, u32[]{:S(2)}) collective-permute-start(bf16[96,768]{1,0:T(8,128)(2,1)S(1)} %get-tuple-element.88), channel_id=1, source_target_pairs={{0,16},{2,18},{4,20},{6,22},{8,24},{10,26},{12,28},{14,30},{16,0},... | collective-permute-start | bytes 442376 | tf_op jit(solution)/shard_map/ppermute | solution.py:508
  200.8 23.3 %collective-permute-start.33 = (bf16[96,768]{1,0:T(8,128)(2,1)S(1)}, bf16[96,768]{1,0:T(8,128)(2,1)S(1)}, u32[]{:S(2)}, u32[]{:S(2)}) collective-permute-start(bf16[96,768]{1,0:T(8,128)(2,1)S(1)} %get-tuple-element.87), channel_id=1, source_target_pairs={{0,24},{2,26},{4,28},{6,30},{8,0},{10,2},{12,4},{14,6},{16,8},{18,... | collective-permute-start | bytes 442376 | tf_op jit(solution)/shard_map/ppermute | solution.py:508
  208.3 17.5 %collective-permute-start.13 = (bf16[96,1152]{1,0:T(8,128)(2,1)S(1)}, bf16[96,1152]{1,0:T(8,128)(2,1)S(1)}, u32[]{:S(2)}, u32[]{:S(2)}) collective-permute-start(bf16[96,1152]{1,0:T(8,128)(2,1)S(1)} %get-tuple-element.70), channel_id=1, source_target_pairs={{0,8},{2,10},{4,12},{6,14},{8,16},{10,18},{12,20},{14,22},{16,24},... | collective-permute-start | bytes 663560 | tf_op jit(solution)/shard_map/ppermute | solution.py:508
  209.3 22.7 %collective-permute-start.14 = (bf16[96,1152]{1,0:T(8,128)(2,1)S(1)}, bf16[96,1152]{1,0:T(8,128)(2,1)S(1)}, u32[]{:S(2)}, u32[]{:S(2)}) collective-permute-start(bf16[96,1152]{1,0:T(8,128)(2,1)S(1)} %get-tuple-element.72), channel_id=1, source_target_pairs={{0,16},{2,18},{4,20},{6,22},{8,24},{10,26},{12,28},{14,30},{16,0},... | collective-permute-start | bytes 663560 | tf_op jit(solution)/shard_map/ppermute | solution.py:508
  214.4 17.6 %collective-permute-start.15 = (bf16[96,1152]{1,0:T(8,128)(2,1)S(1)}, bf16[96,1152]{1,0:T(8,128)(2,1)S(1)}, u32[]{:S(2)}, u32[]{:S(2)}) collective-permute-start(bf16[96,1152]{1,0:T(8,128)(2,1)S(1)} %get-tuple-element.71), channel_id=1, source_target_pairs={{0,24},{2,26},{4,28},{6,30},{8,0},{10,2},{12,4},{14,6},{16,8},{18,... | collective-permute-start | bytes 663560 | tf_op jit(solution)/shard_map/ppermute | solution.py:508
  (86 other events, 1131.7 us)

commit v2 on v1

v2 whole, which is shorter than its diff:
```python
import functools
import math

import jax
import jax.numpy as jnp
from jax import lax
from jax.experimental import pallas as pl
from jax.experimental.pallas import tpu as pltpu
from jax.sharding import PartitionSpec as P

HSIZE = 192
DILATION_STEP = 16
EPSILON = 1e-06
SOFT_CAP = 6.0
GELU_C = math.sqrt(2.0 / math.pi)
GELU_A = 0.044715
BF = jnp.bfloat16
F32 = jnp.float32
VMEM_BYTES = 56 * 1024 * 1024
NO_COST = pl.CostEstimate(flops=0, bytes_accessed=0, transcendentals=0)


def gelu(x):
    return 0.5 * x * (1.0 + jnp.tanh(GELU_C * (x + GELU_A * (x * x * x))))


def gelu_slope(x):
    t = jnp.tanh(GELU_C * (x + GELU_A * (x * x * x)))
    return 0.5 * (1.0 + t) + 0.5 * x * (1.0 - t * t) * GELU_C * (1.0 + 3.0 * GELU_A * x * x)


def dot_nn(a, b):
    return lax.dot_general(a, b, (((1,), (0,)), ((), ())), preferred_element_type=F32)


def dot_nt(a, b):
    return lax.dot_general(a, b, (((1,), (1,)), ((), ())), preferred_element_type=F32)


def dot_tn(a, b):
    return lax.dot_general(a, b, (((0,), (0,)), ((), ())), preferred_element_type=F32)


def rms_scale(x):
    return lax.rsqrt(jnp.mean(x * x, axis=-1, keepdims=True) + EPSILON)


def row_chunk(rows):
    return 128 if rows % 128 == 0 else rows


def loop_chunks(count, body):
    if count <= 2:
        for i in range(count):
            body(i)
    else:

        def step(i, carry):
            body(i)
            return carry

        lax.fori_loop(0, count, step, 0)


def rows_at(i, size):
    if isinstance(i, int):
        return pl.ds(i * size, size)
    return pl.ds(pl.multiple_of(i * size, size), size)


def emit_rows(starts, wide, outs, rows):
    parts = starts.shape[0] // len(outs)
    size = rows // parts
    for p, out in enumerate(outs):
        for k in range(parts):
            at = pl.multiple_of(starts[p * parts + k], 16)
            out[k * size : (k + 1) * size, :] = wide[pl.ds(at, size), :]


def shifted_sum(first, middle, last, offset):
    length = middle.shape[0]
    step = DILATION_STEP
    pos = lax.rem(lax.broadcasted_iota(jnp.int32, (length, 1), 0) + offset, length)
    down = jnp.concatenate([first[length - step :], first[: length - step]], axis=0)
    up = jnp.concatenate([last[step:], last[:step]], axis=0)
    return jnp.where(pos >= step, down, 0.0) + middle + jnp.where(pos < length - step, up, 0.0)


def call(kernel, out_shape, operands, smem=1, scratch=()):
    specs = [pl.BlockSpec(memory_space=pltpu.SMEM)] * smem
    specs += [pl.BlockSpec(memory_space=pltpu.VMEM)] * (len(operands) - smem)
    return pl.pallas_call(
        kernel,
        out_shape=out_shape,
        in_specs=specs,
        out_specs=[pl.BlockSpec(memory_space=pltpu.VMEM)] * len(out_shape),
        scratch_shapes=list(scratch),
        compiler_params=pltpu.CompilerParams(vmem_limit_bytes=VMEM_BYTES),
        cost_estimate=NO_COST,
    )(*operands)


def shape_of(rows, cols, dtype=BF):
    return jax.ShapeDtypeStruct((rows, cols), dtype)


def piece_rows(j, rows, i, size):
    if isinstance(i, int):
        return pl.ds(j * rows + i * size, size)
    return pl.ds(pl.multiple_of(j * rows + i * size, size), size)


def conv_block(starts, offset, pieces, taps, point, ring_rows, group):
    count = len(pieces)
    rows = pieces[0].shape[0]
    length, channels = rows * count, pieces[0].shape[1]
    inner = point.shape[0]

    def kernel(*refs):
        starts_ref, offset_ref = refs[:2]
        ins = refs[2 : 2 + count]
        taps_ref, point_ref = refs[2 + count : 4 + count]
        pre_ref = refs[4 + count]
        parts = refs[5 + count : 5 + 2 * count]
        sent = refs[5 + 2 * count : 5 + 2 * count + group]
        act, wide, prod, mid = refs[5 + 2 * count + group :]
        size = row_chunk(rows)
        for j in range(count):

            def body(i, j=j):
                x = ins[j][rows_at(i, size), :].astype(F32)
                a = gelu(x * rms_scale(x)).astype(BF)
                here = piece_rows(j, rows, i, size)
                act[here, :] = a
                wide[:, here] = a.T

            loop_chunks(rows // size, body)
        big = min(256, length)

        def product(i):
            here = rows_at(i, big)
            prod[here, :] = dot_nt(act[here, :], taps_ref[...])

        loop_chunks(length // big, product)
        pre = shifted_sum(
            prod[:, :inner], prod[:, inner : 2 * inner], prod[:, 2 * inner :], offset_ref[0]
        )
        pre_ref[...] = pre
        middle = gelu(pre).astype(BF)
        mid[...] = middle
        for j in range(count):

            def back(i, j=j):
                here = piece_rows(j, rows, i, size)
                parts[j][rows_at(i, size), :] = dot_nn(mid[here, :], point_ref[...]).astype(BF)

            loop_chunks(rows // size, back)
        emit_rows(starts_ref, wide, sent, ring_rows)
        for out in sent:
            out[ring_rows:, :] = middle.T

    outs = [shape_of(length, inner, F32)] + [shape_of(rows, channels)] * count
    outs += [shape_of(ring_rows + inner, length)] * group
    scratch = [
        pltpu.VMEM((length, channels), BF),
        pltpu.VMEM((channels, length), BF),
        pltpu.VMEM((length, 3 * inner), F32),
        pltpu.VMEM((length, inner), BF),
    ]
    res = call(kernel, outs, [starts, offset, *pieces, taps, point], 2, scratch)
    return res[0], res[1 : 1 + count], res[1 + count :]


def norm_block(near, cross, pieces, parts, moved, ring_rows, group):
    count = len(pieces)
    rows, channels = pieces[0].shape
    length = rows * count

    def kernel(*refs):
        near_ref, cross_ref = refs[:2]
        ins = refs[2 : 2 + count]
        firsts = refs[2 + count : 2 + 2 * count]
        adds = refs[2 + 2 * count : 2 + 2 * count + len(moved)]
        rest = refs[2 + 2 * count + len(moved) :]
        res_ref, norm_ref = rest[:2]
        sent = rest[2 : 2 + 2 * group]
        wide = rest[2 + 2 * group]
        size = row_chunk(rows)
        for j in range(count):

            def body(i, j=j):
                here = piece_rows(j, rows, i, size)
                total = firsts[j][rows_at(i, size), :].astype(F32)
                if adds:
                    total = total + adds[j][rows_at(i, size), :].astype(F32)
                res = (ins[j][rows_at(i, size), :].astype(F32) + total).astype(BF)
                res_ref[here, :] = res
                res = res.astype(F32)
                a = (res * rms_scale(res)).astype(BF)
                norm_ref[here, :] = a
                wide[:, here] = a.T

            loop_chunks(rows // size, body)
        emit_rows(near_ref, wide, sent[:group], ring_rows)
        emit_rows(cross_ref, wide, sent[group:], ring_rows)

    outs = [shape_of(length, channels), shape_of(length, channels)]
    outs += [shape_of(ring_rows, length)] * (2 * group)
    scratch = [pltpu.VMEM((channels, length), BF)]
    res = call(kernel, outs, [near, cross, *pieces, *parts, *moved], 2, scratch)
    return res[0], res[1], res[2 : 2 + group], res[2 + group :]


def widen_block(starts, pieces, ring_rows, group):
    count = len(pieces)
    rows, channels = pieces[0].shape
    length = rows * count

    def kernel(*refs):
        starts_ref = refs[0]
        ins = refs[1 : 1 + count]
        whole_ref = refs[1 + count]
        sent = refs[2 + count : 2 + count + group]
        wide = refs[2 + count + group]
        size = row_chunk(rows)
        for j in range(count):

            def body(i, j=j):
                here = piece_rows(j, rows, i, size)
                a = ins[j][rows_at(i, size), :]
                whole_ref[here, :] = a
                wide[:, here] = a.T

            loop_chunks(rows // size, body)
        emit_rows(starts_ref, wide, sent, ring_rows)

    outs = [shape_of(length, channels)] + [shape_of(ring_rows, length)] * group
    scratch = [pltpu.VMEM((channels, length), BF)]
    res = call(kernel, outs, [starts, *pieces], 1, scratch)
    return res[0], res[1:]


def attention_block(normed, grad_y, query_w, key_w, value_w, out_w, count):
    length, channels = normed.shape
    rows = length // count
    features = query_w.shape[0]
    heads = features // HSIZE
    per_step = 2 if heads % 2 == 0 else 1
    width = per_step * HSIZE
    inv_root = 1.0 / math.sqrt(HSIZE)
    chunk = min(256, length)

    def kernel(n_ref, gy_ref, wq, wk, wv, wo, qk_ref, va_ref, *rest):
        dns, acc = rest[:count], rest[count]
        step = pl.program_id(0)
        n = n_ref[...]
        gy = gy_ref[...]
        dqs, dks, dvs, ats = [], [], [], []
        for h in range(per_step):
            head = pl.ds(h * HSIZE, HSIZE)
            q = dot_nt(n, wq[head, :]).astype(BF)
            k = dot_nt(n, wk[head, :]).astype(BF)
            v = dot_nt(n, wv[head, :]).astype(BF)
            g = dot_nt(gy, wo[head, :]).astype(BF)
            dq, at = [], []
            dk = dv = None
            for c in range(length // chunk):
                qc = q[c * chunk : (c + 1) * chunk]
                gc = g[c * chunk : (c + 1) * chunk]
                ratio = jnp.tanh(dot_nt(qc, k) * (inv_root / SOFT_CAP))
                unnormed = jnp.exp(SOFT_CAP * ratio)
                soft = unnormed / jnp.sum(unnormed, axis=-1, keepdims=True)
                low = soft.astype(BF)
                at.append(dot_nn(low, v))
                gs = dot_nt(gc, v)
                gs = soft * (gs - jnp.sum(soft * gs, axis=-1, keepdims=True))
                gs = (gs * (1.0 - ratio * ratio)).astype(BF)
                dq.append(dot_nn(gs, k) * inv_root)
                dk_c = dot_tn(gs, qc)
                dv_c = dot_tn(low, gc)
                dk = dk_c if dk is None else dk + dk_c
                dv = dv_c if dv is None else dv + dv_c
            join = (lambda parts: parts[0] if len(parts) == 1 else jnp.concatenate(parts, axis=0))
            dqs.append(join(dq))
            ats.append(join(at))
            dks.append(dk * inv_root)
            dvs.append(dv)
        side = (lambda parts: parts[0] if len(parts) == 1 else jnp.concatenate(parts, axis=1))
        dq, dk, dv, at = [side(t).astype(BF) for t in (dqs, dks, dvs, ats)]
        qk_ref[0] = dq
        qk_ref[1] = dk
        va_ref[0] = dv
        va_ref[1] = at
        total = dot_nn(dq, wq[...]) + dot_nn(dk, wk[...]) + dot_nn(dv, wv[...])

        @pl.when(step == 0)
        def _():
            acc[...] = total

        @pl.when(step > 0)
        def _():
            acc[...] += total

        @pl.when(step == pl.num_programs(0) - 1)
        def _():
            for j in range(count):
                dns[j][...] = acc[pl.ds(j * rows, rows), :].astype(BF)

    whole = pl.BlockSpec((length, channels), lambda i: (0, 0))
    weight = pl.BlockSpec((width, channels), lambda i: (i, 0))
    column = pl.BlockSpec((2, length, width), lambda i: (0, 0, i))
    piece = pl.BlockSpec((rows, channels), lambda i: (0, 0))
    return pl.pallas_call(
        kernel,
        grid=(heads // per_step,),
        out_shape=[jax.ShapeDtypeStruct((2, length, features), BF)] * 2
        + [shape_of(rows, channels)] * count,
        in_specs=[whole, whole, weight, weight, weight, weight],
        out_specs=[column] * 2 + [piece] * count,
        scratch_shapes=[pltpu.VMEM((length, channels), F32)],
        compiler_params=pltpu.CompilerParams(vmem_limit_bytes=VMEM_BYTES),
        cost_estimate=NO_COST,
    )(normed, grad_y, query_w, key_w, value_w, out_w)


def back_block(starts, residual, grad_y, parts, moved, pre, point, ring_rows, group):
    length, channels = residual.shape
    inner = point.shape[0]
    count = len(parts)
    rows = length // count

    def kernel(*refs):
        starts_ref, res_ref, gy_ref = refs[:3]
        firsts = refs[3 : 3 + count]
        adds = refs[3 + count : 3 + count + len(moved)]
        pre_ref, point_ref = refs[3 + count + len(moved) : 5 + count + len(moved)]
        rest = refs[5 + count + len(moved) :]
        gc_ref = rest[0]
        sent = rest[1 : 1 + group]
        wide, resid_grad = rest[1 + group :]
        size = row_chunk(rows)
        for j in range(count):

            def body(i, j=j):
                here = piece_rows(j, rows, i, size)
                gn = firsts[j][rows_at(i, size), :].astype(F32)
                if adds:
                    gn = gn + adds[j][rows_at(i, size), :].astype(F32)
                res = res_ref[here, :].astype(F32)
                scale = rms_scale(res)
                inner_mean = jnp.mean(gn * res, axis=-1, keepdims=True)
                a = gy_ref[here, :].astype(F32) + (
                    scale * gn - res * (scale * scale * scale) * inner_mean
                )
                a = a.astype(BF)
                resid_grad[here, :] = a
                wide[:, here] = a.T

            loop_chunks(rows // size, body)
        big = min(256, length)

        def product(i):
            here = rows_at(i, big)
            gm = dot_nt(resid_grad[here, :], point_ref[...])
            gc_ref[here, :] = (gelu_slope(pre_ref[here, :]) * gm).astype(BF)

        loop_chunks(length // big, product)
        emit_rows(starts_ref, wide, sent, ring_rows)

    outs = [shape_of(length, inner)] + [shape_of(ring_rows, length)] * group
    scratch = [pltpu.VMEM((channels, length), BF), pltpu.VMEM((length, channels), BF)]
    res = call(
        kernel,
        outs,
        [starts, residual, grad_y, *parts, *moved, pre, point],
        1,
        scratch,
    )
    return res[0], res[1:]


def store_halves(outs, total, side, cols):
    half = total.shape[0] // len(outs)
    for k, out in enumerate(outs):
        part = total[k * half : (k + 1) * half]
        out[:, side * cols : (side + 1) * cols] = part


def pair_sum(first_wides, second_wides, narrows, halves):
    group = len(first_wides)
    rows, length = first_wides[0].shape
    cols = narrows[0].shape[2]
    same = first_wides is second_wides
    wides = first_wides if same else first_wides + second_wides

    def kernel(*refs):
        a_refs, b_refs = refs[: len(wides)], refs[len(wides) : len(wides) + group]
        outs = refs[len(wides) + group :]
        for side in range(2):
            total = None
            for p in range(group):
                a = a_refs[p if same else side * group + p][...]
                term = dot_nn(a, b_refs[p][side])
                total = term if total is None else total + term
            store_halves(outs, total.astype(BF), side, cols)

    return call(kernel, [shape_of(rows // halves, 2 * cols)] * halves, [*wides, *narrows], 0)


def tap_sum(offset, packs, conv_narrows, halves, rows):
    group = len(packs)
    length, inner = conv_narrows[0].shape
    step = DILATION_STEP

    def kernel(offset_ref, *refs):
        pack_refs, conv_refs = refs[:group], refs[group : 2 * group]
        outs = refs[2 * group :]
        pos = lax.rem(lax.broadcasted_iota(jnp.int32, (length, 1), 0) + offset_ref[0], length)
        total = [None] * 3
        for p in range(group):
            a = pack_refs[p][:rows, :]
            b = conv_refs[p][...]
            up = jnp.concatenate([b[step:], b[:step]], axis=0).astype(F32)
            down = jnp.concatenate([b[length - step :], b[: length - step]], axis=0).astype(F32)
            first = jnp.where(pos < length - step, up, 0.0).astype(BF)
            last = jnp.where(pos >= step, down, 0.0).astype(BF)
            terms = [dot_nn(a, moved) for moved in (first, b, last)]
            total = [t if old is None else old + t for old, t in zip(total, terms)]
        for side in range(3):
            store_halves(outs, total[side].astype(BF), side, inner)

    outs = [shape_of(rows // halves, 3 * inner)] * halves
    return call(kernel, outs, [offset, *packs, *conv_narrows], 1)


def point_sum(packs, resid_wides, halves):
    group = len(packs)
    rows = resid_wides[0].shape[0]
    inner = packs[0].shape[0] - rows

    def kernel(*refs):
        pack_refs, wide_refs = refs[:group], refs[group : 2 * group]
        total = None
        for p in range(group):
            term = dot_nt(wide_refs[p][...], pack_refs[p][rows:, :])
            total = term if total is None else total + term
        store_halves(refs[2 * group :], total.astype(BF), 0, inner)

    outs = [shape_of(rows // halves, inner)] * halves
    return call(kernel, outs, [*packs, *resid_wides], 0)


def after(value, *others):
    return lax.optimization_barrier((value, others))[0]


def shards(
    inputs,
    dilated_tap_weight,
    point_weight,
    query_weight,
    key_weight,
    value_weight,
    out_weight,
    cotangent,
):
    channels = inputs.shape[2]
    own = inputs[0]
    rows = own.shape[0]
    n_seq = lax.axis_size("seq")
    n_dp = lax.axis_size("dp")
    length = rows * n_seq
    pair = n_seq == 2
    block = channels // n_dp
    inner = point_weight.shape[0]
    features = query_weight.shape[0]
    inv_tokens = 1.0 / math.sqrt(inputs.shape[0] * n_dp * length)

    bits = [1 << i for i in range(n_dp.bit_length() - 1)]
    near_bits, near_rest = bits[:2], bits[2:]
    if len(bits) > 2:
        cross_bits, cross_rest = [bits[0], bits[2]], [bits[1], *bits[3:]]
    else:
        cross_bits, cross_rest = near_bits, near_rest
    group = 1 << len(near_bits)
    ring_rows = channels // group
    halves = 2 if near_rest else 1

    me_dp = lax.axis_index("dp")
    me_seq = lax.axis_index("seq")

    def combos(of):
        found = [0]
        for bit in of:
            found += [value | bit for value in found]
        return found

    def starts_of(peers, rest):
        order = combos(rest[::-1])
        places = [peer ^ k for peer in combos(peers) for k in order]
        return ((me_dp ^ jnp.array(places, jnp.int32)) * block).astype(jnp.int32)

    near = starts_of(near_bits, near_rest)
    cross = starts_of(cross_bits, cross_rest)
    offset = (me_seq * rows if pair else jnp.int32(0)).astype(jnp.int32).reshape(1)

    def swap_seq(x):
        return lax.ppermute(x, "seq", [(0, 1), (1, 0)])

    def to_peer(x, bit):
        if bit == 0:
            return x
        return lax.ppermute(x, "dp", [(i, i ^ bit) for i in range(n_dp)])

    def gather_seq(x):
        if pair:
            return [x, swap_seq(x)]
        return [lax.all_gather(x, "seq", axis=0, tiled=True)]

    def add_seq(parts):
        if pair:
            return parts, [swap_seq(parts[1]), swap_seq(parts[0])]
        summed = lax.psum_scatter(parts[0], "seq", scatter_dimension=0, tiled=True)
        return [lax.all_gather(summed, "seq", axis=0, tiled=True)], []

    def share_wide(pieces, peers):
        return [to_peer(piece, p) for piece, p in zip(pieces, combos(peers))]

    def send_narrow(x, peers):
        return [x] + [to_peer(x, bit) for bit in peers]

    def pass_narrow(got, peers):
        return got + [to_peer(got[2], peers[0])] if len(peers) == 2 else got

    def first_half(totals, rest):
        return to_peer(totals[1], rest[0]) if rest else None

    def add_half(totals, got):
        kept = totals[0].astype(F32)
        return kept if got is None else kept + got.astype(F32)

    def later_halves(kept, rest):
        for bit in rest[1:]:
            half = kept.shape[0] // 2
            got = to_peer(kept[half:].astype(BF), bit)
            kept = kept[:half] + got.astype(F32)
        return kept

    pieces = gather_seq(own)
    grad_own = (cotangent[0].astype(F32) * inv_tokens).astype(BF)
    taps = dilated_tap_weight.reshape(3 * inner, channels)
    pre, parts, packs = conv_block(near, offset, pieces, taps, point_weight, ring_rows, group)
    grad_pieces = gather_seq(grad_own)
    parts, moved = add_seq(parts)
    packs = share_wide(packs, near_bits)
    grad_y, grad_sent = widen_block(cross, grad_pieces, ring_rows, group)
    grad_cross = share_wide(grad_sent, cross_bits)
    moved = after(moved, packs)
    residual, normed, norm_near, norm_cross = norm_block(
        near, cross, pieces, parts, moved, ring_rows, group
    )
    norm_near = share_wide(norm_near, near_bits)
    norm_cross = share_wide(norm_cross, cross_bits)

    delta_qk, delta_va, *grad_parts = attention_block(
        normed, grad_y, query_weight, key_weight, value_weight, out_weight, len(pieces)
    )
    grad_parts, delta_qk, delta_va, norm_near, norm_cross, grad_cross = lax.optimization_barrier(
        (grad_parts, delta_qk, delta_va, norm_near, norm_cross, grad_cross)
    )
    grad_parts, grad_moved = add_seq(grad_parts)
    qk_all = send_narrow(delta_qk, near_bits)
    va_all = send_narrow(delta_va, cross_bits)
    attn_part = dot_nn(delta_va[1], out_weight).astype(BF)
    grad_moved = after(grad_moved, qk_all, va_all)
    grad_conv, resid_sent = back_block(
        near, residual, grad_y, grad_parts, grad_moved, pre, point_weight, ring_rows, group
    )
    conv_all = send_narrow(grad_conv, near_bits)
    qk_all = pass_narrow(after(qk_all, grad_conv), near_bits)
    va_all = pass_narrow(after(va_all, grad_conv), cross_bits)
    resid_near = share_wide(resid_sent, near_bits)
    attn_part = after(attn_part, grad_conv)
    if pair:
        attn_rows = attn_part[:rows].astype(F32) + swap_seq(attn_part[rows:]).astype(F32)
        res_own = residual[:rows]
    else:
        attn_rows = lax.psum_scatter(attn_part, "seq", scatter_dimension=0, tiled=True)
        attn_rows = attn_rows.astype(F32)
        res_own = lax.dynamic_slice_in_dim(residual, me_seq * rows, rows, 0)
    output = (res_own.astype(F32) + attn_rows).astype(BF)[None]

    qk_total = pair_sum(norm_near, norm_near, qk_all, halves)
    qk_got = first_half(qk_total, near_rest)
    conv_all = pass_narrow(after(conv_all, qk_total), near_bits)
    tap_total = tap_sum(offset, packs, conv_all, halves, ring_rows)
    tap_got = first_half(tap_total, near_rest)
    va_total = pair_sum(norm_cross, grad_cross, after(va_all, tap_total), halves)
    va_got = first_half(va_total, cross_rest)
    point_total = point_sum(packs, after(resid_near, va_total), halves)
    point_got = first_half(point_total, near_rest)

    qk_kept = add_half(qk_total, after(qk_got, point_total))
    tap_kept = add_half(tap_total, after(tap_got, qk_kept))
    va_kept = add_half(va_total, after(va_got, tap_kept))
    point_kept = add_half(point_total, after(point_got, va_kept))
    qk_done = later_halves(qk_kept, near_rest)
    tap_done = later_halves(tap_kept, near_rest)
    va_done = later_halves(va_kept, cross_rest)
    point_done = later_halves(point_kept, near_rest)
    return (
        output,
        tap_done.reshape(block, 3, inner).transpose(1, 0, 2),
        point_done.T,
        qk_done[:, :features],
        qk_done[:, features:],
        va_done[:, :features],
        va_done[:, features:].T,
    )


def solution(mesh):
    placed = (
        P("dp", "seq", None),
        P(None, "seq", None),
        P("seq", None),
        P("seq", None),
        P("seq", None),
        P("seq", None),
        P("seq", None),
        P("dp", "seq", None),
    )
    return jax.shard_map(
        shards,
        mesh=mesh,
        in_specs=placed,
        out_specs=(
            P("dp", "seq", None),
            P(None, "dp", "seq"),
            P("seq", "dp"),
            P("dp", "seq"),
            P("dp", "seq"),
            P("dp", "seq"),
            P("seq", "dp"),
        ),
        check_vma=False,
    )
```

time: 237 us -> 178 us (0.75)
  waiting for transfers between devices: 100 us -> 74.1 us
  starting transfers between devices: 58.5 us -> 39.4 us
  local copies, waits for them, and re-layouts: 12.6 us -> 7.89 us
  other arithmetic: 9.62 us -> 6.42 us
    ppermute x48 -> x32, waiting for transfers between devices: 72 us -> 50.2 us  [to_peer(): return lax.ppermute(x, 'dp', [(i, i ^ bit) for i in range(n_dp)])]
    ppermute x48 -> x32, starting transfers between devices: 49.5 us -> 29.3 us  [to_peer(): return lax.ppermute(x, 'dp', [(i, i ^ bit) for i in range(n_dp)])]
    slice x8 -> x5, local copies, waits for them, and re-layouts: 6.81 us -> 2.38 us  [the longest x4 1.53 us: later_halves(): got = to_peer(kept[half:].astype(BF), bit)]
    ppermute x7, waiting for transfers between devices: 28 us -> 23.9 us  [swap_seq(): return lax.ppermute(x, 'seq', [(0, 1), (1, 0)])]
    add x4 -> x7, other arithmetic: 5.22 us -> 2.51 us  [the longest x3 2.08 us: later_halves(): kept = kept[:half] + got.astype(F32)]
    pallas_call x10 -> x8, Pallas kernels: 36.2 us -> 34.1 us  [call(): pl.pallas_call(kernel, out_shape=out_shape, in_specs=specs, out_specs=[pl...]
    unnamed x111 -> x81, local copies, waits for them, and re-layouts: 5.02 us -> 4.46 us
  transfers between devices with their start and end apart: 55 -> 39, of which waited for: 19 -> 11; matrix products, arithmetic and copies ran while one was open for 7% -> 5% of each run, Pallas kernels for 14% -> 24%
where the time goes in v2:
time: 178 us; the launch traced here: 177 us
  waiting for transfers between devices  74.1 us (42%)
  Pallas kernels  47.6 us (27%)
  starting transfers between devices  39.4 us (22%)
  local copies, waits for them, and re-layouts  7.89 us (4%)
  other arithmetic  6.42 us (4%)
    ppermute x32, waiting for transfers between devices, to_peer(): return lax.ppermute(x, 'dp', [(i, i ^ bit) for i in range(n_dp)])  50.2 us
    pallas_call x8, Pallas kernels, call(): pl.pallas_call(kernel, out_shape=out_shape, in_specs=specs, out_specs=[pl...  34.1 us
    ppermute x32, starting transfers between devices, to_peer(): return lax.ppermute(x, 'dp', [(i, i ^ bit) for i in range(n_dp)])  29.3 us
    ppermute x7, waiting for transfers between devices, swap_seq(): return lax.ppermute(x, 'seq', [(0, 1), (1, 0)])  23.9 us
    pallas_call x1, Pallas kernels, attention_block(): pl.pallas_call(kernel, grid=(heads // per_step,), out_shape=[jax.ShapeDty...  13.5 us
    ppermute x7, starting transfers between devices, swap_seq(): return lax.ppermute(x, 'seq', [(0, 1), (1, 0)])  10.1 us
    unnamed x81, local copies, waits for them, and re-layouts  4.46 us
  transfers between devices with their start and end apart: 39, of which 11 were waited for; matrix products, arithmetic and copies ran while one was open for 5% of the time, Pallas kernels for 24%

profile of v2, /device:TPU:0, one launch (start us, length us, event | category | flops | bytes accessed | tf_op | source)
XLA Modules:
  0.0 177.3 jit_solution(15846801921152552474)
XLA Ops:
  0.6 3.0 %collective-permute-start = (bf16[128,1536]{1,0:T(8,128)(2,1)}, bf16[128,1536]{1,0:T(8,128)(2,1)S(1)}, u32[]{:S(2)}, u32[]{:S(2)}) collective-permute-start(bf16[128,1536]{1,0:T(8,128)(2,1)} %bitcast.18), channel_id=1, source_target_pairs={{0,1},{1,0},{2,3},{3,2},{4,5},{5,4},{6,7},{7,6},{8,9},{9,8},{10,11... | collective-permute-start | bytes 1179656 | tf_op jit(solution)/shard_map/ppermute | solution.py:508
  6.1 7.7 %collective-permute-done.refs_3_ = bf16[128,1536]{1,0:T(8,128)(2,1)S(1)} collective-permute-done((bf16[128,1536]{1,0:T(8,128)(2,1)}, bf16[128,1536]{1,0:T(8,128)(2,1)S(1)}, u32[]{:S(2)}, u32[]{:S(2)}) %collective-permute-start) | collective-permute-done | bytes 393248 | tf_op jit(solution)/shard_map/ppermute | solution.py:508
  14.6 6.7 %shard_map.153 = (f32[256,384]{1,0:T(8,128)}, bf16[128,1536]{1,0:T(8,128)(2,1)}, bf16[128,1536]{1,0:T(8,128)(2,1)}, bf16[768,256]{1,0:T(8,128)(2,1)}, bf16[768,2...) custom-call(s32[16]{0:T(128)} %get-tuple-element.181.refs_0_, s32[1]{0:T(128)} %bitcast.1.refs_1_.offset_ref, ...), custom_call_target="tpu_custom_call" | custom-call | tf_op jit(solution)/shard_map/pallas_call | solution.py:92
  21.3 2.1 %collective-permute-start.4 = (bf16[768,256]{1,0:T(8,128)(2,1)}, bf16[768,256]{1,0:T(8,128)(2,1)S(1)}, u32[]{:S(2)}, u32[]{:S(2)}) collective-permute-start(bf16[768,256]{1,0:T(8,128)(2,1)} %get-tuple-element.92), channel_id=1, source_target_pairs={{0,4},{2,6},{4,0},{6,2},{8,12},{10,14},{12,8},{14,10},{16,20},{18,... | collective-permute-start | bytes 1179656 | tf_op jit(solution)/shard_map/ppermute | solution.py:513
  26.0 2.5 %shard_map.155 = (bf16[256,1536]{1,0:T(8,128)(2,1)}, bf16[384,256]{1,0:T(8,128)(2,1)}, bf16[384,256]{1,0:T(8,128)(2,1)}, bf16[384,256]{1,0:T(8,128)(2,1)}, bf16[384,256]{1,0:T(8,128)(2,1)}) custom-call(s32[16]{0:T(128)} %get-tuple-element.180.refs_1_.refs_0_, bf16[128,1536]{1,0:T(8,128)(2,1)} %copy-done.5, bf16[128,1536]{1,0:T(8,128)(2,1)} %copy-done.19), custom_call_target="tpu_custom_call" | custom-call | tf_op jit(solution)/shard_map/pallas_call | solution.py:92
  28.6 5.0 %collective-permute-done.4.refs_2_ = bf16[768,256]{1,0:T(8,128)(2,1)S(1)} collective-permute-done((bf16[768,256]{1,0:T(8,128)(2,1)}, bf16[768,256]{1,0:T(8,128)(2,1)S(1)}, u32[]{:S(2)}, u32[]{:S(2)}) %collective-permute-start.4) | collective-permute-done | bytes 393248 | tf_op jit(solution)/shard_map/ppermute | solution.py:513
  33.6 2.0 %collective-permute-start.14 = (bf16[384,256]{1,0:T(8,128)(2,1)}, bf16[384,256]{1,0:T(8,128)(2,1)S(1)}, u32[]{:S(2)}, u32[]{:S(2)}) collective-permute-start(bf16[384,256]{1,0:T(8,128)(2,1)} %get-tuple-element.113), channel_id=1, source_target_pairs={{0,8},{2,10},{4,12},{6,14},{8,0},{10,2},{12,4},{14,6},{16,24},{18,... | collective-permute-start | bytes 589832 | tf_op jit(solution)/shard_map/ppermute | solution.py:513
  35.6 5.9 %collective-permute-done.5.refs_3_ = bf16[768,256]{1,0:T(8,128)(2,1)S(1)} collective-permute-done((bf16[768,256]{1,0:T(8,128)(2,1)}, bf16[768,256]{1,0:T(8,128)(2,1)S(1)}, u32[]{:S(2)}, u32[]{:S(2)}) %collective-permute-start.5) | collective-permute-done | bytes 393248 | tf_op jit(solution)/shard_map/ppermute | solution.py:513
  44.2 3.8 %shard_map.154 = (bf16[256,1536]{1,0:T(8,128)(2,1)}, bf16[256,1536]{1,0:T(8,128)(2,1)}, bf16[384,256]{1,0:T(8,128)(2,1)}, bf16[384,256]{1,0:T(8,128)(2,1)}, bf16...) custom-call(s32[16]{0:T(128)} %get-tuple-element.181.refs_0_, ...), custom_call_target="tpu_custom_call" | custom-call | tf_op jit(solution)/shard_map/pallas_call | solution.py:92
  48.2 1.9 %collective-permute-start.11 = (bf16[384,256]{1,0:T(8,128)(2,1)}, bf16[384,256]{1,0:T(8,128)(2,1)S(1)}, u32[]{:S(2)}, u32[]{:S(2)}) collective-permute-start(bf16[384,256]{1,0:T(8,128)(2,1)} %get-tuple-element.109), channel_id=1, source_target_pairs={{0,8},{2,10},{4,12},{6,14},{8,0},{10,2},{12,4},{14,6},{16,24},{18,... | collective-permute-start | bytes 589832 | tf_op jit(solution)/shard_map/ppermute | solution.py:513
  52.1 13.5 %shard_map.156 = (bf16[2,256,768]{2,1,0:T(8,128)(2,1)}, bf16[2,256,768]{2,1,0:T(8,128)(2,1)}, bf16[128,1536]{1,0:T(8,128)(2,1)}, bf16[128,1536]{1,0:T(8,128)(2,1)}) custom-call(bf16[256,1536]{1,0:T(8,128)(2,1)} %get-tuple-element.97.n_ref, bf16[256,1536]{1,0:T(8,128)(2,1)} %get-tuple-element.98.gy_ref.refs_2_, bf16[768,1536]{1,0:T(8,128)(2,1)} %wq.1, ...), custom_call_target="tpu_custom_call" | custom-call | tf_op jit(solution)/shard_map/pallas_call | solution.py:313
  70.7 6.7 %collective-permute-done.16.refs_5_ = bf16[128,1536]{1,0:T(8,128)(2,1)S(1)} collective-permute-done((bf16[128,1536]{1,0:T(8,128)(2,1)}, bf16[128,1536]{1,0:T(8,128)(2,1)S(1)}, u32[]{:S(2)}, u32[]{:S(2)}) %collective-permute-start.16) | collective-permute-done | bytes 393248 | tf_op jit(solution)/shard_map/ppermute | solution.py:508
  79.1 9.3 %collective-permute-done.17.refs_6_ = bf16[128,1536]{1,0:T(8,128)(2,1)S(1)} collective-permute-done((bf16[128,1536]{1,0:T(8,128)(2,1)}, bf16[128,1536]{1,0:T(8,128)(2,1)S(1)}, u32[]{:S(2)}, u32[]{:S(2)}) %collective-permute-start.17) | collective-permute-done | bytes 393248 | tf_op jit(solution)/shard_map/ppermute | solution.py:508
  89.3 4.8 %shard_map.157 = (bf16[256,384]{1,0:T(8,128)(2,1)}, bf16[384,256]{1,0:T(8,128)(2,1)}, bf16[384,256]{1,0:T(8,128)(2,1)}, bf16[384,256]{1,0:T(8,128)(2,1)}, bf16[384,256]{1,0:T(8,128)(2,1)}) custom-call(s32[16]{0:T(128)} %get-tuple-element.181.refs_0_, bf16[256,1536]{1,0:T(8,128)(2,1)} %get-tuple-element.96.refs_1_, ...), custom_call_target="tpu_custom_call" | custom-call | tf_op jit(solution)/shard_map/pallas_call | solution.py:92
  97.4 4.6 %shard_map.158 = (bf16[192,1536]{1,0:T(8,128)(2,1)}, bf16[192,1536]{1,0:T(8,128)(2,1)}) custom-call(bf16[384,256]{1,0:T(8,128)(2,1)} %get-tuple-element.124.refs_0_, bf16[384,256]{1,0:T(8,128)(2,1)} %copy-done.34, bf16[384,256]{1,0:T(8,128)(2,1)} %copy-done.35, bf16[384,256]{1,0:T(8,128)(2,1)} %copy-done.36, ...), custom_call_target="tpu_custom_call" | custom-call | tf_op jit(solution)/shard_map/pallas_call | solution.py:92
  107.5 3.9 %shard_map.159 = (bf16[192,1152]{1,0:T(8,128)(2,1)}, bf16[192,1152]{1,0:T(8,128)(2,1)}) custom-call(s32[1]{0:T(128)} %bitcast.1.refs_1_.offset_ref, bf16[768,256]{1,0:T(8,128)(2,1)} %get-tuple-element.90.refs_0_, bf16[768,256]{1,0:T(8,128)(2,1)} %copy-done.2, bf16[768,256]{1,0:T(8,128)(2,1)} %copy-done.3, bf16[768,256]{1,0:T(8,128)(2,1)} %copy-done.4, ...), custom_call_target="tpu_custom_call" | custom-call | tf_op jit(solution)/shard_map/pallas_call | solution.py:92
  113.0 4.9 %shard_map.160 = (bf16[192,1536]{1,0:T(8,128)(2,1)}, bf16[192,1536]{1,0:T(8,128)(2,1)}) custom-call(bf16[384,256]{1,0:T(8,128)(2,1)} %get-tuple-element.142.refs_0_, bf16[384,256]{1,0:T(8,128)(2,1)} %copy-done.25, bf16[384,256]{1,0:T(8,128)(2,1)} %copy-done.26, bf16[384,256]{1,0:T(8,128)(2,1)} %copy-done.27, bf16[384,256]{1,0:T(8,128)(2,1)} %get-tuple-element.146.refs_4_, ...), custom_call_target="tpu_custom_call" | custom-call | tf_op jit(solution)/shard_map/pallas_call | solution.py:92
  119.9 2.9 %shard_map.161 = (bf16[192,384]{1,0:T(8,128)(2,1)}, bf16[192,384]{1,0:T(8,128)(2,1)}) custom-call(bf16[768,256]{1,0:T(8,128)(2,1)} %get-tuple-element.90.refs_0_, bf16[768,256]{1,0:T(8,128)(2,1)} %copy-done.2, bf16[768,256]{1,0:T(8,128)(2,1)} %copy-done.3, bf16[768,256]{1,0:T(8,128)(2,1)} %copy-done.4, bf16[384,256]{1,0:T(8,128)(2,1)} %get-tuple-element.159.refs_4_, ...), custom_call_target="tpu_custom_call" | custom-call | tf_op jit(solution)/shard_map/pallas_call | solution.py:92
  124.5 6.4 %collective-permute-done.27 = bf16[192,1152]{1,0:T(8,128)(2,1)S(1)} collective-permute-done((bf16[192,1152]{1,0:T(8,128)(2,1)S(1)}, bf16[192,1152]{1,0:T(8,128)(2,1)S(1)}, u32[]{:S(2)}, u32[]{:S(2)}) %collective-permute-start.27) | collective-permute-done | bytes 442400 | tf_op jit(solution)/shard_map/ppermute | solution.py:513
  131.1 2.6 %collective-permute-done.35 = bf16[192,1536]{1,0:T(8,128)(2,1)S(1)} collective-permute-done((bf16[192,1536]{1,0:T(8,128)(2,1)}, bf16[192,1536]{1,0:T(8,128)(2,1)S(1)}, u32[]{:S(2)}, u32[]{:S(2)}) %collective-permute-start.35) | collective-permute-done | bytes 589856 | tf_op jit(solution)/shard_map/ppermute | solution.py:513
  133.9 2.7 %collective-permute-start.36 = (bf16[96,384]{1,0:T(8,128)(2,1)S(1)}, bf16[96,384]{1,0:T(8,128)(2,1)S(1)}, u32[]{:S(2)}, u32[]{:S(2)}) collective-permute-start(bf16[96,384]{1,0:T(8,128)(2,1)S(1)} %slice.100), channel_id=1, source_target_pairs={{0,16},{2,18},{4,20},{6,22},{8,24},{10,26},{12,28},{14,30},{16,0},... | collective-permute-start | bytes 221192 | tf_op jit(solution)/shard_map/ppermute | solution.py:513
  138.5 2.7 %collective-permute-start.33 = (bf16[96,1152]{1,0:T(8,128)(2,1)S(1)}, bf16[96,1152]{1,0:T(8,128)(2,1)S(1)}, u32[]{:S(2)}, u32[]{:S(2)}) collective-permute-start(bf16[96,1152]{1,0:T(8,128)(2,1)S(1)} %slice.99), channel_id=1, source_target_pairs={{0,16},{2,18},{4,20},{6,22},{8,24},{10,26},{12,28},{14,30},{16,0},... | collective-permute-start | bytes 663560 | tf_op jit(solution)/shard_map/ppermute | solution.py:513
  143.0 27.2 %collective-permute-done.33 = bf16[96,1152]{1,0:T(8,128)(2,1)S(1)} collective-permute-done((bf16[96,1152]{1,0:T(8,128)(2,1)S(1)}, bf16[96,1152]{1,0:T(8,128)(2,1)S(1)}, u32[]{:S(2)}, u32[]{:S(2)}) %collective-permute-start.33) | collective-permute-done | bytes 221216 | tf_op jit(solution)/shard_map/ppermute | solution.py:513
  173.0 2.3 %collective-permute-done.38 = bf16[96,1536]{1,0:T(8,128)(2,1)} collective-permute-done((bf16[96,1536]{1,0:T(8,128)(2,1)}, bf16[96,1536]{1,0:T(8,128)(2,1)}, u32[]{:S(2)}, u32[]{:S(2)}) %collective-permute-start.38) | collective-permute-done | bytes 294944 | tf_op jit(solution)/shard_map/ppermute | solution.py:513
  (164 shorter events, 41.2 us)
Async XLA Ops:
  4.7 20.5 %collective-permute-start.6 = (bf16[128,1536]{1,0:T(8,128)(2,1)S(1)}, bf16[128,1536]{1,0:T(8,128)(2,1)S(1)}, u32[]{:S(2)}, u32[]{:S(2)}) collective-permute-start(bf16[128,1536]{1,0:T(8,128)(2,1)S(1)} %fusion.refs_1_), channel_id=1, source_target_pairs={{0,1},{1,0},{2,3},{3,2},{4,5},{5,4},{6,7},{7,6},{8,9},{9,8},{10,11... | collective-permute-start | bytes 1179656 | tf_op jit(solution)/shard_map/ppermute | solution.py:508
  23.4 18.1 %collective-permute-start.5 = (bf16[768,256]{1,0:T(8,128)(2,1)}, bf16[768,256]{1,0:T(8,128)(2,1)S(1)}, u32[]{:S(2)}, u32[]{:S(2)}) collective-permute-start(bf16[768,256]{1,0:T(8,128)(2,1)} %get-tuple-element.93), channel_id=1, source_target_pairs={{0,6},{2,4},{4,2},{6,0},{8,14},{10,12},{12,10},{14,8},{16,22},{18,... | collective-permute-start | bytes 1179656 | tf_op jit(solution)/shard_map/ppermute | solution.py:513
  23.5 19.8 %collective-permute-start.1 = (bf16[128,1536]{1,0:T(8,128)(2,1)}, bf16[128,1536]{1,0:T(8,128)(2,1)S(1)}, u32[]{:S(2)}, u32[]{:S(2)}) collective-permute-start(bf16[128,1536]{1,0:T(8,128)(2,1)} %get-tuple-element.89.refs_5_), channel_id=1, source_target_pairs={{0,1},{1,0},{2,3},{3,2},{4,5},{5,4},{6,7},{7,6},{8,9},{9,8},{10,11... | collective-permute-start | bytes 1179656 | tf_op jit(solution)/shard_map/ppermute | solution.py:508
  25.2 18.3 %collective-permute-start.2 = (bf16[128,1536]{1,0:T(8,128)(2,1)}, bf16[128,1536]{1,0:T(8,128)(2,1)S(1)}, u32[]{:S(2)}, u32[]{:S(2)}) collective-permute-start(bf16[128,1536]{1,0:T(8,128)(2,1)} %get-tuple-element.88.refs_4_), channel_id=1, source_target_pairs={{0,1},{1,0},{2,3},{3,2},{4,5},{5,4},{6,7},{7,6},{8,9},{9,8},{10,11... | collective-permute-start | bytes 1179656 | tf_op jit(solution)/shard_map/ppermute | solution.py:508
  28.5 21.5 %collective-permute-start.13 = (bf16[384,256]{1,0:T(8,128)(2,1)}, bf16[384,256]{1,0:T(8,128)(2,1)S(1)}, u32[]{:S(2)}, u32[]{:S(2)}) collective-permute-start(bf16[384,256]{1,0:T(8,128)(2,1)} %get-tuple-element.112), channel_id=1, source_target_pairs={{0,2},{2,0},{4,6},{6,4},{8,10},{10,8},{12,14},{14,12},{16,18},{18,... | collective-permute-start | bytes 589832 | tf_op jit(solution)/shard_map/ppermute | solution.py:513
  33.6 16.6 %collective-permute-start.14 = (bf16[384,256]{1,0:T(8,128)(2,1)}, bf16[384,256]{1,0:T(8,128)(2,1)S(1)}, u32[]{:S(2)}, u32[]{:S(2)}) collective-permute-start(bf16[384,256]{1,0:T(8,128)(2,1)} %get-tuple-element.113), channel_id=1, source_target_pairs={{0,8},{2,10},{4,12},{6,14},{8,0},{10,2},{12,4},{14,6},{16,24},{18,... | collective-permute-start | bytes 589832 | tf_op jit(solution)/shard_map/ppermute | solution.py:513
  48.2 17.5 %collective-permute-start.11 = (bf16[384,256]{1,0:T(8,128)(2,1)}, bf16[384,256]{1,0:T(8,128)(2,1)S(1)}, u32[]{:S(2)}, u32[]{:S(2)}) collective-permute-start(bf16[384,256]{1,0:T(8,128)(2,1)} %get-tuple-element.109), channel_id=1, source_target_pairs={{0,8},{2,10},{4,12},{6,14},{8,0},{10,2},{12,4},{14,6},{16,24},{18,... | collective-permute-start | bytes 589832 | tf_op jit(solution)/shard_map/ppermute | solution.py:513
  50.0 15.6 %collective-permute-start.12 = (bf16[384,256]{1,0:T(8,128)(2,1)}, bf16[384,256]{1,0:T(8,128)(2,1)S(1)}, u32[]{:S(2)}, u32[]{:S(2)}) collective-permute-start(bf16[384,256]{1,0:T(8,128)(2,1)} %get-tuple-element.110), channel_id=1, source_target_pairs={{0,10},{2,8},{4,14},{6,12},{8,2},{10,0},{12,6},{14,4},{16,26},{18,... | collective-permute-start | bytes 589832 | tf_op jit(solution)/shard_map/ppermute | solution.py:513
  50.1 15.5 %collective-permute-start.7 = (bf16[384,256]{1,0:T(8,128)(2,1)}, bf16[384,256]{1,0:T(8,128)(2,1)S(1)}, u32[]{:S(2)}, u32[]{:S(2)}) collective-permute-start(bf16[384,256]{1,0:T(8,128)(2,1)} %get-tuple-element.104), channel_id=1, source_target_pairs={{0,2},{2,0},{4,6},{6,4},{8,10},{10,8},{12,14},{14,12},{16,18},{18,... | collective-permute-start | bytes 589832 | tf_op jit(solution)/shard_map/ppermute | solution.py:513
  50.4 15.3 %collective-permute-start.8 = (bf16[384,256]{1,0:T(8,128)(2,1)}, bf16[384,256]{1,0:T(8,128)(2,1)S(1)}, u32[]{:S(2)}, u32[]{:S(2)}) collective-permute-start(bf16[384,256]{1,0:T(8,128)(2,1)} %get-tuple-element.105), channel_id=1, source_target_pairs={{0,4},{2,6},{4,0},{6,2},{8,12},{10,14},{12,8},{14,10},{16,20},{18,... | collective-permute-start | bytes 589832 | tf_op jit(solution)/shard_map/ppermute | solution.py:513
  52.1 13.6 %collective-permute-start.9 = (bf16[384,256]{1,0:T(8,128)(2,1)}, bf16[384,256]{1,0:T(8,128)(2,1)S(1)}, u32[]{:S(2)}, u32[]{:S(2)}) collective-permute-start(bf16[384,256]{1,0:T(8,128)(2,1)} %get-tuple-element.106), channel_id=1, source_target_pairs={{0,6},{2,4},{4,2},{6,0},{8,14},{10,12},{12,10},{14,8},{16,22},{18,... | collective-permute-start | bytes 589832 | tf_op jit(solution)/shard_map/ppermute | solution.py:513
  67.3 21.1 %collective-permute-start.18 = (bf16[2,256,768]{2,1,0:T(8,128)(2,1)}, bf16[2,256,768]{2,1,0:T(8,128)(2,1)S(1)}, u32[]{:S(2)}, u32[]{:S(2)}) collective-permute-start(bf16[2,256,768]{2,1,0:T(8,128)(2,1)} %get-tuple-element.128.refs_4_), channel_id=1, source_target_pairs={{0,2},{2,0},{4,6},{6,4},{8,10},{10,8},{12,14},{14,12},{16,18},{18,... | collective-permute-start | bytes 2359304 | tf_op jit(solution)/shard_map/ppermute | solution.py:513
  67.6 20.8 %collective-permute-start.19 = (bf16[2,256,768]{2,1,0:T(8,128)(2,1)}, bf16[2,256,768]{2,1,0:T(8,128)(2,1)S(1)}, u32[]{:S(2)}, u32[]{:S(2)}) collective-permute-start(bf16[2,256,768]{2,1,0:T(8,128)(2,1)} %get-tuple-element.128.refs_4_), channel_id=1, source_target_pairs={{0,4},{2,6},{4,0},{6,2},{8,12},{10,14},{12,8},{14,10},{16,20},{18,... | collective-permute-start | bytes 2359304 | tf_op jit(solution)/shard_map/ppermute | solution.py:513
  69.1 19.4 %collective-permute-start.20 = (bf16[2,256,768]{2,1,0:T(8,128)(2,1)}, bf16[2,256,768]{2,1,0:T(8,128)(2,1)S(1)}, u32[]{:S(2)}, u32[]{:S(2)}) collective-permute-start(bf16[2,256,768]{2,1,0:T(8,128)(2,1)} %get-tuple-element.153.refs_8_), channel_id=1, source_target_pairs={{0,2},{2,0},{4,6},{6,4},{8,10},{10,8},{12,14},{14,12},{16,18},{18,... | collective-permute-start | bytes 2359304 | tf_op jit(solution)/shard_map/ppermute | solution.py:513
  69.1 20.2 %collective-permute-start.21 = (bf16[2,256,768]{2,1,0:T(8,128)(2,1)}, bf16[2,256,768]{2,1,0:T(8,128)(2,1)S(1)}, u32[]{:S(2)}, u32[]{:S(2)}) collective-permute-start(bf16[2,256,768]{2,1,0:T(8,128)(2,1)} %get-tuple-element.153.refs_8_), channel_id=1, source_target_pairs={{0,8},{2,10},{4,12},{6,14},{8,0},{10,2},{12,4},{14,6},{16,24},{18,... | collective-permute-start | bytes 2359304 | tf_op jit(solution)/shard_map/ppermute | solution.py:513
  94.3 17.1 %collective-permute-start.32 = (bf16[2,256,768]{2,1,0:T(8,128)(2,1)S(1)}, bf16[2,256,768]{2,1,0:T(8,128)(2,1)S(1)}, u32[]{:S(2)}, u32[]{:S(2)}) collective-permute-start(bf16[2,256,768]{2,1,0:T(8,128)(2,1)S(1)} %collective-permute-done.21.refs_10_), channel_id=1, source_target_pairs={{0,2},{2,0},{4,6},{6,4},{8,10},{10,8},{12,14},{14,12},{16,18},{18,... | collective-permute-start | bytes 2359304 | tf_op jit(solution)/shard_map/ppermute | solution.py:513
  102.1 22.3 %collective-permute-start.28 = (bf16[192,1536]{1,0:T(8,128)(2,1)}, bf16[192,1536]{1,0:T(8,128)(2,1)S(1)}, u32[]{:S(2)}, u32[]{:S(2)}) collective-permute-start(bf16[192,1536]{1,0:T(8,128)(2,1)} %get-tuple-element.132), channel_id=1, source_target_pairs={{0,8},{2,10},{4,12},{6,14},{8,0},{10,2},{12,4},{14,6},{16,24},{18,... | collective-permute-start | bytes 1769480 | tf_op jit(solution)/shard_map/ppermute | solution.py:513
  104.0 13.8 %collective-permute-start.29 = (bf16[384,256]{1,0:T(8,128)(2,1)}, bf16[384,256]{1,0:T(8,128)(2,1)S(1)}, u32[]{:S(2)}, u32[]{:S(2)}) collective-permute-start(bf16[384,256]{1,0:T(8,128)(2,1)} %get-tuple-element.139), channel_id=1, source_target_pairs={{0,2},{2,0},{4,6},{6,4},{8,10},{10,8},{12,14},{14,12},{16,18},{18,... | collective-permute-start | bytes 589832 | tf_op jit(solution)/shard_map/ppermute | solution.py:513
  104.5 13.9 %collective-permute-start.30 = (bf16[384,256]{1,0:T(8,128)(2,1)}, bf16[384,256]{1,0:T(8,128)(2,1)S(1)}, u32[]{:S(2)}, u32[]{:S(2)}) collective-permute-start(bf16[384,256]{1,0:T(8,128)(2,1)} %get-tuple-element.140), channel_id=1, source_target_pairs={{0,4},{2,6},{4,0},{6,2},{8,12},{10,14},{12,8},{14,10},{16,20},{18,... | collective-permute-start | bytes 589832 | tf_op jit(solution)/shard_map/ppermute | solution.py:513
  111.4 25.2 %collective-permute-start.22 = (bf16[128,1536]{1,0:T(8,128)(2,1)S(1)}, bf16[128,1536]{1,0:T(8,128)(2,1)S(1)}, u32[]{:S(2)}, u32[]{:S(2)}) collective-permute-start(bf16[128,1536]{1,0:T(8,128)(2,1)S(1)} %slice.55), channel_id=1, source_target_pairs={{0,1},{1,0},{2,3},{3,2},{4,5},{5,4},{6,7},{7,6},{8,9},{9,8},{10,11... | collective-permute-start | bytes 1179656 | tf_op jit(solution)/shard_map/ppermute | solution.py:508
  118.4 15.2 %collective-permute-start.35 = (bf16[192,1536]{1,0:T(8,128)(2,1)}, bf16[192,1536]{1,0:T(8,128)(2,1)S(1)}, u32[]{:S(2)}, u32[]{:S(2)}) collective-permute-start(bf16[192,1536]{1,0:T(8,128)(2,1)} %get-tuple-element.158), channel_id=1, source_target_pairs={{0,4},{2,6},{4,0},{6,2},{8,12},{10,14},{12,8},{14,10},{16,20},{18,... | collective-permute-start | bytes 1769480 | tf_op jit(solution)/shard_map/ppermute | solution.py:513
  138.2 33.0 %collective-permute-start.37 = (bf16[96,1536]{1,0:T(8,128)(2,1)}, bf16[96,1536]{1,0:T(8,128)(2,1)}, u32[]{:S(2)}, u32[]{:S(2)}) collective-permute-start(bf16[96,1536]{1,0:T(8,128)(2,1)} %slice.98), channel_id=1, source_target_pairs={{0,16},{2,18},{4,20},{6,22},{8,24},{10,26},{12,28},{14,30},{16,0},... | collective-permute-start | bytes 884744 | tf_op jit(solution)/shard_map/ppermute | solution.py:513
  138.5 31.6 %collective-permute-start.33 = (bf16[96,1152]{1,0:T(8,128)(2,1)S(1)}, bf16[96,1152]{1,0:T(8,128)(2,1)S(1)}, u32[]{:S(2)}, u32[]{:S(2)}) collective-permute-start(bf16[96,1152]{1,0:T(8,128)(2,1)S(1)} %slice.99), channel_id=1, source_target_pairs={{0,16},{2,18},{4,20},{6,22},{8,24},{10,26},{12,28},{14,30},{16,0},... | collective-permute-start | bytes 663560 | tf_op jit(solution)/shard_map/ppermute | solution.py:513
  142.0 33.4 %collective-permute-start.38 = (bf16[96,1536]{1,0:T(8,128)(2,1)}, bf16[96,1536]{1,0:T(8,128)(2,1)}, u32[]{:S(2)}, u32[]{:S(2)}) collective-permute-start(bf16[96,1536]{1,0:T(8,128)(2,1)} %slice.97), channel_id=1, source_target_pairs={{0,16},{2,18},{4,20},{6,22},{8,24},{10,26},{12,28},{14,30},{16,0},... | collective-permute-start | bytes 884744 | tf_op jit(solution)/shard_map/ppermute | solution.py:513
  (55 other events, 540.7 us)

commit v3 on v2

v3 whole, which is shorter than its diff:
```python
import functools
import math

import jax
import jax.numpy as jnp
from jax import lax
from jax.experimental import pallas as pl
from jax.experimental.pallas import tpu as pltpu
from jax.sharding import PartitionSpec as P

HSIZE = 192
DILATION_STEP = 16
EPSILON = 1e-06
SOFT_CAP = 6.0
GELU_C = math.sqrt(2.0 / math.pi)
GELU_A = 0.044715
BF = jnp.bfloat16
F32 = jnp.float32
ORDER = (
    "q_sum", "mm", "v_sum", "back", "q_add", "k_sum", "tap_sum", "q_end", "v_add", "k_add", "o_sum",
    "v_end", "point_sum", "tap_add", "k_end", "o_add", "point_add", "tap_end", "o_end", "point_end",
)
SENDS = (
    ("q_far", "start"), ("v_far", "start"), ("k_far", "q_far"), ("wides", "near"),
    ("q_pass", "start"), ("v_pass", "start"), ("tap_far", "back"), ("resid_far", "tap_far"),
    ("k_pass", "back"), ("o_far", "back"), ("tap_pass", "back"), ("olds", "back"),
    ("o_pass", "tap_sum"), ("point_pass", "tap_sum"),
)
NEEDED = ("q_got",)
NO_COST = pl.CostEstimate(flops=0, bytes_accessed=0, transcendentals=0)


def gelu(x):
    return 0.5 * x * (1.0 + jnp.tanh(GELU_C * (x + GELU_A * (x * x * x))))


def gelu_slope(x):
    t = jnp.tanh(GELU_C * (x + GELU_A * (x * x * x)))
    return 0.5 * (1.0 + t) + 0.5 * x * (1.0 - t * t) * GELU_C * (1.0 + 3.0 * GELU_A * x * x)


def dot_nn(a, b):
    return lax.dot_general(a, b, (((1,), (0,)), ((), ())), preferred_element_type=F32)


def dot_nt(a, b):
    return lax.dot_general(a, b, (((1,), (1,)), ((), ())), preferred_element_type=F32)


def dot_tn(a, b):
    return lax.dot_general(a, b, (((0,), (0,)), ((), ())), preferred_element_type=F32)


def rms_scale(x):
    return lax.rsqrt(jnp.mean(x * x, axis=-1, keepdims=True) + EPSILON)


def row_chunk(rows):
    return 128 if rows % 128 == 0 else rows


def loop_chunks(count, body):
    if count <= 2:
        for i in range(count):
            body(i)
    else:

        def step(i, carry):
            body(i)
            return carry

        lax.fori_loop(0, count, step, 0)


def rows_at(i, size):
    if isinstance(i, int):
        return pl.ds(i * size, size)
    return pl.ds(pl.multiple_of(i * size, size), size)


def emit_rows(starts, wide, outs, rows):
    peers = len(outs) if len(outs) < 3 else 4
    parts = starts.shape[0] // peers
    size = rows // parts
    for p in range(peers):
        out, base = (outs[2], (p - 2) * rows) if p > 1 else (outs[p], 0)
        for k in range(parts):
            at = pl.multiple_of(starts[p * parts + k], 16)
            out[base + k * size : base + (k + 1) * size, :] = wide[pl.ds(at, size), :]


def wide_shapes(group, rows, length, extra=0):
    found = [shape_of(rows + extra, length)] * min(group, 2)
    return found + [shape_of(2 * rows + extra, length)] * (group > 2)


def shifted_sum(first, middle, last, offset):
    length = middle.shape[0]
    step = DILATION_STEP
    pos = lax.rem(lax.broadcasted_iota(jnp.int32, (length, 1), 0) + offset, length)
    down = jnp.concatenate([first[length - step :], first[: length - step]], axis=0)
    up = jnp.concatenate([last[step:], last[:step]], axis=0)
    return jnp.where(pos >= step, down, 0.0) + middle + jnp.where(pos < length - step, up, 0.0)


def vmem_params(arrays, copies=1):
    held = sum(math.prod(t.shape) * jnp.dtype(t.dtype).itemsize for t in arrays)
    return pltpu.CompilerParams(vmem_limit_bytes=min(56 << 20, copies * held + (8 << 20)))


def call(kernel, out_shape, operands, smem=1, scratch=()):
    specs = [pl.BlockSpec(memory_space=pltpu.SMEM)] * smem
    specs += [pl.BlockSpec(memory_space=pltpu.VMEM)] * (len(operands) - smem)
    return pl.pallas_call(
        kernel,
        out_shape=out_shape,
        in_specs=specs,
        out_specs=[pl.BlockSpec(memory_space=pltpu.VMEM)] * len(out_shape),
        scratch_shapes=list(scratch),
        compiler_params=vmem_params([*operands, *out_shape, *scratch]),
        cost_estimate=NO_COST,
    )(*operands)


def shape_of(rows, cols, dtype=BF):
    return jax.ShapeDtypeStruct((rows, cols), dtype)


def parts_shape(count, rows, cols):
    return jax.ShapeDtypeStruct((count, rows, cols), BF)


def store_parts(parts_ref, place, value):
    rows, size = parts_ref.shape[1], value.shape[0]
    for at in range(0, size, min(rows, size)):
        j, first = divmod(place * size + at, rows)
        parts_ref[j, first : first + min(rows, size), :] = value[at : at + min(rows, size)]


def summed_rows(parts_ref, moved, j, here):
    total = parts_ref[j, here, :].astype(F32)
    for ref in moved:
        total = total + ref[1 - j, here, :].astype(F32)
    return total


def piece_rows(j, rows, i, size):
    if isinstance(i, int):
        return pl.ds(j * rows + i * size, size)
    return pl.ds(pl.multiple_of(j * rows + i * size, size), size)


def scaled_rows(rows, factor, *ahead):
    def kernel(*refs):
        refs[-1][...] = (refs[0][...].astype(F32) * factor).astype(BF)

    return call(kernel, [shape_of(*rows.shape)], [rows, *ahead], 0)[0]


def conv_block(offset, pieces, taps, point):
    count = len(pieces)
    rows, channels = pieces[0].shape
    length = rows * count
    inner = point.shape[0]

    def kernel(*refs):
        offset_ref, ins = refs[0], refs[1 : 1 + count]
        taps_ref, point_ref, pre_ref, parts_ref, mid_ref, act_ref, prod = refs[1 + count :]
        size = row_chunk(rows)
        for j in range(count):

            def body(i, j=j):
                x = ins[j][rows_at(i, size), :].astype(F32)
                act_ref[piece_rows(j, rows, i, size), :] = gelu(x * rms_scale(x)).astype(BF)

            loop_chunks(rows // size, body)
        big = min(256, length)

        def product(i):
            here = rows_at(i, big)
            prod[here, :] = dot_nt(act_ref[here, :], taps_ref[...])

        loop_chunks(length // big, product)
        pre = shifted_sum(
            prod[:, :inner], prod[:, inner : 2 * inner], prod[:, 2 * inner :], offset_ref[0]
        )
        pre_ref[...] = pre
        mid_ref[...] = gelu(pre).astype(BF)
        for c in range(length // big):
            total = dot_nn(mid_ref[c * big : (c + 1) * big, :], point_ref[...])
            store_parts(parts_ref, c, total.astype(BF))

    outs = [
        shape_of(length, inner, F32),
        parts_shape(count, rows, channels),
        shape_of(length, inner),
        shape_of(length, channels),
    ]
    scratch = [pltpu.VMEM((length, 3 * inner), F32)]
    return call(kernel, outs, [offset, *pieces, taps, point], 1, scratch)


def pack_block(starts, act, middle, ring_rows, group):
    length, inner = middle.shape
    channels = act.shape[1]

    def kernel(*refs):
        starts_ref, act_ref, mid_ref = refs[:3]
        sent, wide = refs[3:-1], refs[-1]
        size = row_chunk(length)

        def body(i):
            here = rows_at(i, size)
            wide[:, here] = act_ref[here, :].T

        loop_chunks(length // size, body)
        emit_rows(starts_ref, wide, sent, ring_rows)
        turned = mid_ref[...].T
        for out in sent:
            out[out.shape[0] - inner :, :] = turned

    outs = wide_shapes(group, ring_rows, length, inner)
    scratch = [pltpu.VMEM((channels, length), BF)]
    return call(kernel, outs, [starts, act, middle], 1, scratch)


def head_grads(grad_y, out_w):
    def kernel(gy_ref, wo_ref, out_ref):
        out_ref[...] = dot_nt(gy_ref[...], wo_ref[...]).astype(BF)

    return call(kernel, [shape_of(grad_y.shape[0], out_w.shape[0])], [grad_y, out_w], 0)[0]


def norm_block(near, cross, pieces, parts, moved, ring_rows, group):
    count = len(pieces)
    rows, channels = pieces[0].shape
    length = rows * count

    def kernel(*refs):
        near_ref, cross_ref = refs[:2]
        ins = refs[2 : 2 + count]
        parts_ref = refs[2 + count]
        adds = refs[3 + count : 3 + count + len(moved)]
        rest = refs[3 + count + len(moved) :]
        res_ref, norm_ref = rest[:2]
        sent, wide = rest[2:-1], rest[-1]
        size = row_chunk(rows)
        for j in range(count):

            def body(i, j=j):
                here = piece_rows(j, rows, i, size)
                total = summed_rows(parts_ref, adds, j, rows_at(i, size))
                res = (ins[j][rows_at(i, size), :].astype(F32) + total).astype(BF)
                res_ref[here, :] = res
                res = res.astype(F32)
                a = (res * rms_scale(res)).astype(BF)
                norm_ref[here, :] = a
                wide[:, here] = a.T

            loop_chunks(rows // size, body)
        emit_rows(near_ref, wide, sent[: len(sent) // 2], ring_rows)
        emit_rows(cross_ref, wide, sent[len(sent) // 2 :], ring_rows)

    outs = [shape_of(length, channels), shape_of(length, channels)]
    sides = wide_shapes(group, ring_rows, length)
    outs += sides + sides
    scratch = [pltpu.VMEM((channels, length), BF)]
    res = call(kernel, outs, [near, cross, *pieces, parts, *moved], 2, scratch)
    return res[0], res[1], res[2 : 2 + len(sides)], res[2 + len(sides) :]


def widen_block(starts, pieces, ring_rows, group):
    count = len(pieces)
    rows, channels = pieces[0].shape
    length = rows * count

    def kernel(*refs):
        starts_ref = refs[0]
        ins = refs[1 : 1 + count]
        whole_ref = refs[1 + count]
        sent, wide = refs[2 + count : -1], refs[-1]
        size = row_chunk(rows)
        for j in range(count):

            def body(i, j=j):
                here = piece_rows(j, rows, i, size)
                a = ins[j][rows_at(i, size), :]
                whole_ref[here, :] = a
                wide[:, here] = a.T

            loop_chunks(rows // size, body)
        emit_rows(starts_ref, wide, sent, ring_rows)

    outs = [shape_of(length, channels)] + wide_shapes(group, ring_rows, length)
    scratch = [pltpu.VMEM((channels, length), BF)]
    res = call(kernel, outs, [starts, *pieces], 1, scratch)
    return res[0], res[1:]


def attention_block(normed, grad_heads, query_w, key_w, value_w, count):
    length, channels = normed.shape
    rows = length // count
    features = query_w.shape[0]
    heads = features // HSIZE
    joined = 2 if heads % 2 == 0 else 1
    inv_root = 1.0 / math.sqrt(HSIZE)
    chunk = min(256, length)

    def one_head(q, k, v, g):
        dq, at = [], []
        dk = dv = None
        for c in range(length // chunk):
            qc = q[c * chunk : (c + 1) * chunk]
            gc = g[c * chunk : (c + 1) * chunk]
            ratio = jnp.tanh(dot_nt(qc, k) * (inv_root / SOFT_CAP))
            unnormed = jnp.exp(SOFT_CAP * ratio)
            soft = unnormed / jnp.sum(unnormed, axis=-1, keepdims=True)
            low = soft.astype(BF)
            at.append(dot_nn(low, v))
            gs = dot_nt(gc, v)
            gs = soft * (gs - jnp.sum(soft * gs, axis=-1, keepdims=True))
            gs = (gs * (1.0 - ratio * ratio)).astype(BF)
            dq.append(dot_nn(gs, k) * inv_root)
            dk_c = dot_tn(gs, qc)
            dv_c = dot_tn(low, gc)
            dk = dk_c if dk is None else dk + dk_c
            dv = dv_c if dv is None else dv + dv_c
        return side(dq, 0), dk * inv_root, dv, side(at, 0)

    def side(parts, axis):
        return parts[0] if len(parts) == 1 else jnp.concatenate(parts, axis=axis)

    def kernel(n_ref, gh_ref, wq, wk, wv, *rest):
        refs, all_ref, dn_ref = rest[:4], rest[4], rest[5]
        q_ref, k_ref, v_ref = rest[6:]

        def project(i):
            here = rows_at(i, chunk)
            n = n_ref[here, :]
            for w, ref in ((wq, q_ref), (wk, k_ref), (wv, v_ref)):
                ref[here, :] = dot_nt(n, w[...]).astype(BF)

        loop_chunks(length // chunk, project)
        for h in range(0, heads, joined):
            found = []
            for m in range(h, h + joined):
                cols = slice(m * HSIZE, (m + 1) * HSIZE)
                found.append(
                    one_head(q_ref[:, cols], k_ref[:, cols], v_ref[:, cols], gh_ref[:, cols])
                )
            cols = slice(h * HSIZE, (h + joined) * HSIZE)
            for place, ref in enumerate(refs):
                value = side([t[place] for t in found], 1).astype(BF)
                ref[:, cols] = value
                all_ref[place, :, cols] = value
        for c in range(length // chunk):
            here = pl.ds(c * chunk, chunk)
            total = None
            for ref, w in zip(refs, (wq, wk, wv)):
                term = dot_nn(ref[here, :], w[...])
                total = term if total is None else total + term
            store_parts(dn_ref, c, total.astype(BF))

    outs = [shape_of(length, features)] * 4
    outs += [parts_shape(4, length, features), parts_shape(count, rows, channels)]
    scratch = [pltpu.VMEM((length, features), BF)] * 3
    return call(kernel, outs, [normed, grad_heads, query_w, key_w, value_w], 0, scratch)


def back_block(starts, residual, grad_y, parts, moved, pre, point, ring_rows, group):
    length, channels = residual.shape
    inner = point.shape[0]
    count, rows = parts.shape[:2]

    def kernel(*refs):
        starts_ref, res_ref, gy_ref, parts_ref = refs[:4]
        adds = refs[4 : 4 + len(moved)]
        pre_ref, point_ref = refs[4 + len(moved) : 6 + len(moved)]
        rest = refs[6 + len(moved) :]
        gc_ref = rest[0]
        sent = rest[1:-2]
        wide, resid_grad = rest[-2:]
        size = row_chunk(rows)
        for j in range(count):

            def body(i, j=j):
                here = piece_rows(j, rows, i, size)
                gn = summed_rows(parts_ref, adds, j, rows_at(i, size))
                res = res_ref[here, :].astype(F32)
                scale = rms_scale(res)
                inner_mean = jnp.mean(gn * res, axis=-1, keepdims=True)
                a = gy_ref[here, :].astype(F32) + (
                    scale * gn - res * (scale * scale * scale) * inner_mean
                )
                a = a.astype(BF)
                resid_grad[here, :] = a
                wide[:, here] = a.T

            loop_chunks(rows // size, body)
        big = min(256, length)

        def product(i):
            here = rows_at(i, big)
            gm = dot_nt(resid_grad[here, :], point_ref[...])
            gc_ref[here, :] = (gelu_slope(pre_ref[here, :]) * gm).astype(BF)

        loop_chunks(length // big, product)
        emit_rows(starts_ref, wide, sent, ring_rows)

    outs = [shape_of(length, inner)] + wide_shapes(group, ring_rows, length)
    scratch = [pltpu.VMEM((channels, length), BF), pltpu.VMEM((length, channels), BF)]
    res = call(
        kernel,
        outs,
        [starts, residual, grad_y, parts, *moved, pre, point],
        1,
        scratch,
    )
    return res[0], res[1:]


def store_halves(outs, total, side, cols):
    half = total.shape[0] // len(outs)
    for k, out in enumerate(outs):
        part = total[k * half : (k + 1) * half]
        out[:, side * cols : (side + 1) * cols] = part


def wide_rows(ref, place, rows):
    return ref[rows : 2 * rows, :] if place == 3 else ref[:rows, :]


def weight_sum(wides, narrows, place, halves):
    group = len(wides)
    rows = wides[0].shape[0]
    cols = narrows[0].shape[1]

    def kernel(*refs):
        total = None
        for p in range(group):
            b_ref = refs[group + p]
            b = b_ref[place] if len(b_ref.shape) == 3 else b_ref[...]
            term = dot_nn(wide_rows(refs[p], p, rows), b)
            total = term if total is None else total + term
        store_halves(refs[2 * group :], total.astype(BF), 0, cols)

    return call(kernel, [shape_of(rows // halves, cols)] * halves, [*wides, *narrows], 0)


def tap_sum(offset, packs, conv_narrows, halves, rows):
    group = len(packs)
    length, inner = conv_narrows[0].shape
    step = DILATION_STEP

    def kernel(offset_ref, *refs):
        pack_refs, conv_refs = refs[:group], refs[group : 2 * group]
        outs = refs[2 * group :]
        pos = lax.rem(lax.broadcasted_iota(jnp.int32, (length, 1), 0) + offset_ref[0], length)
        total = [None] * 3
        for p in range(group):
            a = wide_rows(pack_refs[p], p, rows)
            b = conv_refs[p][...]
            up = jnp.concatenate([b[step:], b[:step]], axis=0).astype(F32)
            down = jnp.concatenate([b[length - step :], b[: length - step]], axis=0).astype(F32)
            first = jnp.where(pos < length - step, up, 0.0).astype(BF)
            last = jnp.where(pos >= step, down, 0.0).astype(BF)
            terms = [dot_nn(a, moved) for moved in (first, b, last)]
            total = [t if old is None else old + t for old, t in zip(total, terms)]
        for side in range(3):
            store_halves(outs, total[side].astype(BF), side, inner)

    outs = [shape_of(rows // halves, 3 * inner)] * halves
    return call(kernel, outs, [offset, *packs, *conv_narrows], 1)


def point_sum(packs, resid_wides, halves):
    group = len(packs)
    rows = resid_wides[0].shape[0]
    inner = packs[0].shape[0] - rows

    def kernel(*refs):
        pack_refs, wide_refs = refs[:group], refs[group : 2 * group]
        total = None
        for p in range(group):
            middle = pack_refs[p][pack_refs[p].shape[0] - inner :, :]
            term = dot_nt(wide_rows(wide_refs[p], p, rows), middle)
            total = term if total is None else total + term
        store_halves(refs[2 * group :], total.astype(BF), 0, inner)

    outs = [shape_of(rows // halves, inner)] * halves
    return call(kernel, outs, [*packs, *resid_wides], 0)


def add_block(kept, got):
    rows, cols = kept.shape
    half = rows // 2

    def kernel(kept_ref, got_ref, first_ref, second_ref):
        first_ref[...] = kept_ref[:half, :].astype(F32) + got_ref[:half, :].astype(F32)
        second = kept_ref[half:, :].astype(F32) + got_ref[half:, :].astype(F32)
        second_ref[...] = second.astype(BF)

    return call(kernel, [shape_of(half, cols, F32), shape_of(half, cols)], [kept, got], 0)


def last_block(kept, got, form):
    rows, cols = kept.shape
    if form == "taps":
        out = jax.ShapeDtypeStruct((3, rows, cols // 3), F32)
    else:
        out = shape_of(rows, cols, F32)

    def kernel(*refs):
        total = refs[0][...].astype(F32)
        for ref in refs[1:-1]:
            total = total + ref[...].astype(F32)
        out_ref = refs[-1]
        if form == "taps":
            for k in range(3):
                out_ref[k] = total[:, k * (cols // 3) : (k + 1) * (cols // 3)]
        else:
            out_ref[...] = total

    return call(kernel, [out], [kept] if got is None else [kept, got], 0)[0]


def after(value, *others):
    return lax.optimization_barrier((value, others))[0]


def shards(
    inputs,
    dilated_tap_weight,
    point_weight,
    query_weight,
    key_weight,
    value_weight,
    out_weight,
    cotangent,
):
    channels = inputs.shape[2]
    own = inputs[0]
    rows = own.shape[0]
    n_seq = lax.axis_size("seq")
    n_dp = lax.axis_size("dp")
    length = rows * n_seq
    pair = n_seq == 2
    block = channels // n_dp
    inner = point_weight.shape[0]
    features = query_weight.shape[0]
    inv_tokens = 1.0 / math.sqrt(inputs.shape[0] * n_dp * length)

    bits = [1 << i for i in range(n_dp.bit_length() - 1)]
    near_bits, near_rest = bits[:2], bits[2:]
    cross_bits, cross_rest = near_bits, near_rest
    if len(bits) > 2:
        cross_bits, cross_rest = [bits[0], bits[2]], [bits[1], *bits[3:]]
    group = 1 << len(near_bits)
    ring_rows = channels // group
    halves = 2 if near_rest else 1

    me_dp = lax.axis_index("dp")
    me_seq = lax.axis_index("seq")

    def combos(of):
        found = [0]
        for bit in of:
            found += [value | bit for value in found]
        return found

    def starts_of(peers, rest):
        order = combos(rest[::-1])
        places = [peer ^ k for peer in combos(peers) for k in order]
        return ((me_dp ^ jnp.array(places, jnp.int32)) * block).astype(jnp.int32)

    near = starts_of(near_bits, near_rest)
    cross = starts_of(cross_bits, cross_rest)
    offset = (me_seq * rows if pair else jnp.int32(0)).astype(jnp.int32).reshape(1)

    def swap_seq(x):
        return lax.ppermute(x, "seq", [(0, 1), (1, 0)])

    def to_peer(x, bit):
        if bit == 0:
            return x
        return lax.ppermute(x, "dp", [(i, i ^ bit) for i in range(n_dp)])

    def gather_seq(x):
        if pair:
            return [x, swap_seq(x)]
        return [lax.all_gather(x, "seq", axis=0, tiled=True)]

    def add_seq(parts):
        if pair:
            return parts, [swap_seq(parts)]
        summed = lax.psum_scatter(parts[0], "seq", scatter_dimension=0, tiled=True)
        return lax.all_gather(summed, "seq", axis=0, tiled=True)[None], []

    def send_wide(pieces, peers):
        return [pieces[0]] + [to_peer(piece, p) for piece, p in zip(pieces[1:], peers)]

    def pass_on(got, peers):
        return list(got) + ([to_peer(got[2], peers[0])] if len(peers) > 1 else [])

    def send_far(x, peers):
        return to_peer(x, peers[1]) if len(peers) > 1 else None

    def gathered(x, near_copy, far_copy, peers):
        return pass_on([x, near_copy, far_copy][: 1 + len(peers)], peers)

    def send_half(totals, rest):
        return to_peer(totals[1], rest[0]) if rest else None

    def add_half(totals, got, rest):
        kept = totals[0]
        for bit in rest[1:]:
            kept, sent = add_block(kept, got)
            got = to_peer(sent, bit)
        return kept, got

    pieces = gather_seq(own)
    taps = dilated_tap_weight.reshape(3 * inner, channels)
    grad_own = scaled_rows(cotangent[0], inv_tokens, own, taps)
    grad_pieces = gather_seq(grad_own)
    pre, parts, middle, act = conv_block(offset, pieces, taps, point_weight)
    pre, parts, middle, act, grad_pieces = lax.optimization_barrier(
        (pre, parts, middle, act, grad_pieces)
    )
    parts, moved = add_seq(parts)
    packs = pack_block(near, act, middle, ring_rows, group)
    packs = send_wide(packs, near_bits)
    grad_y, grad_wide = widen_block(cross, grad_pieces, ring_rows, group)
    grad_wide = send_wide(grad_wide, cross_bits)
    grad_heads = head_grads(grad_y, out_weight)
    moved = after(moved, packs, grad_wide, grad_heads)
    residual, normed, norm_near, norm_cross = norm_block(
        near, cross, pieces, parts, moved, ring_rows, group
    )
    norm_near = send_wide(norm_near, near_bits)
    norm_cross = send_wide(norm_cross, cross_bits)

    *deltas, delta_all, grad_parts = attention_block(
        normed, grad_heads, query_weight, key_weight, value_weight, len(pieces)
    )
    grad_parts, deltas, delta_all, norm_near, norm_cross = lax.optimization_barrier(
        (grad_parts, deltas, delta_all, norm_near, norm_cross)
    )
    attended = deltas[3]
    grad_parts, grad_moved = add_seq(grad_parts)
    delta_near = to_peer(delta_all, bits[0]) if bits else None

    peers = {name: near_bits for name in ("q", "k", "tap", "point")}
    peers.update({name: cross_bits for name in ("v", "o")})
    rest = {name: cross_rest if peers[name] is cross_bits else near_rest for name in peers}
    place = {"q": 0, "k": 1, "v": 2, "o": 3}
    found = {}

    def wanted(value, *names):
        names = [name for name in names if name in found]
        return after(value, *[found[name] for name in names]) if names else value

    wides = {"q": norm_near, "k": norm_near, "v": norm_cross, "o": grad_wide, "tap": packs}

    def open_gates():
        for name, condition in SENDS:
            if name in found or condition not in found:
                continue
            if name == "wides":
                near_wide = pass_on(after(norm_near, found[condition]), near_bits)
                cross_wide = pass_on(after(norm_cross, found[condition]), cross_bits)
                wides.update({"q": near_wide, "k": near_wide, "v": cross_wide})
                found[name] = near_wide
            elif name == "olds":
                wides["o"] = pass_on(after(grad_wide, found[condition]), cross_bits)
                wides["tap"] = pass_on(after(packs, found[condition]), near_bits)
                found[name] = wides["o"]
            elif name == "resid_far":
                found[name] = send_wide(after(found["resid"], found[condition]), near_bits)
            elif name in ("q_pass", "k_pass", "v_pass", "o_pass", "tap_pass", "point_pass"):
                which = name[:-5]
                if which == "point":
                    got = after(found["resid_far"], found[condition])
                    found[name] = pass_on(got, near_bits)
                    continue
                far = after(found[which + "_far"], found[condition])
                mine = found["conv"] if which == "tap" else deltas[place[which]]
                near_copy = found["conv_near"] if which == "tap" else delta_near
                found[name] = gathered(mine, near_copy, far, peers[which])
            elif name == "tap_far":
                found[name] = send_far(after(found["conv"], found[condition]), near_bits)
            else:
                which = name[:-4]
                mine = after(deltas[place[which]], found[condition])
                found[name] = send_far(mine, peers[which])

    found["start"] = grad_parts
    found["near"] = delta_near
    previous = "start"
    open_gates()
    for step in ORDER:
        which, _, kind = step.partition("_")
        if step == "mm":
            found[step] = dot_nn(wanted(attended, previous), out_weight).astype(BF)
        elif step == "back":
            moved = wanted(grad_moved, previous)
            conv, resid = back_block(
                near, residual, grad_y, grad_parts, moved, pre, point_weight, ring_rows, group
            )
            names = [name for name in NEEDED if name in found]
            conv, resid, gots = lax.optimization_barrier(
                (conv, resid, [found[name] for name in names])
            )
            found.update(dict(zip(names, gots)))
            found["conv"], found["resid"], found[step] = conv, resid, conv
            found["conv_near"] = to_peer(conv, bits[0]) if bits else None
        elif kind == "sum":
            if which == "tap":
                narrow = wanted(found["tap_pass"], previous)
                total = tap_sum(offset, wides["tap"], narrow, halves, ring_rows)
            elif which == "point":
                total = point_sum(wides["tap"], wanted(found["point_pass"], previous), halves)
            else:
                narrow = wanted(found[which + "_pass"], previous)
                total = weight_sum(wides[which], narrow, place[which], halves)
            found[step] = total
            found[which + "_got"] = send_half(total, rest[which])
        elif kind == "add":
            got = wanted(found[which + "_got"], previous)
            found[step] = add_half(found[which + "_sum"], got, rest[which])
        elif kind == "end":
            kept, got = wanted(found[which + "_add"], previous)
            found[step] = last_block(kept, got, "taps" if which == "tap" else "plain")
        if kind == "add":
            found[step + "_kept"] = found[step][0]
            previous = step + "_kept"
        else:
            previous = step
        open_gates()

    attn_part = after(found["mm"], found["back"])
    if pair:
        attn_rows = attn_part[:rows].astype(F32) + swap_seq(attn_part[rows:]).astype(F32)
        res_own = residual[:rows]
    else:
        attn_rows = lax.psum_scatter(attn_part, "seq", scatter_dimension=0, tiled=True)
        attn_rows = attn_rows.astype(F32)
        res_own = lax.dynamic_slice_in_dim(residual, me_seq * rows, rows, 0)
    output = (res_own.astype(F32) + attn_rows).astype(BF)[None]
    return (
        output,
        found["tap_end"],
        found["point_end"].T,
        found["q_end"],
        found["k_end"],
        found["v_end"],
        found["o_end"].T,
    )


def solution(mesh):
    placed = (
        P("dp", "seq", None),
        P(None, "seq", None),
        P("seq", None),
        P("seq", None),
        P("seq", None),
        P("seq", None),
        P("seq", None),
        P("dp", "seq", None),
    )
    return jax.shard_map(
        shards,
        mesh=mesh,
        in_specs=placed,
        out_specs=(
            P("dp", "seq", None),
            P(None, "dp", "seq"),
            P("seq", "dp"),
            P("dp", "seq"),
            P("dp", "seq"),
            P("dp", "seq"),
            P("seq", "dp"),
        ),
        check_vma=False,
    )
```

time: 178 us -> 147 us (0.83)
  Pallas kernels: 47.6 us -> 27 us
  waiting for transfers between devices: 74.1 us -> 67.6 us
  other arithmetic: 6.42 us -> 0.89 us
  starting transfers between devices: 39.4 us -> 43.4 us
    pallas_call x1 -> x0, Pallas kernels: 13.5 us -> none  [attention_block(): pl.pallas_call(kernel, grid=(heads // per_step,), out_shape=[jax.ShapeDty...]
    ppermute x7 -> x5, waiting for transfers between devices: 23.9 us -> 13.1 us  [swap_seq(): return lax.ppermute(x, 'seq', [(0, 1), (1, 0)])]
    pallas_call x8 -> x26, Pallas kernels: 34.1 us -> 27 us  [call(): pl.pallas_call(kernel, out_shape=out_shape, in_specs=specs, out_specs=[pl...]
    ppermute x32 -> x39, starting transfers between devices: 29.3 us -> 35.5 us  [to_peer(): return lax.ppermute(x, 'dp', [(i, i ^ bit) for i in range(n_dp)])]
    ppermute x32 -> x39, waiting for transfers between devices: 50.2 us -> 54.5 us  [to_peer(): return lax.ppermute(x, 'dp', [(i, i ^ bit) for i in range(n_dp)])]
    add x7 -> x0, other arithmetic: 2.51 us -> none  [the longest x3 2.08 us: later_halves(): kept = kept[:half] + got.astype(F32)]
    slice x5 -> x0, local copies, waits for them, and re-layouts: 2.38 us -> none  [the longest x4 1.53 us: later_halves(): got = to_peer(kept[half:].astype(BF), bit)]
    ppermute x7 -> x5, starting transfers between devices: 10.1 us -> 7.89 us  [swap_seq(): return lax.ppermute(x, 'seq', [(0, 1), (1, 0)])]
  transfers between devices with their start and end apart: 39 -> 44, of which waited for: 11 -> 21; matrix products, arithmetic and copies ran while one was open for 5% -> 1% of each run, Pallas kernels for 24% -> 17%
where the time goes in v3:
time: 147 us
  waiting for transfers between devices  67.6 us (46%)
  starting transfers between devices  43.4 us (30%)
  Pallas kernels  27 us (18%)
  local copies, waits for them, and re-layouts  6.32 us (4%)
    ppermute x39, waiting for transfers between devices, to_peer(): return lax.ppermute(x, 'dp', [(i, i ^ bit) for i in range(n_dp)])  54.5 us
    ppermute x39, starting transfers between devices, to_peer(): return lax.ppermute(x, 'dp', [(i, i ^ bit) for i in range(n_dp)])  35.5 us
    pallas_call x26, Pallas kernels, call(): pl.pallas_call(kernel, out_shape=out_shape, in_specs=specs, out_specs=[pl...  27 us
    ppermute x5, waiting for transfers between devices, swap_seq(): return lax.ppermute(x, 'seq', [(0, 1), (1, 0)])  13.1 us
    ppermute x5, starting transfers between devices, swap_seq(): return lax.ppermute(x, 'seq', [(0, 1), (1, 0)])  7.89 us
    unnamed x28, local copies, waits for them, and re-layouts  6.3 us
  transfers between devices with their start and end apart: 44, of which 21 were waited for; matrix products, arithmetic and copies ran while one was open for 1% of the time, Pallas kernels for 17%

profile of v3, /device:TPU:0, one launch (start us, length us, event | category | flops | bytes accessed | tf_op | source)
XLA Modules:
  0.0 146.9 jit_solution(6509500823189374413)
XLA Ops:
  0.6 3.0 %collective-permute-start = (bf16[128,1536]{1,0:T(8,128)(2,1)}, bf16[128,1536]{1,0:T(8,128)(2,1)}, u32[]{:S(2)}, u32[]{:S(2)}) collective-permute-start(bf16[128,1536]{1,0:T(8,128)(2,1)} %bitcast.12), channel_id=1, source_target_pairs={{0,1},{1,0},{2,3},{3,2},{4,5},{5,4},{6,7},{7,6},{8,9},{9,8},{10,11... | collective-permute-start | bytes 1179656 | tf_op jit(solution)/shard_map/ppermute | solution.py:581
  3.7 2.0 %copy-done = bf16[3,384,1536]{2,1,0:T(8,128)(2,1)S(1)} copy-done((bf16[3,384,1536]{2,1,0:T(8,128)(2,1)S(1)}, bf16[3,384,1536]{2,1,0:T(8,128)(2,1)}, u32[]{:S(2)}) %copy-start) | copy-done | bytes 3538968
  8.5 5.4 %collective-permute-done.refs_2_.refs_3_ = bf16[128,1536]{1,0:T(8,128)(2,1)} collective-permute-done((bf16[128,1536]{1,0:T(8,128)(2,1)}, bf16[128,1536]{1,0:T(8,128)(2,1)}, u32[]{:S(2)}, u32[]{:S(2)}) %collective-permute-start) | collective-permute-done | bytes 393248 | tf_op jit(solution)/shard_map/ppermute | solution.py:581
  16.2 3.4 %shard_map.153 = (f32[256,384]{1,0:T(8,128)S(1)}, bf16[2,128,1536]{2,1,0:T(8,128)(2,1)S(1)}, bf16[256,384]{1,0:T(8,128)(2,1)S(1)}, bf16[256,1536]{1,0:T(8,128)(2,1)S(1)}) custom-call(s32[1]{0:T(128)} %bitcast.1.refs_0_.offset_ref, bf16[128,1536]{1,0:T(8,128)(2,1)S(1)} %bitcast.14, bf16[128,1536]{1,0:T(8,128)(2,1)} %collective-permute-done.refs_2_.refs_3_, ...), custom_call_target="tpu_custom_call" | custom-call | tf_op jit(solution)/shard_map/pallas_call | solution.py:114
  19.6 1.9 %collective-permute-done.1.refs_2_ = bf16[128,1536]{1,0:T(8,128)(2,1)} collective-permute-done((bf16[128,1536]{1,0:T(8,128)(2,1)}, bf16[128,1536]{1,0:T(8,128)(2,1)}, u32[]{:S(2)}, u32[]{:S(2)}) %collective-permute-start.1) | collective-permute-done | bytes 393248 | tf_op jit(solution)/shard_map/ppermute | solution.py:581
  21.5 1.7 %collective-permute-start.2 = (bf16[2,128,1536]{2,1,0:T(8,128)(2,1)S(1)}, bf16[2,128,1536]{2,1,0:T(8,128)(2,1)S(1)}, u32[]{:S(2)}, u32[]{:S(2)}) collective-permute-start(bf16[2,128,1536]{2,1,0:T(8,128)(2,1)S(1)} %get-tuple-element.161.refs_4_), channel_id=1, source_target_pairs={{0,1},{1,0},{2,3},{3,2},{4,5},{5,4},{6,7},{7,6},{8,9},{9,8},{10,11... | collective-permute-start | bytes 2359304 | tf_op jit(solution)/shard_map/ppermute | solution.py:581
  30.8 5.8 %collective-permute-done.6.refs_2_ = bf16[768,256]{1,0:T(8,128)(2,1)S(1)} collective-permute-done((bf16[768,256]{1,0:T(8,128)(2,1)S(1)}, bf16[768,256]{1,0:T(8,128)(2,1)S(1)}, u32[]{:S(2)}, u32[]{:S(2)}) %collective-permute-start.6) | collective-permute-done | bytes 393248 | tf_op jit(solution)/shard_map/ppermute | solution.py:586
  38.2 2.1 %collective-permute-done.2.refs_5_ = bf16[2,128,1536]{2,1,0:T(8,128)(2,1)S(1)} collective-permute-done((bf16[2,128,1536]{2,1,0:T(8,128)(2,1)S(1)}, bf16[2,128,1536]{2,1,0:T(8,128)(2,1)S(1)}, u32[]{:S(2)}, u32[]{:S(2)}) %collective-permute-start.2) | collective-permute-done | bytes 786464 | tf_op jit(solution)/shard_map/ppermute | solution.py:581
  40.3 1.8 %shard_map.158 = (bf16[256,1536]{1,0:T(8,128)(2,1)S(1)}, bf16[256,1536]{1,0:T(8,128)(2,1)S(1)}, bf16[384,256]{1,0:T(8,128)(2,1)S(1)}, bf16[384,256]{1,0:T(8,128)...) custom-call(s32[16]{0:T(128)S(1)} %get-tuple-element.308.refs_0_, ...), custom_call_target="tpu_custom_call" | custom-call | tf_op jit(solution)/shard_map/pallas_call | solution.py:114
  45.6 5.8 %shard_map.159 = (bf16[256,768]{1,0:T(8,128)(2,1)S(1)}, bf16[256,768]{1,0:T(8,128)(2,1)S(1)}, bf16[256,768]{1,0:T(8,128)(2,1)S(1)}, bf16[256,768]{1,0:T(8,128)(2...) custom-call(bf16[256,1536]{1,0:T(8,128)(2,1)S(1)} %get-tuple-element.175.n_ref, ...), custom_call_target="tpu_custom_call" | custom-call | tf_op jit(solution)/shard_map/pallas_call | solution.py:114
  55.8 8.1 %collective-permute-done.13.refs_6_ = bf16[256,768]{1,0:T(8,128)(2,1)S(1)} collective-permute-done((bf16[256,768]{1,0:T(8,128)(2,1)S(1)}, bf16[256,768]{1,0:T(8,128)(2,1)S(1)}, u32[]{:S(2)}, u32[]{:S(2)}) %collective-permute-start.13) | collective-permute-done | bytes 393248 | tf_op jit(solution)/shard_map/ppermute | solution.py:586
  70.0 3.7 %collective-permute-done.15.refs_4_ = bf16[2,128,1536]{2,1,0:T(8,128)(2,1)S(1)} collective-permute-done((bf16[2,128,1536]{2,1,0:T(8,128)(2,1)S(1)}, bf16[2,128,1536]{2,1,0:T(8,128)(2,1)S(1)}, u32[]{:S(2)}, u32[]{:S(2)}) %collective-permute-start.15) | collective-permute-done | bytes 786464 | tf_op jit(solution)/shard_map/ppermute | solution.py:581
  73.7 2.1 %shard_map.162 = (bf16[256,384]{1,0:T(8,128)(2,1)S(1)}, bf16[384,256]{1,0:T(8,128)(2,1)S(1)}, bf16[384,256]{1,0:T(8,128)(2,1)S(1)}, bf16[768,256]{1,0:T(8,128)(2,1)S(1)}) custom-call(s32[16]{0:T(128)S(1)} %get-tuple-element.308.refs_0_, bf16[256,1536]{1,0:T(8,128)(2,1)S(1)} %get-tuple-element.174.refs_1_, ...), custom_call_target="tpu_custom_call" | custom-call | tf_op jit(solution)/shard_map/pallas_call | solution.py:114
  79.0 5.1 %collective-permute-done.23.refs_6_ = bf16[256,384]{1,0:T(8,128)(2,1)S(1)} collective-permute-done((bf16[256,384]{1,0:T(8,128)(2,1)S(1)}, bf16[256,384]{1,0:T(8,128)(2,1)S(1)}, u32[]{:S(2)}, u32[]{:S(2)}) %collective-permute-start.23) | collective-permute-done | bytes 196640 | tf_op jit(solution)/shard_map/ppermute | solution.py:586
  90.8 5.2 %collective-permute-done.29.refs_6_ = bf16[768,256]{1,0:T(8,128)(2,1)S(1)} collective-permute-done((bf16[768,256]{1,0:T(8,128)(2,1)S(1)}, bf16[768,256]{1,0:T(8,128)(2,1)S(1)}, u32[]{:S(2)}, u32[]{:S(2)}) %collective-permute-start.29) | collective-permute-done | bytes 393248 | tf_op jit(solution)/shard_map/ppermute | solution.py:586
  96.0 2.6 %collective-permute-start.32 = (bf16[96,768]{1,0:T(8,128)(2,1)S(1)}, bf16[96,768]{1,0:T(8,128)(2,1)S(1)}, u32[]{:S(2)}, u32[]{:S(2)}) collective-permute-start(bf16[96,768]{1,0:T(8,128)(2,1)S(1)} %get-tuple-element.262), channel_id=1, source_target_pairs={{0,16},{2,18},{4,20},{6,22},{8,24},{10,26},{12,28},{14,30},{16,0},... | collective-permute-start | bytes 442376 | tf_op jit(solution)/shard_map/ppermute | solution.py:586
  98.6 3.3 %collective-permute-done.31.got_ref = bf16[192,768]{1,0:T(8,128)(2,1)S(1)} collective-permute-done((bf16[192,768]{1,0:T(8,128)(2,1)S(1)}, bf16[192,768]{1,0:T(8,128)(2,1)S(1)}, u32[]{:S(2)}, u32[]{:S(2)}) %collective-permute-start.31) | collective-permute-done | bytes 294944 | tf_op jit(solution)/shard_map/ppermute | solution.py:586
  102.0 3.3 %collective-permute-done.32.refs_1_ = bf16[96,768]{1,0:T(8,128)(2,1)S(1)} collective-permute-done((bf16[96,768]{1,0:T(8,128)(2,1)S(1)}, bf16[96,768]{1,0:T(8,128)(2,1)S(1)}, u32[]{:S(2)}, u32[]{:S(2)}) %collective-permute-start.32) | collective-permute-done | bytes 147488 | tf_op jit(solution)/shard_map/ppermute | solution.py:586
  107.7 3.3 %collective-permute-start.33 = (bf16[96,768]{1,0:T(8,128)(2,1)S(1)}, bf16[96,768]{1,0:T(8,128)(2,1)S(1)}, u32[]{:S(2)}, u32[]{:S(2)}) collective-permute-start(bf16[96,768]{1,0:T(8,128)(2,1)S(1)} %get-tuple-element.267), channel_id=1, source_target_pairs={{0,16},{2,18},{4,20},{6,22},{8,24},{10,26},{12,28},{14,30},{16,0},... | collective-permute-start | bytes 442376 | tf_op jit(solution)/shard_map/ppermute | solution.py:586
  113.2 3.9 %collective-permute-done.33.refs_1_ = bf16[96,768]{1,0:T(8,128)(2,1)S(1)} collective-permute-done((bf16[96,768]{1,0:T(8,128)(2,1)S(1)}, bf16[96,768]{1,0:T(8,128)(2,1)S(1)}, u32[]{:S(2)}, u32[]{:S(2)}) %collective-permute-start.33) | collective-permute-done | bytes 147488 | tf_op jit(solution)/shard_map/ppermute | solution.py:586
  117.1 3.4 %collective-permute-start.41 = (bf16[96,768]{1,0:T(8,128)(2,1)S(1)}, bf16[96,768]{1,0:T(8,128)(2,1)S(1)}, u32[]{:S(2)}, u32[]{:S(2)}) collective-permute-start(bf16[96,768]{1,0:T(8,128)(2,1)S(1)} %get-tuple-element.292), channel_id=1, source_target_pairs={{0,16},{2,18},{4,20},{6,22},{8,24},{10,26},{12,28},{14,30},{16,0},... | collective-permute-start | bytes 442376 | tf_op jit(solution)/shard_map/ppermute | solution.py:586
  122.9 2.7 %collective-permute-done.41.refs_1_ = bf16[96,768]{1,0:T(8,128)(2,1)S(1)} collective-permute-done((bf16[96,768]{1,0:T(8,128)(2,1)S(1)}, bf16[96,768]{1,0:T(8,128)(2,1)S(1)}, u32[]{:S(2)}, u32[]{:S(2)}) %collective-permute-start.41) | collective-permute-done | bytes 147488 | tf_op jit(solution)/shard_map/ppermute | solution.py:586
  125.5 2.7 %collective-permute-start.38 = (bf16[96,1152]{1,0:T(8,128)(2,1)S(1)}, bf16[96,1152]{1,0:T(8,128)(2,1)S(1)}, u32[]{:S(2)}, u32[]{:S(2)}) collective-permute-start(bf16[96,1152]{1,0:T(8,128)(2,1)S(1)} %get-tuple-element.291), channel_id=1, source_target_pairs={{0,16},{2,18},{4,20},{6,22},{8,24},{10,26},{12,28},{14,30},{16,0},... | collective-permute-start | bytes 663560 | tf_op jit(solution)/shard_map/ppermute | solution.py:586
  133.0 10.5 %collective-permute-done.38.refs_1_ = bf16[96,1152]{1,0:T(8,128)(2,1)S(1)} collective-permute-done((bf16[96,1152]{1,0:T(8,128)(2,1)S(1)}, bf16[96,1152]{1,0:T(8,128)(2,1)S(1)}, u32[]{:S(2)}, u32[]{:S(2)}) %collective-permute-start.38) | collective-permute-done | bytes 221216 | tf_op jit(solution)/shard_map/ppermute | solution.py:586
  (122 shorter events, 53.0 us)
Async XLA Ops:
  0.6 13.3 %collective-permute-start = (bf16[128,1536]{1,0:T(8,128)(2,1)}, bf16[128,1536]{1,0:T(8,128)(2,1)}, u32[]{:S(2)}, u32[]{:S(2)}) collective-permute-start(bf16[128,1536]{1,0:T(8,128)(2,1)} %bitcast.12), channel_id=1, source_target_pairs={{0,1},{1,0},{2,3},{3,2},{4,5},{5,4},{6,7},{7,6},{8,9},{9,8},{10,11... | collective-permute-start | bytes 1179656 | tf_op jit(solution)/shard_map/ppermute | solution.py:581
  8.5 13.1 %collective-permute-start.1 = (bf16[128,1536]{1,0:T(8,128)(2,1)}, bf16[128,1536]{1,0:T(8,128)(2,1)}, u32[]{:S(2)}, u32[]{:S(2)}) collective-permute-start(bf16[128,1536]{1,0:T(8,128)(2,1)} %shard_map.154.refs_1_), channel_id=1, source_target_pairs={{0,1},{1,0},{2,3},{3,2},{4,5},{5,4},{6,7},{7,6},{8,9},{9,8},{10,11... | collective-permute-start | bytes 1179656 | tf_op jit(solution)/shard_map/ppermute | solution.py:581
  21.5 18.7 %collective-permute-start.2 = (bf16[2,128,1536]{2,1,0:T(8,128)(2,1)S(1)}, bf16[2,128,1536]{2,1,0:T(8,128)(2,1)S(1)}, u32[]{:S(2)}, u32[]{:S(2)}) collective-permute-start(bf16[2,128,1536]{2,1,0:T(8,128)(2,1)S(1)} %get-tuple-element.161.refs_4_), channel_id=1, source_target_pairs={{0,1},{1,0},{2,3},{3,2},{4,5},{5,4},{6,7},{7,6},{8,9},{9,8},{10,11... | collective-permute-start | bytes 2359304 | tf_op jit(solution)/shard_map/ppermute | solution.py:581
  24.2 14.0 %collective-permute-start.4 = (bf16[1152,256]{1,0:T(8,128)(2,1)S(1)}, bf16[1152,256]{1,0:T(8,128)(2,1)S(1)}, u32[]{:S(2)}, u32[]{:S(2)}) collective-permute-start(bf16[1152,256]{1,0:T(8,128)(2,1)S(1)} %get-tuple-element.166), channel_id=1, source_target_pairs={{0,4},{2,6},{4,0},{6,2},{8,12},{10,14},{12,8},{14,10},{16,20},{18,... | collective-permute-start | bytes 1769480 | tf_op jit(solution)/shard_map/ppermute | solution.py:586
  27.2 9.5 %collective-permute-start.6 = (bf16[768,256]{1,0:T(8,128)(2,1)S(1)}, bf16[768,256]{1,0:T(8,128)(2,1)S(1)}, u32[]{:S(2)}, u32[]{:S(2)}) collective-permute-start(bf16[768,256]{1,0:T(8,128)(2,1)S(1)} %get-tuple-element.171), channel_id=1, source_target_pairs={{0,8},{2,10},{4,12},{6,14},{8,0},{10,2},{12,4},{14,6},{16,24},{18,... | collective-permute-start | bytes 1179656 | tf_op jit(solution)/shard_map/ppermute | solution.py:586
  52.4 11.5 %collective-permute-start.11 = (bf16[4,256,768]{2,1,0:T(8,128)(2,1)S(1)}, bf16[4,256,768]{2,1,0:T(8,128)(2,1)S(1)}, u32[]{:S(2)}, u32[]{:S(2)}) collective-permute-start(bf16[4,256,768]{2,1,0:T(8,128)(2,1)S(1)} %get-tuple-element.192), channel_id=1, source_target_pairs={{0,2},{2,0},{4,6},{6,4},{8,10},{10,8},{12,14},{14,12},{16,18},{18,... | collective-permute-start | bytes 4718600 | tf_op jit(solution)/shard_map/ppermute | solution.py:586
  52.4 11.5 %collective-permute-start.13 = (bf16[256,768]{1,0:T(8,128)(2,1)S(1)}, bf16[256,768]{1,0:T(8,128)(2,1)S(1)}, u32[]{:S(2)}, u32[]{:S(2)}) collective-permute-start(bf16[256,768]{1,0:T(8,128)(2,1)S(1)} %get-tuple-element.200.refs_4_), channel_id=1, source_target_pairs={{0,4},{2,6},{4,0},{6,2},{8,12},{10,14},{12,8},{14,10},{16,20},{18,... | collective-permute-start | bytes 1179656 | tf_op jit(solution)/shard_map/ppermute | solution.py:586
  53.9 11.2 %collective-permute-start.17 = (bf16[256,768]{1,0:T(8,128)(2,1)S(1)}, bf16[256,768]{1,0:T(8,128)(2,1)S(1)}, u32[]{:S(2)}, u32[]{:S(2)}) collective-permute-start(bf16[256,768]{1,0:T(8,128)(2,1)S(1)} %get-tuple-element.216.refs_4_), channel_id=1, source_target_pairs={{0,8},{2,10},{4,12},{6,14},{8,0},{10,2},{12,4},{14,6},{16,24},{18,... | collective-permute-start | bytes 1179656 | tf_op jit(solution)/shard_map/ppermute | solution.py:586
  54.3 19.4 %collective-permute-start.15 = (bf16[2,128,1536]{2,1,0:T(8,128)(2,1)S(1)}, bf16[2,128,1536]{2,1,0:T(8,128)(2,1)S(1)}, u32[]{:S(2)}, u32[]{:S(2)}) collective-permute-start(bf16[2,128,1536]{2,1,0:T(8,128)(2,1)S(1)} %get-tuple-element.197.refs_3_), channel_id=1, source_target_pairs={{0,1},{1,0},{2,3},{3,2},{4,5},{5,4},{6,7},{7,6},{8,9},{9,8},{10,11... | collective-permute-start | bytes 2359304 | tf_op jit(solution)/shard_map/ppermute | solution.py:581
  65.6 11.2 %collective-permute-start.25 = (bf16[256,768]{1,0:T(8,128)(2,1)S(1)}, bf16[256,768]{1,0:T(8,128)(2,1)S(1)}, u32[]{:S(2)}, u32[]{:S(2)}) collective-permute-start(bf16[256,768]{1,0:T(8,128)(2,1)S(1)} %get-tuple-element.241.refs_4_), channel_id=1, source_target_pairs={{0,4},{2,6},{4,0},{6,2},{8,12},{10,14},{12,8},{14,10},{16,20},{18,... | collective-permute-start | bytes 1179656 | tf_op jit(solution)/shard_map/ppermute | solution.py:586
  76.8 11.2 %collective-permute-start.21 = (bf16[1152,256]{1,0:T(8,128)(2,1)S(1)}, bf16[1152,256]{1,0:T(8,128)(2,1)S(1)}, u32[]{:S(2)}, u32[]{:S(2)}) collective-permute-start(bf16[1152,256]{1,0:T(8,128)(2,1)S(1)} %collective-permute-done.4.refs_2_), channel_id=1, source_target_pairs={{0,2},{2,0},{4,6},{6,4},{8,10},{10,8},{12,14},{14,12},{16,18},{18,... | collective-permute-start | bytes 1769480 | tf_op jit(solution)/shard_map/ppermute | solution.py:586
  78.5 11.3 %collective-permute-start.35 = (bf16[256,768]{1,0:T(8,128)(2,1)S(1)}, bf16[256,768]{1,0:T(8,128)(2,1)S(1)}, u32[]{:S(2)}, u32[]{:S(2)}) collective-permute-start(bf16[256,768]{1,0:T(8,128)(2,1)S(1)} %get-tuple-element.275.refs_4_), channel_id=1, source_target_pairs={{0,8},{2,10},{4,12},{6,14},{8,0},{10,2},{12,4},{14,6},{16,24},{18,... | collective-permute-start | bytes 1179656 | tf_op jit(solution)/shard_map/ppermute | solution.py:586
  84.1 11.9 %collective-permute-start.29 = (bf16[768,256]{1,0:T(8,128)(2,1)S(1)}, bf16[768,256]{1,0:T(8,128)(2,1)S(1)}, u32[]{:S(2)}, u32[]{:S(2)}) collective-permute-start(bf16[768,256]{1,0:T(8,128)(2,1)S(1)} %get-tuple-element.258), channel_id=1, source_target_pairs={{0,4},{2,6},{4,0},{6,2},{8,12},{10,14},{12,8},{14,10},{16,20},{18,... | collective-permute-start | bytes 1179656 | tf_op jit(solution)/shard_map/ppermute | solution.py:586
  85.8 16.1 %collective-permute-start.31 = (bf16[192,768]{1,0:T(8,128)(2,1)S(1)}, bf16[192,768]{1,0:T(8,128)(2,1)S(1)}, u32[]{:S(2)}, u32[]{:S(2)}) collective-permute-start(bf16[192,768]{1,0:T(8,128)(2,1)S(1)} %get-tuple-element.221), channel_id=1, source_target_pairs={{0,4},{2,6},{4,0},{6,2},{8,12},{10,14},{12,8},{14,10},{16,20},{18,... | collective-permute-start | bytes 884744 | tf_op jit(solution)/shard_map/ppermute | solution.py:586
  89.8 17.9 %collective-permute-start.36 = (bf16[256,768]{1,0:T(8,128)(2,1)S(1)}, bf16[256,768]{1,0:T(8,128)(2,1)S(1)}, u32[]{:S(2)}, u32[]{:S(2)}) collective-permute-start(bf16[256,768]{1,0:T(8,128)(2,1)S(1)} %collective-permute-done.35.refs_6_), channel_id=1, source_target_pairs={{0,2},{2,0},{4,6},{6,4},{8,10},{10,8},{12,14},{14,12},{16,18},{18,... | collective-permute-start | bytes 1179656 | tf_op jit(solution)/shard_map/ppermute | solution.py:586
  89.8 21.3 %collective-permute-start.34 = (bf16[768,256]{1,0:T(8,128)(2,1)S(1)}, bf16[768,256]{1,0:T(8,128)(2,1)S(1)}, u32[]{:S(2)}, u32[]{:S(2)}) collective-permute-start(bf16[768,256]{1,0:T(8,128)(2,1)S(1)} %collective-permute-done.6.refs_2_), channel_id=1, source_target_pairs={{0,2},{2,0},{4,6},{6,4},{8,10},{10,8},{12,14},{14,12},{16,18},{18,... | collective-permute-start | bytes 1179656 | tf_op jit(solution)/shard_map/ppermute | solution.py:586
  90.3 14.9 %collective-permute-start.37 = (bf16[192,768]{1,0:T(8,128)(2,1)S(1)}, bf16[192,768]{1,0:T(8,128)(2,1)S(1)}, u32[]{:S(2)}, u32[]{:S(2)}) collective-permute-start(bf16[192,768]{1,0:T(8,128)(2,1)S(1)} %get-tuple-element.246), channel_id=1, source_target_pairs={{0,8},{2,10},{4,12},{6,14},{8,0},{10,2},{12,4},{14,6},{16,24},{18,... | collective-permute-start | bytes 884744 | tf_op jit(solution)/shard_map/ppermute | solution.py:586
  102.0 19.3 %collective-permute-start.30 = (bf16[768,256]{1,0:T(8,128)(2,1)S(1)}, bf16[768,256]{1,0:T(8,128)(2,1)S(1)}, u32[]{:S(2)}, u32[]{:S(2)}) collective-permute-start(bf16[768,256]{1,0:T(8,128)(2,1)S(1)} %collective-permute-done.29.refs_6_), channel_id=1, source_target_pairs={{0,2},{2,0},{4,6},{6,4},{8,10},{10,8},{12,14},{14,12},{16,18},{18,... | collective-permute-start | bytes 1179656 | tf_op jit(solution)/shard_map/ppermute | solution.py:586
  105.2 17.5 %collective-permute-start.27 = (bf16[192,1152]{1,0:T(8,128)(2,1)S(1)}, bf16[192,1152]{1,0:T(8,128)(2,1)S(1)}, u32[]{:S(2)}, u32[]{:S(2)}) collective-permute-start(bf16[192,1152]{1,0:T(8,128)(2,1)S(1)} %get-tuple-element.252), channel_id=1, source_target_pairs={{0,8},{2,10},{4,12},{6,14},{8,0},{10,2},{12,4},{14,6},{16,24},{18,... | collective-permute-start | bytes 1327112 | tf_op jit(solution)/shard_map/ppermute | solution.py:586
  105.3 26.8 %collective-permute-start.20 = (bf16[128,1536]{1,0:T(8,128)(2,1)S(1)}, bf16[128,1536]{1,0:T(8,128)(2,1)S(1)}, u32[]{:S(2)}, u32[]{:S(2)}) collective-permute-start(bf16[128,1536]{1,0:T(8,128)(2,1)S(1)} %slice.11), channel_id=1, source_target_pairs={{0,1},{1,0},{2,3},{3,2},{4,5},{5,4},{6,7},{7,6},{8,9},{9,8},{10,11... | collective-permute-start | bytes 1179656 | tf_op jit(solution)/shard_map/ppermute | solution.py:581
  111.9 17.1 %collective-permute-start.40 = (bf16[192,768]{1,0:T(8,128)(2,1)S(1)}, bf16[192,768]{1,0:T(8,128)(2,1)S(1)}, u32[]{:S(2)}, u32[]{:S(2)}) collective-permute-start(bf16[192,768]{1,0:T(8,128)(2,1)S(1)} %get-tuple-element.280), channel_id=1, source_target_pairs={{0,4},{2,6},{4,0},{6,2},{8,12},{10,14},{12,8},{14,10},{16,20},{18,... | collective-permute-start | bytes 884744 | tf_op jit(solution)/shard_map/ppermute | solution.py:586
  125.5 18.0 %collective-permute-start.38 = (bf16[96,1152]{1,0:T(8,128)(2,1)S(1)}, bf16[96,1152]{1,0:T(8,128)(2,1)S(1)}, u32[]{:S(2)}, u32[]{:S(2)}) collective-permute-start(bf16[96,1152]{1,0:T(8,128)(2,1)S(1)} %get-tuple-element.291), channel_id=1, source_target_pairs={{0,16},{2,18},{4,20},{6,22},{8,24},{10,26},{12,28},{14,30},{16,0},... | collective-permute-start | bytes 663560 | tf_op jit(solution)/shard_map/ppermute | solution.py:586
  129.1 16.3 %collective-permute-start.43 = (bf16[96,768]{1,0:T(8,128)(2,1)S(1)}, bf16[96,768]{1,0:T(8,128)(2,1)S(1)}, u32[]{:S(2)}, u32[]{:S(2)}) collective-permute-start(bf16[96,768]{1,0:T(8,128)(2,1)S(1)} %get-tuple-element.302), channel_id=1, source_target_pairs={{0,16},{2,18},{4,20},{6,22},{8,24},{10,26},{12,28},{14,30},{16,0},... | collective-permute-start | bytes 442376 | tf_op jit(solution)/shard_map/ppermute | solution.py:586
  130.5 15.7 %collective-permute-start.42 = (bf16[96,384]{1,0:T(8,128)(2,1)S(1)}, bf16[96,384]{1,0:T(8,128)(2,1)S(1)}, u32[]{:S(2)}, u32[]{:S(2)}) collective-permute-start(bf16[96,384]{1,0:T(8,128)(2,1)S(1)} %get-tuple-element.301), channel_id=1, source_target_pairs={{0,16},{2,18},{4,20},{6,22},{8,24},{10,26},{12,28},{14,30},{16,0},... | collective-permute-start | bytes 221192 | tf_op jit(solution)/shard_map/ppermute | solution.py:586
  (34 other events, 240.1 us)

commit v4 on v3

--- a/solution.py
+++ b/solution.py
@@ -17,13 +17,14 @@
 BF = jnp.bfloat16
 F32 = jnp.float32
 ORDER = (
-    "q_sum", "mm", "v_sum", "back", "q_add", "k_sum", "tap_sum", "q_end", "v_add", "k_add", "o_sum",
-    "v_end", "point_sum", "tap_add", "k_end", "o_add", "point_add", "tap_end", "o_end", "point_end",
+    "q_sum", "v_sum", "back", "q_add", "k_sum", "tap_sum", "mm", "v_add", "k_add", "q_end",
+    "o_sum", "v_end", "point_sum", "tap_add", "o_add", "k_end", "point_add", "tap_end", "o_end",
+    "point_end",
 )
 SENDS = (
     ("q_far", "start"), ("v_far", "start"), ("k_far", "q_far"), ("wides", "near"),
     ("q_pass", "start"), ("v_pass", "start"), ("tap_far", "back"), ("resid_far", "tap_far"),
-    ("k_pass", "back"), ("o_far", "back"), ("tap_pass", "back"), ("olds", "back"),
+    ("k_pass", "q_add_kept"), ("o_far", "back"), ("tap_pass", "back"), ("olds", "near"),
     ("o_pass", "tap_sum"), ("point_pass", "tap_sum"),
 )
 NEEDED = ("q_got",)
@@ -620,7 +621,7 @@
 
     pieces = gather_seq(own)
     taps = dilated_tap_weight.reshape(3 * inner, channels)
-    grad_own = scaled_rows(cotangent[0], inv_tokens, own, taps)
+    grad_own = scaled_rows(cotangent[0], inv_tokens, own, taps, point_weight)
     grad_pieces = gather_seq(grad_own)
     pre, parts, middle, act = conv_block(offset, pieces, taps, point_weight)
     pre, parts, middle, act, grad_pieces = lax.optimization_barrier(

time: 147 us -> 142 us (0.966)
  starting transfers between devices: 43.4 us -> 38.9 us
  waiting for transfers between devices: 67.6 us -> 65.1 us
    ppermute x39, starting transfers between devices: 35.5 us -> 31.6 us  [to_peer(): return lax.ppermute(x, 'dp', [(i, i ^ bit) for i in range(n_dp)])]
    ppermute x39, waiting for transfers between devices: 54.5 us -> 52.4 us  [to_peer(): return lax.ppermute(x, 'dp', [(i, i ^ bit) for i in range(n_dp)])]
    unnamed x28 -> x30, local copies, waits for them, and re-layouts: 6.3 us -> 7.57 us
  transfers between devices with their start and end apart: 44 -> 44, of which waited for: 21 -> 20; matrix products, arithmetic and copies ran while one was open for 1% -> 1% of each run, Pallas kernels for 17% -> 17%
where the time goes in v4:
time: 142 us; the launch traced here: 141 us
  waiting for transfers between devices  65.1 us (46%)
  starting transfers between devices  38.9 us (27%)
  Pallas kernels  27 us (19%)
  local copies, waits for them, and re-layouts  7.6 us (5%)
    ppermute x39, waiting for transfers between devices, to_peer(): return lax.ppermute(x, 'dp', [(i, i ^ bit) for i in range(n_dp)])  52.4 us
    ppermute x39, starting transfers between devices, to_peer(): return lax.ppermute(x, 'dp', [(i, i ^ bit) for i in range(n_dp)])  31.6 us
    pallas_call x26, Pallas kernels, call(): pl.pallas_call(kernel, out_shape=out_shape, in_specs=specs, out_specs=[pl...  27 us
    ppermute x5, waiting for transfers between devices, swap_seq(): return lax.ppermute(x, 'seq', [(0, 1), (1, 0)])  12.6 us
    unnamed x30, local copies, waits for them, and re-layouts  7.57 us
    ppermute x5, starting transfers between devices, swap_seq(): return lax.ppermute(x, 'seq', [(0, 1), (1, 0)])  7.39 us
  transfers between devices with their start and end apart: 44, of which 20 were waited for; matrix products, arithmetic and copies ran while one was open for 1% of the time, Pallas kernels for 17%

profile of v4, /device:TPU:0, one launch (start us, length us, event | category | flops | bytes accessed | tf_op | source)
XLA Modules:
  0.0 141.1 jit_solution(15175713742468629891)
XLA Ops:
  0.6 3.0 %collective-permute-start = (bf16[128,1536]{1,0:T(8,128)(2,1)}, bf16[128,1536]{1,0:T(8,128)(2,1)}, u32[]{:S(2)}, u32[]{:S(2)}) collective-permute-start(bf16[128,1536]{1,0:T(8,128)(2,1)} %bitcast.12), channel_id=1, source_target_pairs={{0,1},{1,0},{2,3},{3,2},{4,5},{5,4},{6,7},{7,6},{8,9},{9,8},{10,11... | collective-permute-start | bytes 1179656 | tf_op jit(solution)/shard_map/ppermute | solution.py:582
  3.7 2.0 %copy-done = bf16[3,384,1536]{2,1,0:T(8,128)(2,1)S(1)} copy-done((bf16[3,384,1536]{2,1,0:T(8,128)(2,1)S(1)}, bf16[3,384,1536]{2,1,0:T(8,128)(2,1)}, u32[]{:S(2)}) %copy-start) | copy-done | bytes 3538968
  9.8 4.2 %collective-permute-done.refs_2_.refs_3_ = bf16[128,1536]{1,0:T(8,128)(2,1)} collective-permute-done((bf16[128,1536]{1,0:T(8,128)(2,1)}, bf16[128,1536]{1,0:T(8,128)(2,1)}, u32[]{:S(2)}, u32[]{:S(2)}) %collective-permute-start) | collective-permute-done | bytes 393248 | tf_op jit(solution)/shard_map/ppermute | solution.py:582
  16.2 3.4 %shard_map.153 = (f32[256,384]{1,0:T(8,128)S(1)}, bf16[2,128,1536]{2,1,0:T(8,128)(2,1)S(1)}, bf16[256,384]{1,0:T(8,128)(2,1)S(1)}, bf16[256,1536]{1,0:T(8,128)(2,1)S(1)}) custom-call(s32[1]{0:T(128)} %bitcast.1.refs_0_.offset_ref, bf16[128,1536]{1,0:T(8,128)(2,1)S(1)} %bitcast.14, bf16[128,1536]{1,0:T(8,128)(2,1)} %collective-permute-done.refs_2_.refs_3_, ...), custom_call_target="tpu_custom_call" | custom-call | tf_op jit(solution)/shard_map/pallas_call | solution.py:115
  19.6 1.9 %collective-permute-done.1.refs_2_ = bf16[128,1536]{1,0:T(8,128)(2,1)} collective-permute-done((bf16[128,1536]{1,0:T(8,128)(2,1)}, bf16[128,1536]{1,0:T(8,128)(2,1)}, u32[]{:S(2)}, u32[]{:S(2)}) %collective-permute-start.1) | collective-permute-done | bytes 393248 | tf_op jit(solution)/shard_map/ppermute | solution.py:582
  21.5 1.7 %collective-permute-start.2 = (bf16[2,128,1536]{2,1,0:T(8,128)(2,1)S(1)}, bf16[2,128,1536]{2,1,0:T(8,128)(2,1)S(1)}, u32[]{:S(2)}, u32[]{:S(2)}) collective-permute-start(bf16[2,128,1536]{2,1,0:T(8,128)(2,1)S(1)} %get-tuple-element.161.refs_4_), channel_id=1, source_target_pairs={{0,1},{1,0},{2,3},{3,2},{4,5},{5,4},{6,7},{7,6},{8,9},{9,8},{10,11... | collective-permute-start | bytes 2359304 | tf_op jit(solution)/shard_map/ppermute | solution.py:582
  30.8 5.8 %collective-permute-done.6.refs_2_ = bf16[768,256]{1,0:T(8,128)(2,1)S(1)} collective-permute-done((bf16[768,256]{1,0:T(8,128)(2,1)S(1)}, bf16[768,256]{1,0:T(8,128)(2,1)S(1)}, u32[]{:S(2)}, u32[]{:S(2)}) %collective-permute-start.6) | collective-permute-done | bytes 393248 | tf_op jit(solution)/shard_map/ppermute | solution.py:587
  38.2 2.1 %collective-permute-done.2.refs_5_ = bf16[2,128,1536]{2,1,0:T(8,128)(2,1)S(1)} collective-permute-done((bf16[2,128,1536]{2,1,0:T(8,128)(2,1)S(1)}, bf16[2,128,1536]{2,1,0:T(8,128)(2,1)S(1)}, u32[]{:S(2)}, u32[]{:S(2)}) %collective-permute-start.2) | collective-permute-done | bytes 786464 | tf_op jit(solution)/shard_map/ppermute | solution.py:582
  40.3 1.8 %shard_map.158 = (bf16[256,1536]{1,0:T(8,128)(2,1)S(1)}, bf16[256,1536]{1,0:T(8,128)(2,1)S(1)}, bf16[384,256]{1,0:T(8,128)(2,1)S(1)}, bf16[384,256]{1,0:T(8,128)...) custom-call(s32[16]{0:T(128)S(1)} %get-tuple-element.308.refs_0_, ...), custom_call_target="tpu_custom_call" | custom-call | tf_op jit(solution)/shard_map/pallas_call | solution.py:115
  45.7 5.8 %shard_map.159 = (bf16[256,768]{1,0:T(8,128)(2,1)S(1)}, bf16[256,768]{1,0:T(8,128)(2,1)S(1)}, bf16[256,768]{1,0:T(8,128)(2,1)S(1)}, bf16[256,768]{1,0:T(8,128)(2...) custom-call(bf16[256,1536]{1,0:T(8,128)(2,1)S(1)} %get-tuple-element.175.n_ref, ...), custom_call_target="tpu_custom_call" | custom-call | tf_op jit(solution)/shard_map/pallas_call | solution.py:115
  55.8 8.3 %collective-permute-done.18.refs_6_ = bf16[256,768]{1,0:T(8,128)(2,1)S(1)} collective-permute-done((bf16[256,768]{1,0:T(8,128)(2,1)S(1)}, bf16[256,768]{1,0:T(8,128)(2,1)S(1)}, u32[]{:S(2)}, u32[]{:S(2)}) %collective-permute-start.18) | collective-permute-done | bytes 393248 | tf_op jit(solution)/shard_map/ppermute | solution.py:587
  69.5 4.5 %collective-permute-done.13.refs_4_ = bf16[2,128,1536]{2,1,0:T(8,128)(2,1)S(1)} collective-permute-done((bf16[2,128,1536]{2,1,0:T(8,128)(2,1)S(1)}, bf16[2,128,1536]{2,1,0:T(8,128)(2,1)S(1)}, u32[]{:S(2)}, u32[]{:S(2)}) %collective-permute-start.13) | collective-permute-done | bytes 786464 | tf_op jit(solution)/shard_map/ppermute | solution.py:582
  73.9 2.1 %shard_map.162 = (bf16[256,384]{1,0:T(8,128)(2,1)S(1)}, bf16[384,256]{1,0:T(8,128)(2,1)S(1)}, bf16[384,256]{1,0:T(8,128)(2,1)S(1)}, bf16[768,256]{1,0:T(8,128)(2,1)S(1)}) custom-call(s32[16]{0:T(128)S(1)} %get-tuple-element.308.refs_0_, bf16[256,1536]{1,0:T(8,128)(2,1)S(1)} %get-tuple-element.174.refs_1_, ...), custom_call_target="tpu_custom_call" | custom-call | tf_op jit(solution)/shard_map/pallas_call | solution.py:115
  79.5 4.8 %collective-permute-done.22.refs_6_ = bf16[256,384]{1,0:T(8,128)(2,1)S(1)} collective-permute-done((bf16[256,384]{1,0:T(8,128)(2,1)S(1)}, bf16[256,384]{1,0:T(8,128)(2,1)S(1)}, u32[]{:S(2)}, u32[]{:S(2)}) %collective-permute-start.22) | collective-permute-done | bytes 196640 | tf_op jit(solution)/shard_map/ppermute | solution.py:587
  86.6 2.6 %collective-permute-start.36 = (bf16[96,768]{1,0:T(8,128)(2,1)S(1)}, bf16[96,768]{1,0:T(8,128)(2,1)S(1)}, u32[]{:S(2)}, u32[]{:S(2)}) collective-permute-start(bf16[96,768]{1,0:T(8,128)(2,1)S(1)} %get-tuple-element.270), channel_id=1, source_target_pairs={{0,16},{2,18},{4,20},{6,22},{8,24},{10,26},{12,28},{14,30},{16,0},... | collective-permute-start | bytes 442376 | tf_op jit(solution)/shard_map/ppermute | solution.py:587
  92.0 4.4 %collective-permute-done.29.refs_6_ = bf16[768,256]{1,0:T(8,128)(2,1)S(1)} collective-permute-done((bf16[768,256]{1,0:T(8,128)(2,1)S(1)}, bf16[768,256]{1,0:T(8,128)(2,1)S(1)}, u32[]{:S(2)}, u32[]{:S(2)}) %collective-permute-start.29) | collective-permute-done | bytes 393248 | tf_op jit(solution)/shard_map/ppermute | solution.py:587
  96.8 3.7 %collective-permute-done.31.got_ref = bf16[192,768]{1,0:T(8,128)(2,1)S(1)} collective-permute-done((bf16[192,768]{1,0:T(8,128)(2,1)S(1)}, bf16[192,768]{1,0:T(8,128)(2,1)S(1)}, u32[]{:S(2)}, u32[]{:S(2)}) %collective-permute-start.31) | collective-permute-done | bytes 294944 | tf_op jit(solution)/shard_map/ppermute | solution.py:587
  107.8 4.0 %collective-permute-done.32.refs_1_ = bf16[96,768]{1,0:T(8,128)(2,1)S(1)} collective-permute-done((bf16[96,768]{1,0:T(8,128)(2,1)S(1)}, bf16[96,768]{1,0:T(8,128)(2,1)S(1)}, u32[]{:S(2)}, u32[]{:S(2)}) %collective-permute-start.32) | collective-permute-done | bytes 147488 | tf_op jit(solution)/shard_map/ppermute | solution.py:587
  111.9 3.4 %collective-permute-start.40 = (bf16[96,768]{1,0:T(8,128)(2,1)S(1)}, bf16[96,768]{1,0:T(8,128)(2,1)S(1)}, u32[]{:S(2)}, u32[]{:S(2)}) collective-permute-start(bf16[96,768]{1,0:T(8,128)(2,1)S(1)} %get-tuple-element.292), channel_id=1, source_target_pairs={{0,16},{2,18},{4,20},{6,22},{8,24},{10,26},{12,28},{14,30},{16,0},... | collective-permute-start | bytes 442376 | tf_op jit(solution)/shard_map/ppermute | solution.py:587
  116.6 1.8 %collective-permute-start.39 = (bf16[192,384]{1,0:T(8,128)(2,1)S(1)}, bf16[192,384]{1,0:T(8,128)(2,1)S(1)}, u32[]{:S(2)}, u32[]{:S(2)}) collective-permute-start(bf16[192,384]{1,0:T(8,128)(2,1)S(1)} %get-tuple-element.288), channel_id=1, source_target_pairs={{0,8},{2,10},{4,12},{6,14},{8,0},{10,2},{12,4},{14,6},{16,24},{18,... | collective-permute-start | bytes 442376 | tf_op jit(solution)/shard_map/ppermute | solution.py:587
  120.1 3.1 %collective-permute-done.40.refs_1_ = bf16[96,768]{1,0:T(8,128)(2,1)S(1)} collective-permute-done((bf16[96,768]{1,0:T(8,128)(2,1)S(1)}, bf16[96,768]{1,0:T(8,128)(2,1)S(1)}, u32[]{:S(2)}, u32[]{:S(2)}) %collective-permute-start.40) | collective-permute-done | bytes 147488 | tf_op jit(solution)/shard_map/ppermute | solution.py:587
  124.5 2.5 %collective-permute-start.42 = (bf16[96,384]{1,0:T(8,128)(2,1)S(1)}, bf16[96,384]{1,0:T(8,128)(2,1)S(1)}, u32[]{:S(2)}, u32[]{:S(2)}) collective-permute-start(bf16[96,384]{1,0:T(8,128)(2,1)S(1)} %get-tuple-element.301), channel_id=1, source_target_pairs={{0,16},{2,18},{4,20},{6,22},{8,24},{10,26},{12,28},{14,30},{16,0},... | collective-permute-start | bytes 221192 | tf_op jit(solution)/shard_map/ppermute | solution.py:587
  127.9 7.1 %collective-permute-done.38.refs_1_ = bf16[96,1152]{1,0:T(8,128)(2,1)S(1)} collective-permute-done((bf16[96,1152]{1,0:T(8,128)(2,1)S(1)}, bf16[96,1152]{1,0:T(8,128)(2,1)S(1)}, u32[]{:S(2)}, u32[]{:S(2)}) %collective-permute-start.38) | collective-permute-done | bytes 221216 | tf_op jit(solution)/shard_map/ppermute | solution.py:587
  135.7 3.9 %collective-permute-done.43.refs_1_ = bf16[96,768]{1,0:T(8,128)(2,1)S(1)} collective-permute-done((bf16[96,768]{1,0:T(8,128)(2,1)S(1)}, bf16[96,768]{1,0:T(8,128)(2,1)S(1)}, u32[]{:S(2)}, u32[]{:S(2)}) %collective-permute-start.43) | collective-permute-done | bytes 147488 | tf_op jit(solution)/shard_map/ppermute | solution.py:587
  (124 shorter events, 52.4 us)
Async XLA Ops:
  0.6 13.3 %collective-permute-start = (bf16[128,1536]{1,0:T(8,128)(2,1)}, bf16[128,1536]{1,0:T(8,128)(2,1)}, u32[]{:S(2)}, u32[]{:S(2)}) collective-permute-start(bf16[128,1536]{1,0:T(8,128)(2,1)} %bitcast.12), channel_id=1, source_target_pairs={{0,1},{1,0},{2,3},{3,2},{4,5},{5,4},{6,7},{7,6},{8,9},{9,8},{10,11... | collective-permute-start | bytes 1179656 | tf_op jit(solution)/shard_map/ppermute | solution.py:582
  9.7 11.8 %collective-permute-start.1 = (bf16[128,1536]{1,0:T(8,128)(2,1)}, bf16[128,1536]{1,0:T(8,128)(2,1)}, u32[]{:S(2)}, u32[]{:S(2)}) collective-permute-start(bf16[128,1536]{1,0:T(8,128)(2,1)} %shard_map.154.refs_1_), channel_id=1, source_target_pairs={{0,1},{1,0},{2,3},{3,2},{4,5},{5,4},{6,7},{7,6},{8,9},{9,8},{10,11... | collective-permute-start | bytes 1179656 | tf_op jit(solution)/shard_map/ppermute | solution.py:582
  21.5 18.7 %collective-permute-start.2 = (bf16[2,128,1536]{2,1,0:T(8,128)(2,1)S(1)}, bf16[2,128,1536]{2,1,0:T(8,128)(2,1)S(1)}, u32[]{:S(2)}, u32[]{:S(2)}) collective-permute-start(bf16[2,128,1536]{2,1,0:T(8,128)(2,1)S(1)} %get-tuple-element.161.refs_4_), channel_id=1, source_target_pairs={{0,1},{1,0},{2,3},{3,2},{4,5},{5,4},{6,7},{7,6},{8,9},{9,8},{10,11... | collective-permute-start | bytes 2359304 | tf_op jit(solution)/shard_map/ppermute | solution.py:582
  24.2 14.0 %collective-permute-start.4 = (bf16[1152,256]{1,0:T(8,128)(2,1)S(1)}, bf16[1152,256]{1,0:T(8,128)(2,1)S(1)}, u32[]{:S(2)}, u32[]{:S(2)}) collective-permute-start(bf16[1152,256]{1,0:T(8,128)(2,1)S(1)} %get-tuple-element.166), channel_id=1, source_target_pairs={{0,4},{2,6},{4,0},{6,2},{8,12},{10,14},{12,8},{14,10},{16,20},{18,... | collective-permute-start | bytes 1769480 | tf_op jit(solution)/shard_map/ppermute | solution.py:587
  52.6 11.5 %collective-permute-start.11 = (bf16[4,256,768]{2,1,0:T(8,128)(2,1)S(1)}, bf16[4,256,768]{2,1,0:T(8,128)(2,1)S(1)}, u32[]{:S(2)}, u32[]{:S(2)}) collective-permute-start(bf16[4,256,768]{2,1,0:T(8,128)(2,1)S(1)} %get-tuple-element.189), channel_id=1, source_target_pairs={{0,2},{2,0},{4,6},{6,4},{8,10},{10,8},{12,14},{14,12},{16,18},{18,... | collective-permute-start | bytes 4718600 | tf_op jit(solution)/shard_map/ppermute | solution.py:587
  52.6 11.5 %collective-permute-start.18 = (bf16[256,768]{1,0:T(8,128)(2,1)S(1)}, bf16[256,768]{1,0:T(8,128)(2,1)S(1)}, u32[]{:S(2)}, u32[]{:S(2)}) collective-permute-start(bf16[256,768]{1,0:T(8,128)(2,1)S(1)} %get-tuple-element.212.refs_4_), channel_id=1, source_target_pairs={{0,4},{2,6},{4,0},{6,2},{8,12},{10,14},{12,8},{14,10},{16,20},{18,... | collective-permute-start | bytes 1179656 | tf_op jit(solution)/shard_map/ppermute | solution.py:587
  54.1 11.2 %collective-permute-start.15 = (bf16[256,768]{1,0:T(8,128)(2,1)S(1)}, bf16[256,768]{1,0:T(8,128)(2,1)S(1)}, u32[]{:S(2)}, u32[]{:S(2)}) collective-permute-start(bf16[256,768]{1,0:T(8,128)(2,1)S(1)} %get-tuple-element.218.refs_4_), channel_id=1, source_target_pairs={{0,8},{2,10},{4,12},{6,14},{8,0},{10,2},{12,4},{14,6},{16,24},{18,... | collective-permute-start | bytes 1179656 | tf_op jit(solution)/shard_map/ppermute | solution.py:587
  54.5 19.4 %collective-permute-start.13 = (bf16[2,128,1536]{2,1,0:T(8,128)(2,1)S(1)}, bf16[2,128,1536]{2,1,0:T(8,128)(2,1)S(1)}, u32[]{:S(2)}, u32[]{:S(2)}) collective-permute-start(bf16[2,128,1536]{2,1,0:T(8,128)(2,1)S(1)} %get-tuple-element.193.refs_3_), channel_id=1, source_target_pairs={{0,1},{1,0},{2,3},{3,2},{4,5},{5,4},{6,7},{7,6},{8,9},{9,8},{10,11... | collective-permute-start | bytes 2359304 | tf_op jit(solution)/shard_map/ppermute | solution.py:582
  65.9 12.5 %collective-permute-start.24 = (bf16[256,768]{1,0:T(8,128)(2,1)S(1)}, bf16[256,768]{1,0:T(8,128)(2,1)S(1)}, u32[]{:S(2)}, u32[]{:S(2)}) collective-permute-start(bf16[256,768]{1,0:T(8,128)(2,1)S(1)} %get-tuple-element.239.refs_4_), channel_id=1, source_target_pairs={{0,4},{2,6},{4,0},{6,2},{8,12},{10,14},{12,8},{14,10},{16,20},{18,... | collective-permute-start | bytes 1179656 | tf_op jit(solution)/shard_map/ppermute | solution.py:587
  67.3 17.4 %collective-permute-start.12 = (bf16[1152,256]{1,0:T(8,128)(2,1)S(1)}, bf16[1152,256]{1,0:T(8,128)(2,1)S(1)}, u32[]{:S(2)}, u32[]{:S(2)}) collective-permute-start(bf16[1152,256]{1,0:T(8,128)(2,1)S(1)} %collective-permute-done.4.refs_2_), channel_id=1, source_target_pairs={{0,2},{2,0},{4,6},{6,4},{8,10},{10,8},{12,14},{14,12},{16,18},{18,... | collective-permute-start | bytes 1769480 | tf_op jit(solution)/shard_map/ppermute | solution.py:587
  78.9 12.5 %collective-permute-start.34 = (bf16[256,768]{1,0:T(8,128)(2,1)S(1)}, bf16[256,768]{1,0:T(8,128)(2,1)S(1)}, u32[]{:S(2)}, u32[]{:S(2)}) collective-permute-start(bf16[256,768]{1,0:T(8,128)(2,1)S(1)} %get-tuple-element.275.refs_4_), channel_id=1, source_target_pairs={{0,8},{2,10},{4,12},{6,14},{8,0},{10,2},{12,4},{14,6},{16,24},{18,... | collective-permute-start | bytes 1179656 | tf_op jit(solution)/shard_map/ppermute | solution.py:587
  84.3 12.1 %collective-permute-start.29 = (bf16[768,256]{1,0:T(8,128)(2,1)S(1)}, bf16[768,256]{1,0:T(8,128)(2,1)S(1)}, u32[]{:S(2)}, u32[]{:S(2)}) collective-permute-start(bf16[768,256]{1,0:T(8,128)(2,1)S(1)} %get-tuple-element.258), channel_id=1, source_target_pairs={{0,4},{2,6},{4,0},{6,2},{8,12},{10,14},{12,8},{14,10},{16,20},{18,... | collective-permute-start | bytes 1179656 | tf_op jit(solution)/shard_map/ppermute | solution.py:587
  84.7 15.8 %collective-permute-start.31 = (bf16[192,768]{1,0:T(8,128)(2,1)S(1)}, bf16[192,768]{1,0:T(8,128)(2,1)S(1)}, u32[]{:S(2)}, u32[]{:S(2)}) collective-permute-start(bf16[192,768]{1,0:T(8,128)(2,1)S(1)} %get-tuple-element.223), channel_id=1, source_target_pairs={{0,4},{2,6},{4,0},{6,2},{8,12},{10,14},{12,8},{14,10},{16,20},{18,... | collective-permute-start | bytes 884744 | tf_op jit(solution)/shard_map/ppermute | solution.py:587
  86.6 13.9 %collective-permute-start.36 = (bf16[96,768]{1,0:T(8,128)(2,1)S(1)}, bf16[96,768]{1,0:T(8,128)(2,1)S(1)}, u32[]{:S(2)}, u32[]{:S(2)}) collective-permute-start(bf16[96,768]{1,0:T(8,128)(2,1)S(1)} %get-tuple-element.270), channel_id=1, source_target_pairs={{0,16},{2,18},{4,20},{6,22},{8,24},{10,26},{12,28},{14,30},{16,0},... | collective-permute-start | bytes 442376 | tf_op jit(solution)/shard_map/ppermute | solution.py:587
  91.4 15.3 %collective-permute-start.33 = (bf16[768,256]{1,0:T(8,128)(2,1)S(1)}, bf16[768,256]{1,0:T(8,128)(2,1)S(1)}, u32[]{:S(2)}, u32[]{:S(2)}) collective-permute-start(bf16[768,256]{1,0:T(8,128)(2,1)S(1)} %collective-permute-done.6.refs_2_), channel_id=1, source_target_pairs={{0,2},{2,0},{4,6},{6,4},{8,10},{10,8},{12,14},{14,12},{16,18},{18,... | collective-permute-start | bytes 1179656 | tf_op jit(solution)/shard_map/ppermute | solution.py:587
  91.6 11.4 %collective-permute-start.37 = (bf16[192,768]{1,0:T(8,128)(2,1)S(1)}, bf16[192,768]{1,0:T(8,128)(2,1)S(1)}, u32[]{:S(2)}, u32[]{:S(2)}) collective-permute-start(bf16[192,768]{1,0:T(8,128)(2,1)S(1)} %get-tuple-element.244), channel_id=1, source_target_pairs={{0,8},{2,10},{4,12},{6,14},{8,0},{10,2},{12,4},{14,6},{16,24},{18,... | collective-permute-start | bytes 884744 | tf_op jit(solution)/shard_map/ppermute | solution.py:587
  96.4 22.0 %collective-permute-start.27 = (bf16[192,1152]{1,0:T(8,128)(2,1)S(1)}, bf16[192,1152]{1,0:T(8,128)(2,1)S(1)}, u32[]{:S(2)}, u32[]{:S(2)}) collective-permute-start(bf16[192,1152]{1,0:T(8,128)(2,1)S(1)} %get-tuple-element.250), channel_id=1, source_target_pairs={{0,8},{2,10},{4,12},{6,14},{8,0},{10,2},{12,4},{14,6},{16,24},{18,... | collective-permute-start | bytes 1327112 | tf_op jit(solution)/shard_map/ppermute | solution.py:587
  100.5 15.5 %collective-permute-start.30 = (bf16[768,256]{1,0:T(8,128)(2,1)S(1)}, bf16[768,256]{1,0:T(8,128)(2,1)S(1)}, u32[]{:S(2)}, u32[]{:S(2)}) collective-permute-start(bf16[768,256]{1,0:T(8,128)(2,1)S(1)} %collective-permute-done.29.refs_6_), channel_id=1, source_target_pairs={{0,2},{2,0},{4,6},{6,4},{8,10},{10,8},{12,14},{14,12},{16,18},{18,... | collective-permute-start | bytes 1179656 | tf_op jit(solution)/shard_map/ppermute | solution.py:587
  103.0 24.0 %collective-permute-start.26 = (bf16[128,1536]{1,0:T(8,128)(2,1)S(1)}, bf16[128,1536]{1,0:T(8,128)(2,1)S(1)}, u32[]{:S(2)}, u32[]{:S(2)}) collective-permute-start(bf16[128,1536]{1,0:T(8,128)(2,1)S(1)} %slice.11), channel_id=1, source_target_pairs={{0,1},{1,0},{2,3},{3,2},{4,5},{5,4},{6,7},{7,6},{8,9},{9,8},{10,11... | collective-permute-start | bytes 1179656 | tf_op jit(solution)/shard_map/ppermute | solution.py:582
  107.5 12.5 %collective-permute-start.41 = (bf16[192,768]{1,0:T(8,128)(2,1)S(1)}, bf16[192,768]{1,0:T(8,128)(2,1)S(1)}, u32[]{:S(2)}, u32[]{:S(2)}) collective-permute-start(bf16[192,768]{1,0:T(8,128)(2,1)S(1)} %get-tuple-element.280), channel_id=1, source_target_pairs={{0,4},{2,6},{4,0},{6,2},{8,12},{10,14},{12,8},{14,10},{16,20},{18,... | collective-permute-start | bytes 884744 | tf_op jit(solution)/shard_map/ppermute | solution.py:587
  111.9 11.3 %collective-permute-start.40 = (bf16[96,768]{1,0:T(8,128)(2,1)S(1)}, bf16[96,768]{1,0:T(8,128)(2,1)S(1)}, u32[]{:S(2)}, u32[]{:S(2)}) collective-permute-start(bf16[96,768]{1,0:T(8,128)(2,1)S(1)} %get-tuple-element.292), channel_id=1, source_target_pairs={{0,16},{2,18},{4,20},{6,22},{8,24},{10,26},{12,28},{14,30},{16,0},... | collective-permute-start | bytes 442376 | tf_op jit(solution)/shard_map/ppermute | solution.py:587
  118.5 16.4 %collective-permute-start.38 = (bf16[96,1152]{1,0:T(8,128)(2,1)S(1)}, bf16[96,1152]{1,0:T(8,128)(2,1)S(1)}, u32[]{:S(2)}, u32[]{:S(2)}) collective-permute-start(bf16[96,1152]{1,0:T(8,128)(2,1)S(1)} %get-tuple-element.291), channel_id=1, source_target_pairs={{0,16},{2,18},{4,20},{6,22},{8,24},{10,26},{12,28},{14,30},{16,0},... | collective-permute-start | bytes 663560 | tf_op jit(solution)/shard_map/ppermute | solution.py:587
  123.2 16.5 %collective-permute-start.43 = (bf16[96,768]{1,0:T(8,128)(2,1)S(1)}, bf16[96,768]{1,0:T(8,128)(2,1)S(1)}, u32[]{:S(2)}, u32[]{:S(2)}) collective-permute-start(bf16[96,768]{1,0:T(8,128)(2,1)S(1)} %get-tuple-element.302), channel_id=1, source_target_pairs={{0,16},{2,18},{4,20},{6,22},{8,24},{10,26},{12,28},{14,30},{16,0},... | collective-permute-start | bytes 442376 | tf_op jit(solution)/shard_map/ppermute | solution.py:587
  124.5 16.0 %collective-permute-start.42 = (bf16[96,384]{1,0:T(8,128)(2,1)S(1)}, bf16[96,384]{1,0:T(8,128)(2,1)S(1)}, u32[]{:S(2)}, u32[]{:S(2)}) collective-permute-start(bf16[96,384]{1,0:T(8,128)(2,1)S(1)} %get-tuple-element.301), channel_id=1, source_target_pairs={{0,16},{2,18},{4,20},{6,22},{8,24},{10,26},{12,28},{14,30},{16,0},... | collective-permute-start | bytes 221192 | tf_op jit(solution)/shard_map/ppermute | solution.py:587
  (35 other events, 235.0 us)
